TPU v7x, 256 devices: a whole 4x4x8 slice. The times are simulated.
256 devices in a mesh: row: 64 (over z, y, core), col: 4 (over x).
Axes of the slice: x: 4, y: 4, z: 8, core: 2. Of those that a mesh axis runs over, the one named last changes fastest.
Arguments:
- fine_latent: bfloat16 [98304, 512], P(('row', 'col')), may hold values from -6 to 6
- mid_latent: bfloat16 [8192, 512], P(('row', 'col')), may hold values from -6 to 6
- send_index: int32 [49152], P(('row', 'col')), may hold values from 0 to 383
- edge_src: int32 [589824], P(('row', 'col')), may hold values from 0 to 575
- edge_dst: int32 [589824], P(('row', 'col')), may hold values from 0 to 383
- edge_count: int32 [256], P(('row', 'col')), may hold values from 1152 to 2304, as said below
- up_row: int32 [98304, 1], P(('row', 'col')), may hold values from 0 to 63; in each aligned block of 384 rows (0 to 383, 384 to 767, ...) at most 12 rows name the same one
- up_node: int32 [98304], P(('row', 'col')), may hold values from 0 to 31
- w_src: bfloat16 [512, 512], replicated, may hold values from -0.25 to 0.25
- w_dst: bfloat16 [512, 512], replicated, may hold values from -0.25 to 0.25
- w_msg: bfloat16 [512, 512], replicated, may hold values from -0.25 to 0.25
- w_node: bfloat16 [1024, 512], replicated, may hold values from -0.1875 to 0.1875
- w_mid: bfloat16 [1024, 512], replicated, may hold values from -0.1875 to 0.1875
- cot_fine: bfloat16 [98304, 512], P(('row', 'col')), may hold values from -6 to 6
- cot_mid: bfloat16 [8192, 512], P(('row', 'col')), may hold values from -6 to 6
Outputs:
- fine_out: bfloat16 [98304, 512], P(('row', 'col'))
- mid_out: bfloat16 [8192, 512], P(('row', 'col'))
- grad_fine: bfloat16 [98304, 512], P(('row', 'col'))
- grad_mid: bfloat16 [8192, 512], P(('row', 'col'))
- weight_grads: float32 [1835008], P(('row', 'col'))
Inputs may be any that keep to these rules, and one draw needn't show every extreme that they name: `up_row`: at most 12 of one device's fine nodes name the same row group, and some device reaches 12 in every draw. `edge_count`: some partition has all 2304 slots live in every draw.
All inputs are finite; a program needn't handle non-finite values.
Results may differ from a plain program's by a relative error of at most 0.023.
Values may be sent and summed in bfloat16 or wider, within the bound.
No kernel may reach another device: no remote copies, remote signals or barrier semaphores. Data moves between devices by JAX's collectives and lax.ppermute only.
A program may use at most 64 MiB of HBM per device.

v0:
```python
import jax
import jax.numpy as jnp
from jax import lax
from jax.sharding import PartitionSpec as P


def padded(block, sides, width):
    for axis, dim in sides:
        count = lax.axis_size(axis)
        forward = [(i, i + 1) for i in range(count - 1)]
        forward.append((count - 1, 0))
        backward = [(target, source) for source, target in forward]
        low = lax.ppermute(
            lax.slice_in_dim(block, block.shape[dim] - width, None, axis=dim), axis, forward
        )
        high = lax.ppermute(lax.slice_in_dim(block, 0, width, axis=dim), axis, backward)
        block = jnp.concatenate([low, block, high], axis=dim)
    return block


def fine_part(
    latent, lower_rim, upper_rim, sources, targets, live_count, w_src, w_dst, w_msg, w_node
):
    extended = jnp.concatenate([latent, lower_rim, upper_rim], axis=0)
    proj_src = jnp.dot(extended, w_src, preferred_element_type=jnp.float32).astype(jnp.bfloat16)
    proj_dst = jnp.dot(latent, w_dst, preferred_element_type=jnp.float32).astype(jnp.bfloat16)
    preact = proj_src[sources].astype(jnp.float32) + proj_dst[targets].astype(jnp.float32)
    edge_live = jnp.arange(sources.shape[0], dtype=jnp.int32) < live_count
    activity = jnp.where(edge_live[:, None], jax.nn.silu(preact), 0.0).astype(jnp.bfloat16)
    message = jnp.dot(activity, w_msg, preferred_element_type=jnp.float32).astype(jnp.bfloat16)
    onehot = (targets[:, None] == jnp.arange(latent.shape[0], dtype=jnp.int32)[None, :]).astype(
        jnp.bfloat16
    )
    aggregate = lax.dot_general(
        onehot, message, (((0,), (0,)), ((), ())), preferred_element_type=jnp.float32
    ).astype(jnp.bfloat16)
    joined = jnp.concatenate([latent, aggregate], axis=1)
    update = jnp.dot(joined, w_node, preferred_element_type=jnp.float32)
    return (latent.astype(jnp.float32) + jax.nn.silu(update)).astype(jnp.bfloat16)


def mid_part(mid_block, mid_total, w_mid):
    up_agg = (0.25 * mid_total).astype(jnp.bfloat16)
    joined = jnp.concatenate([mid_block, up_agg], axis=1)
    update = jnp.dot(joined, w_mid, preferred_element_type=jnp.float32)
    return (mid_block.astype(jnp.float32) + jax.nn.silu(update)).astype(jnp.bfloat16)


def on_device(
    fine_latent,
    mid_latent,
    send_index,
    edge_src,
    edge_dst,
    edge_count,
    up_row,
    up_node,
    w_src,
    w_dst,
    w_msg,
    w_node,
    w_mid,
    cot_fine,
    cot_mid,
):
    row_count = lax.axis_size("row")
    rim_rows = send_index.shape[0] // 2
    mid_rows = mid_latent.shape[0]
    send_rows = fine_latent[send_index]
    extended = padded(send_rows, ((("row", "col"), 0),), rim_rows)
    lower_rim = extended[:rim_rows]
    upper_rim = extended[-rim_rows:]
    live_count = edge_count[0]

    def fine_closure(first, second, third, ws, wd, wm, wn):
        return fine_part(first, second, third, edge_src, edge_dst, live_count, ws, wd, wm, wn)

    fine_out, fine_back = jax.vjp(
        fine_closure, fine_latent, lower_rim, upper_rim, w_src, w_dst, w_msg, w_node
    )
    dest_rows = up_row[:, 0]
    owner_key = dest_rows * mid_rows + up_node
    pick_table = (
        owner_key[:, None] == jnp.arange(row_count * mid_rows, dtype=jnp.int32)[None, :]
    ).astype(jnp.bfloat16)
    partial_sums = lax.dot_general(
        pick_table, fine_out, (((0,), (0,)), ((), ())), preferred_element_type=jnp.float32
    )
    mid_total = lax.psum_scatter(partial_sums, "row", scatter_dimension=0, tiled=True)
    mid_out, mid_back = jax.vjp(mid_part, mid_latent, mid_total, w_mid)
    grad_mid, grad_total, grad_wmid = mid_back(cot_mid)
    gathered = lax.all_gather(grad_total.astype(jnp.bfloat16), "row", axis=0, tiled=True)
    up_grad = jnp.dot(pick_table, gathered, preferred_element_type=jnp.float32).astype(jnp.bfloat16)
    fine_cot = (cot_fine.astype(jnp.float32) + up_grad.astype(jnp.float32)).astype(jnp.bfloat16)
    grad_latent, grad_lower, grad_upper, grad_wsrc, grad_wdst, grad_wmsg, grad_wnode = fine_back(
        fine_cot
    )
    back_rims = padded(
        jnp.concatenate([grad_lower, grad_upper], axis=0), ((("row", "col"), 0),), rim_rows
    )
    send_grads = jnp.concatenate([back_rims[:rim_rows], back_rims[-rim_rows:]], axis=0)
    grad_fine = (
        grad_latent.astype(jnp.float32)
        .at[send_index]
        .add(send_grads.astype(jnp.float32))
        .astype(jnp.bfloat16)
    )
    flat_terms = jnp.concatenate(
        [
            piece.astype(jnp.float32).reshape(-1)
            for piece in (grad_wsrc, grad_wdst, grad_wmsg, grad_wnode, grad_wmid)
        ]
    )
    summed = lax.psum(flat_terms, ("row", "col"))
    shard_size = flat_terms.shape[0] // lax.axis_size(("row", "col"))
    weight_grads = lax.dynamic_slice_in_dim(
        summed, lax.axis_index(("row", "col")) * shard_size, shard_size, 0
    )
    return (fine_out, mid_out, grad_fine, grad_mid, weight_grads)


def solution(mesh):
    return jax.shard_map(
        on_device,
        mesh=mesh,
        in_specs=(
            P(("row", "col"), None),
            P(("row", "col"), None),
            P(("row", "col")),
            P(("row", "col")),
            P(("row", "col")),
            P(("row", "col")),
            P(("row", "col"), None),
            P(("row", "col")),
            P(),
            P(),
            P(),
            P(),
            P(),
            P(("row", "col"), None),
            P(("row", "col"), None),
        ),
        out_specs=(
            P(("row", "col"), None),
            P(("row", "col"), None),
            P(("row", "col"), None),
            P(("row", "col"), None),
            P(("row", "col")),
        ),
        check_vma=False,
    )
```

profile of v0, /device:TPU:1, one launch (start us, length us, event | category | flops | bytes accessed | tf_op | source)
XLA Modules:
  0.0 494.7 jit_solution(18395824678197251713)
XLA Ops:
  8.1 2.1 gather_fusion
  10.2 2.1 collective-permute-start
  12.3 1.9 collective-permute-start.1
  15.5 7.5 %gather_fusion.2 = bf16[2304,512]{1,0:T(8,128)(2,1)} fusion(bf16[384,512]{1,0:T(8,128)(2,1)S(1)} %convolution_convert_fusion.12, s32[3072]{0:T(1024)S(1)} %get-tuple-element.13), kind=kCustom, calls=%fused_computation.2 | custom fusion | bytes 4727808 | tf_op jit(solution)/shard_map/jvp()/gather | solution.py:27
  24.2 7.5 %gather_fusion.1 = bf16[2304,512]{1,0:T(8,128)(2,1)} fusion(bf16[576,512]{1,0:T(8,128)(2,1)S(1)} %convolution_convert_fusion.7, s32[3072]{0:T(1024)S(1)} %get-tuple-element.14), kind=kCustom, calls=%fused_computation.1 | custom fusion | bytes 4727808 | tf_op jit(solution)/shard_map/jvp()/gather | solution.py:27
  31.7 4.6 select_convert_fusion
  36.4 4.0 fusion.12
  40.4 1.5 add_convert_fusion
  42.7 3.3 fusion.5
  46.2 140.7 %reduce-scatter.2.cloned.1.call-done = f32[32,512]{1,0:T(8,128)} async-done(((f32[2048,512]{1,0:T(8,128)}), f32[32,512]{1,0:T(8,128)}) %reduce-scatter.2.cloned.1.call-update) | async-done | bytes 65552 | tf_op jit(solution)/shard_map/reduce_scatter | solution.py:89
  187.8 0.9 add_convert_fusion.1
  191.3 80.5 %all-gather.2.cloned.1.call-done = bf16[2048,512]{1,0:T(8,128)(2,1)} async-done(((bf16[32,512]{1,0:T(8,128)(2,1)}), bf16[2048,512]{1,0:T(8,128)(2,1)}) %all-gather.2.cloned.1.call-update) | async-done | bytes 2097168 | tf_op jit(solution)/shard_map/all_gather | solution.py:92
  271.8 2.7 fusion.16
  276.1 2.0 convolution_convert_fusion.1
  278.1 1.4 copy-done.31
  279.5 4.6 fusion.2
  284.1 16.5 %scatter_custom_fusion = bf16[384,512]{1,0:T(8,128)(2,1)S(1)} fusion(s32[2304]{0:T(1024)} %copy-done.20, bf16[2304,512]{1,0:T(8,128)(2,1)} %fusion.2, bf16[]{:T(256)} %constant.21.clone.1), kind=kCustom, calls=%fused_computation.67 | custom fusion | flops 1179648 | bytes 393728 | tf_op jit(solution)/shard_map/transpose(jvp())/scatter-add | solution.py:27
  300.6 16.9 %scatter_custom_fusion.1 = bf16[576,512]{1,0:T(8,128)(2,1)S(1)} fusion(s32[2304]{0:T(1024)} %copy-done.19, bf16[2304,512]{1,0:T(8,128)(2,1)} %fusion.2, bf16[]{:T(256)} %constant.21.clone.1), kind=kCustom, calls=%fused_computation.62 | custom fusion | flops 1179648 | bytes 590336 | tf_op jit(solution)/shard_map/transpose(jvp())/scatter-add | solution.py:27
  317.5 1.7 convolution_convert_fusion.6
  319.2 1.9 fusion.18
  321.1 4.0 fusion.17
  325.1 1.9 fusion.11
  327.7 2.5 collective-permute-start.3
  331.3 1.3 fusion.19
  332.6 1.3 copy.20
  334.1 1.3 copy.23
  337.6 1.0 constant_dynamic-update-slice_fusion.5
  338.7 1.0 constant_dynamic-update-slice_fusion.4
  339.7 142.0 %all-reduce.1 = f32[1835008]{0:T(1024)} all-reduce(bf16[1835008]{0:T(1024)(128)(2,1)} %constant_dynamic-update-slice_fusion.4), channel_id=1, replica_groups=mesh['row'=64,'col'=4] {'row','col'}, use_global_device_ids=true, to_apply=%region_4.5 | all-reduce | flops 1835008 | bytes 11010048 | tf_op jit(solution)/shard_map/psum | solution.py:114
  481.7 1.6 fusion.22
  483.2 1.4 dynamic_slice.3
  484.6 2.5 scatter_custom_fusion.2
  (109 shorter events, 13.5 us)
Async XLA Ops:
  7.2 33.2 %copy-start = (bf16[1024,512]{1,0:T(8,128)(2,1)S(1)}, bf16[1024,512]{1,0:T(8,128)(2,1)}, u32[]{:S(2)}) copy-start(bf16[1024,512]{1,0:T(8,128)(2,1)} %param.26) | copy-start | bytes 3145732
  7.2 7.1 %copy-start.1 = (bf16[384,512]{1,0:T(8,128)(2,1)S(1)}, bf16[384,512]{1,0:T(8,128)(2,1)}, u32[]{:S(2)}) copy-start(bf16[384,512]{1,0:T(8,128)(2,1)} %param.15) | copy-start | bytes 1179652
  7.2 7.1 %copy-start.9 = (bf16[512,512]{1,0:T(8,128)(2,1)S(1)}, bf16[512,512]{1,0:T(8,128)(2,1)}, u32[]{:S(2)}) copy-start(bf16[512,512]{1,0:T(8,128)(2,1)} %param.24) | copy-start | bytes 1572868
  7.2 7.5 %copy-start.23 = (s32[2304]{0:T(1024)S(1)}, s32[2304]{0:T(1024)}, u32[]{:S(2)}) copy-start(s32[2304]{0:T(1024)} %param.19) | copy-start | bytes 27652
  7.2 7.5 %copy-start.22 = (s32[2304]{0:T(1024)S(1)}, s32[2304]{0:T(1024)}, u32[]{:S(2)}) copy-start(s32[2304]{0:T(1024)} %param.18) | copy-start | bytes 27652
  7.2 8.2 %copy-start.27 = (s32[384,1]{0,1:T(1,128)S(1)}, s32[384,1]{0,1:T(1,128)}, u32[]{:S(2)}) copy-start(s32[384,1]{0,1:T(1,128)} %param.21) | copy-start | bytes 4612
  7.2 179.7 %reduce-scatter.2.cloned.1.call-start = ((), (), s32[]{:S(2)}) async-start(), calls=%async_computation.1 | async-start | bytes 4259840 | tf_op jit(solution)/shard_map/reduce_scatter | solution.py:89
  8.1 6.2 %copy-start.25 = (s32[192]{0:T(256)}, s32[192]{0:T(256)S(1)}, u32[]{:S(2)}) copy-start(s32[192]{0:T(256)S(1)} %compare_select_fusion.2) | copy-start | bytes 2308
  10.2 13.4 %collective-permute-start = (bf16[96,512]{1,0:T(8,128)(2,1)S(1)}, bf16[96,512]{1,0:T(8,128)(2,1)S(1)}, u32[]{:S(2)}, u32[]{:S(2)}) collective-permute-start(bf16[96,512]{1,0:T(8,128)(2,1)S(1)} %get-tuple-element.8), channel_id=1, source_target_pairs={{0,1},{1,2},{2,3},{3,4},{4,5},{5,6},{6,7},{7,8},{8,9},{9,10},{10,1... | collective-permute-start | bytes 294920 | tf_op jit(solution)/shard_map/ppermute | solution.py:13
  12.3 11.3 %collective-permute-start.1 = (bf16[96,512]{1,0:T(8,128)(2,1)S(1)}, bf16[96,512]{1,0:T(8,128)(2,1)S(1)}, u32[]{:S(2)}, u32[]{:S(2)}) collective-permute-start(bf16[96,512]{1,0:T(8,128)(2,1)S(1)} %get-tuple-element.7), channel_id=1, source_target_pairs={{1,0},{2,1},{3,2},{4,3},{5,4},{6,5},{7,6},{8,7},{9,8},{10,9},{11,1... | collective-permute-start | bytes 294920 | tf_op jit(solution)/shard_map/ppermute | solution.py:16
  14.7 8.3 %copy-start.20 = (s32[2304]{0:T(1024)}, s32[2304]{0:T(1024)S(1)}, u32[]{:S(2)}) copy-start(s32[2304]{0:T(1024)S(1)} %compare_select_fusion) | copy-start | bytes 27652
  14.7 8.3 %copy-start.19 = (s32[2304]{0:T(1024)}, s32[2304]{0:T(1024)S(1)}, u32[]{:S(2)}) copy-start(s32[2304]{0:T(1024)S(1)} %compare_select_fusion.1) | copy-start | bytes 27652
  15.5 7.6 %copy-start.26 = (s32[384]{0:T(512)S(1)}, s32[384]{0:T(512)}, u32[]{:S(2)}) copy-start(s32[384]{0:T(512)} %param.22) | copy-start | bytes 4612
  15.5 8.2 %copy-start.8 = (bf16[512,512]{1,0:T(8,128)(2,1)S(1)}, bf16[512,512]{1,0:T(8,128)(2,1)}, u32[]{:S(2)}) copy-start(bf16[512,512]{1,0:T(8,128)(2,1)} %param.23) | copy-start | bytes 1572868
  23.7 8.0 %copy-start.10 = (bf16[576,512]{1,0:T(8,128)(2,1)}, bf16[576,512]{1,0:T(8,128)(2,1)S(1)}, u32[]{:S(2)}) copy-start(bf16[576,512]{1,0:T(8,128)(2,1)S(1)} %constant_dynamic-update-slice_fusion) | copy-start | bytes 1769476
  24.2 7.5 %copy-start.21 = (pred[2304]{0:T(1024)(128)(4,1)S(1)}, pred[2304]{0:T(1024)(128)(4,1)}, u32[]{:S(2)}) copy-start(pred[2304]{0:T(1024)(128)(4,1)} %iota_compare_fusion.16) | copy-start | bytes 6916
  31.7 4.7 copy-start.24
  31.7 4.7 copy-start.28
  46.0 141.8 %copy-start.4 = (bf16[1024,512]{1,0:T(8,128)(2,1)S(1)}, bf16[1024,512]{1,0:T(8,128)(2,1)}, u32[]{:S(2)}) copy-start(bf16[1024,512]{1,0:T(8,128)(2,1)} %param.27) | copy-start | bytes 3145732
  46.0 141.8 %copy-start.16 = (bf16[32,512]{1,0:T(8,128)(2,1)S(1)}, bf16[32,512]{1,0:T(8,128)(2,1)}, u32[]{:S(2)}) copy-start(bf16[32,512]{1,0:T(8,128)(2,1)} %param.16) | copy-start | bytes 98308
  46.0 142.7 %copy-start.17 = (bf16[32,512]{1,0:T(8,128)(2,1)S(1)}, bf16[32,512]{1,0:T(8,128)(2,1)}, u32[]{:S(2)}) copy-start(bf16[32,512]{1,0:T(8,128)(2,1)} %param.29) | copy-start | bytes 98308
  46.0 225.8 %all-gather.2.cloned.1.call-start = ((), (), s32[]{:S(2)}) async-start(), calls=%async_computation.2 | async-start | bytes 2129920 | tf_op jit(solution)/shard_map/all_gather | solution.py:92
  188.7 83.1 %copy-start.30 = (bf16[384,512]{1,0:T(8,128)(2,1)S(1)}, bf16[384,512]{1,0:T(8,128)(2,1)}, u32[]{:S(2)}) copy-start(bf16[384,512]{1,0:T(8,128)(2,1)} %param.28) | copy-start | bytes 1179652
  317.5 3.6 copy-start.7
  319.2 7.8 %copy-start.5 = (bf16[576,512]{1,0:T(8,128)(2,1)}, bf16[576,512]{1,0:T(8,128)(2,1)S(1)}, u32[]{:S(2)}) copy-start(bf16[576,512]{1,0:T(8,128)(2,1)S(1)} %convolution_convert_fusion.6) | copy-start | bytes 1769476
  321.1 4.0 copy-start.14
  321.1 4.0 copy-start.33
  321.1 4.0 copy-start.35
  327.7 156.9 %collective-permute-start.3 = (bf16[96,512]{1,0:T(8,128)(2,1)}, bf16[96,512]{1,0:T(8,128)(2,1)}, u32[]{:S(2)}, u32[]{:S(2)}) collective-permute-start(bf16[96,512]{1,0:T(8,128)(2,1)} %get-tuple-element.6), channel_id=1, source_target_pairs={{1,0},{2,1},{3,2},{4,3},{5,4},{6,5},{7,6},{8,7},{9,8},{10,9},{11,1... | collective-permute-start | bytes 294920 | tf_op jit(solution)/shard_map/ppermute | solution.py:16
  330.2 154.4 %collective-permute-start.2 = (bf16[96,512]{1,0:T(8,128)(2,1)}, bf16[96,512]{1,0:T(8,128)(2,1)}, u32[]{:S(2)}, u32[]{:S(2)}) collective-permute-start(bf16[96,512]{1,0:T(8,128)(2,1)} %get-tuple-element.5), channel_id=1, source_target_pairs={{0,1},{1,2},{2,3},{3,4},{4,5},{5,6},{6,7},{7,8},{8,9},{9,10},{10,1... | collective-permute-start | bytes 294920 | tf_op jit(solution)/shard_map/ppermute | solution.py:13
  339.7 142.0 %copy-start.6 = (bf16[576,512]{1,0:T(8,128)(2,1)S(1)}, bf16[576,512]{1,0:T(8,128)(2,1)}, u32[]{:S(2)}) copy-start(bf16[576,512]{1,0:T(8,128)(2,1)} %copy-done.5) | copy-start | bytes 1769476
  339.7 142.0 %copy-start.15 = (bf16[384,512]{1,0:T(8,128)(2,1)S(1)}, bf16[384,512]{1,0:T(8,128)(2,1)}, u32[]{:S(2)}) copy-start(bf16[384,512]{1,0:T(8,128)(2,1)} %copy-done.13) | copy-start | bytes 1179652
  (10 other events, 19.8 us)
Sparse Core Ops, SparseCore 0:
  46.1 140.7 reduce-scatter.1
  190.6 81.1 all-gather.1
where the time goes:
time: 496 us; the launch traced here: 495 us
  waiting for transfers between devices  221 us (45%)
  blocking collectives  142 us (29%)
  other arithmetic  44.8 us (9%)
  matrix products  33.6 us (7%)
  local copies, waits for them, and re-layouts  31 us (6%)
  between operations  15.2 us (3%)
  starting transfers between devices  6.84 us (1%)
    psum x1, blocking collectives, on_device(): summed = lax.psum(flat_terms, ('row', 'col'))  142 us
    reduce_scatter x1, waiting for transfers between devices, on_device(): lax.psum_scatter(partial_sums, 'row', scatter_dimension=0, tiled=True)  141 us
    all_gather x1, waiting for transfers between devices, on_device(): lax.all_gather(grad_total.astype(jnp.bfloat16), 'row', axis=0, tiled=True)  80.5 us
    scatter-add x1, other arithmetic, fine_part(): proj_src[sources].astype(jnp.float32)  16.9 us
    scatter-add x1, other arithmetic, fine_part(): proj_dst[targets].astype(jnp.float32)  16.5 us
  transfers between devices with their start and end apart: 6, of which 2 were waited for; matrix products, arithmetic and copies ran while one was open for 5% of the time, Pallas kernels for 0%

commit v1 on v0

v1 whole, which is shorter than its diff:
```python
import jax
import jax.numpy as jnp
from jax import lax
from jax.sharding import PartitionSpec as P

BF = jnp.bfloat16
F32 = jnp.float32
BOTH = ("row", "col")
CAP = 12
ZN, YN, CN, XN = 8, 4, 2, 4
PLANE = YN * CN


def place(z, y, c, x):
    return ((z * YN + y) * CN + c) * XN + x


def shift(dz=0, dy=0, dc=0, dx=0):
    return [
        (place(z, y, c, x), place((z + dz) % ZN, (y + dy) % YN, (c + dc) % CN, (x + dx) % XN))
        for z in range(ZN)
        for y in range(YN)
        for c in range(CN)
        for x in range(XN)
    ]


PLANES = [[z * PLANE + i for i in range(PLANE)] for z in range(ZN)]
PILLARS = [[z * PLANE + i for z in range(ZN)] for i in range(PLANE)]


def dot(a, b):
    return jnp.dot(a, b, preferred_element_type=F32)


def dot_t(a, b):
    return lax.dot_general(a, b, (((0,), (0,)), ((), ())), preferred_element_type=F32)


def dot_nt(a, b):
    return lax.dot_general(a, b, (((1,), (1,)), ((), ())), preferred_element_type=F32)


def one_hot(index, count):
    return (index[:, None] == jnp.arange(count, dtype=jnp.int32)[None, :]).astype(BF)


def pick(block, index, axis):
    return lax.dynamic_index_in_dim(block, index, axis, keepdims=False)


def silu_pair(u):
    s = jax.nn.sigmoid(u)
    return u * s, s * (1.0 + u * (1.0 - s))


def reduce_weights(flat):
    row = lax.axis_index("row")
    core, yy, xx = row % CN, (row // CN) % YN, lax.axis_index("col")
    cut = flat.astype(BF).reshape(ZN * YN, CN, XN * 14, 512)
    got = lax.ppermute(pick(cut, 1 - core, 1), BOTH, shift(dc=1))
    part = (pick(cut, core, 1).astype(F32) + got.astype(F32)).astype(BF)
    part = part.reshape(ZN * YN, XN, 14, 512)
    terms = [pick(part, xx, 1)]
    for d in (1, 3, 2):
        terms.append(lax.ppermute(pick(part, (xx + d) % XN, 1), BOTH, shift(dx=d)))
    part = sum(t.astype(F32) for t in terms).astype(BF).reshape(ZN, YN, 14, 512)
    terms = [pick(part, yy, 1)]
    for d in (1, 3, 2):
        terms.append(lax.ppermute(pick(part, (yy + d) % YN, 1), BOTH, shift(dy=d)))
    part = sum(t.astype(F32) for t in terms).astype(BF)
    got = lax.all_to_all(part, "row", 0, 0, axis_index_groups=PILLARS)
    return jnp.sum(got.astype(F32), axis=0).reshape(-1)


def on_device(
    fine_latent,
    mid_latent,
    send_index,
    edge_src,
    edge_dst,
    edge_count,
    up_row,
    up_node,
    w_src,
    w_dst,
    w_msg,
    w_node,
    w_mid,
    cot_fine,
    cot_mid,
):
    nodes, width = fine_latent.shape
    rim = send_index.shape[0] // 2
    mids = mid_latent.shape[0]
    row = lax.axis_index("row")

    pick_send = one_hot(send_index, nodes)
    send_rows = dot(pick_send, fine_latent).astype(BF)
    ahead = [(i, (i + 1) % 256) for i in range(256)]
    behind = [(j, i) for i, j in ahead]
    lower_rim = lax.ppermute(send_rows[rim:], BOTH, ahead)
    upper_rim = lax.ppermute(send_rows[:rim], BOTH, behind)

    dest = up_row[:, 0]
    same = dest[:, None] == dest[None, :]
    earlier = jnp.arange(nodes)[None, :] < jnp.arange(nodes)[:, None]
    rank = jnp.sum((same & earlier).astype(jnp.int32), axis=1)
    spot = (dest % PLANE) * (ZN * CAP) + (dest // PLANE) * CAP + rank
    slots = PLANE * ZN * CAP
    to_slot = one_hot(spot, slots)
    names = dot_t(to_slot, (up_node + 1).astype(BF)[:, None])[:, 0].astype(jnp.int32) - 1
    names = lax.all_gather(
        names.reshape(PLANE, ZN * CAP), "row", axis_index_groups=PLANES
    )
    names = pick(names, row % PLANE, 1)
    level = (jnp.arange(ZN * CAP, dtype=jnp.int32) // CAP * mids)[None, :]
    owner = jnp.where(names >= 0, names + level, -1).reshape(-1)
    to_mid = one_hot(owner, ZN * mids)

    extended = jnp.concatenate([fine_latent, lower_rim, upper_rim], axis=0)
    proj_src = dot(extended, w_src).astype(BF)
    proj_dst = dot(fine_latent, w_dst).astype(BF)
    ends = jnp.concatenate(
        [one_hot(edge_src, extended.shape[0]), one_hot(edge_dst, nodes)], axis=1
    )
    preact = dot(ends, jnp.concatenate([proj_src, proj_dst], axis=0))
    live = (jnp.arange(edge_src.shape[0], dtype=jnp.int32) < edge_count[0])[:, None]
    act, slope = silu_pair(preact)
    act = jnp.where(live, act, 0.0).astype(BF)
    slope = jnp.where(live, slope, 0.0).astype(BF)
    pick_dst = one_hot(edge_dst, nodes)
    gathered = dot_t(pick_dst, act).astype(BF)
    aggregate = dot(gathered, w_msg).astype(BF)
    joined = jnp.concatenate([fine_latent, aggregate], axis=1)
    lift, node_slope = silu_pair(dot(joined, w_node))
    fine_out = (fine_latent.astype(F32) + lift).astype(BF)

    sent = dot_t(to_slot, fine_out).astype(BF).reshape(PLANE, ZN * CAP, width)
    got = lax.all_to_all(sent, "row", 0, 0, axis_index_groups=PLANES).reshape(slots, width)
    sums = dot_t(to_mid, got).astype(BF).reshape(ZN, mids, width)
    sums = lax.all_to_all(sums, "row", 0, 0, axis_index_groups=PILLARS)
    mid_total = jnp.sum(sums.astype(F32), axis=0)
    up_agg = (0.25 * mid_total).astype(BF)
    mid_joined = jnp.concatenate([mid_latent, up_agg], axis=1)
    mid_lift, mid_slope = silu_pair(dot(mid_joined, w_mid))
    mid_out = (mid_latent.astype(F32) + mid_lift).astype(BF)
    mid_back = (cot_mid.astype(F32) * mid_slope).astype(BF)
    grad_joined = dot_nt(mid_back, w_mid).astype(BF)
    grad_mid = (cot_mid.astype(F32) + grad_joined[:, :width].astype(F32)).astype(BF)
    grad_total = (0.25 * grad_joined[:, width:].astype(F32)).astype(BF)
    grad_wmid = dot_t(mid_joined, mid_back)

    spread = jnp.broadcast_to(grad_total[None], (ZN, mids, width))
    spread = lax.all_to_all(spread, "row", 0, 0, axis_index_groups=PILLARS)
    back = dot(to_mid, spread.reshape(ZN * mids, width)).astype(BF)
    back = lax.all_to_all(
        back.reshape(PLANE, ZN * CAP, width), "row", 0, 0, axis_index_groups=PLANES
    )
    up_grad = dot(to_slot, back.reshape(slots, width))
    fine_cot = (cot_fine.astype(F32) + up_grad).astype(BF)

    node_back = (fine_cot.astype(F32) * node_slope).astype(BF)
    grad_node = dot_nt(node_back, w_node).astype(BF)
    grad_wnode = dot_t(joined, node_back)
    grad_agg = grad_node[:, width:]
    grad_wmsg = dot_t(gathered, grad_agg)
    grad_gathered = dot_nt(grad_agg, w_msg).astype(BF)
    grad_edge = (dot(pick_dst, grad_gathered) * slope.astype(F32)).astype(BF)
    grad_ends = dot_t(ends, grad_edge).astype(BF)
    grad_src, grad_dst = grad_ends[: extended.shape[0]], grad_ends[extended.shape[0] :]
    grad_wsrc = dot_t(extended, grad_src)
    grad_wdst = dot_t(fine_latent, grad_dst)
    grad_ext = dot_nt(grad_src, w_src)
    rims = grad_ext[nodes:].astype(BF)
    from_low = lax.ppermute(rims[rim:], BOTH, ahead)
    from_high = lax.ppermute(rims[:rim], BOTH, behind)
    direct = (
        fine_cot.astype(F32)
        + grad_node[:, :width].astype(F32)
        + grad_ext[:nodes]
        + dot_nt(grad_dst, w_dst)
    )
    returned = dot_t(pick_send, jnp.concatenate([from_low, from_high], axis=0))
    grad_fine = (direct + returned).astype(BF)

    flat = jnp.concatenate([grad_wsrc, grad_wdst, grad_wmsg, grad_wnode, grad_wmid], axis=0)
    return fine_out, mid_out, grad_fine, grad_mid, reduce_weights(flat)


def solution(mesh):
    rows, line = P(BOTH, None), P(BOTH)
    return jax.shard_map(
        on_device,
        mesh=mesh,
        in_specs=(rows, rows, line, line, line, line, rows, line)
        + (P(),) * 5
        + (rows, rows),
        out_specs=(rows, rows, rows, rows, line),
        check_vma=False,
    )
```

time: 496 us -> 190 us (0.38)
  waiting for transfers between devices: 221 us -> 44.1 us
  blocking collectives: 142 us -> 49.8 us
  other arithmetic: 44.8 us -> 8.31 us
  starting transfers between devices: 6.84 us -> 31.7 us
  local copies, waits for them, and re-layouts: 31 us -> 11.5 us
  between operations: 15.2 us -> 1.95 us
  matrix products: 33.6 us -> 41.1 us
    psum x1 -> x0, blocking collectives: 142 us -> none  [on_device(): summed = lax.psum(flat_terms, ('row', 'col'))]
    reduce_scatter x1 -> x0, waiting for transfers between devices: 141 us -> none  [on_device(): lax.psum_scatter(partial_sums, 'row', scatter_dimension=0, tiled=True)]
    all_gather x1 -> x0, waiting for transfers between devices: 80.5 us -> none  [on_device(): lax.all_gather(grad_total.astype(jnp.bfloat16), 'row', axis=0, tiled=True)]
    scatter-add x3 -> x0, other arithmetic: 35.8 us -> none  [the longest x1 16.9 us: fine_part(): proj_src[sources].astype(jnp.float32)]
    all_to_all x0 -> x2, blocking collectives: none -> 31.4 us  [the longest x1 17.4 us: on_device(): sums = lax.all_to_all(sums, 'row', 0, 0, axis_index_groups=PILLARS)]
    ppermute x4 -> x11, waiting for transfers between devices: 0.01 us -> 26 us  [the longest x3 18.5 us: reduce_weights(): terms.append(lax.ppermute(pick(part, (xx + d) % XN, 1), BOTH, shift(dx=d)))]
    all_to_all x0 -> x3, starting transfers between devices: none -> 19.8 us  [the longest x1 11.8 us: on_device(): lax.all_to_all(sent, 'row', 0, 0, axis_index_groups=PLANES)]
    all_gather x0 -> x1, blocking collectives: none -> 18.4 us  [on_device(): lax.all_gather(names.reshape(PLANE, ZN * CAP), 'row', axis_index_groups=P...]
  transfers between devices with their start and end apart: 6 -> 14, of which waited for: 2 -> 9; matrix products, arithmetic and copies ran while one was open for 5% -> 8% of each run, Pallas kernels for 0% -> 0%
where the time goes in v1:
time: 190 us; the launch traced here: 188 us
  blocking collectives  49.8 us (26%)
  waiting for transfers between devices  44.1 us (23%)
  matrix products  41.1 us (22%)
  starting transfers between devices  31.7 us (17%)
  local copies, waits for them, and re-layouts  11.5 us (6%)
  other arithmetic  8.31 us (4%)
  between operations  1.95 us (1%)
    dot_general x10, matrix products, dot(): return jnp.dot(a, b, preferred_element_type=F32)  20.6 us
    ppermute x3, waiting for transfers between devices, reduce_weights(): terms.append(lax.ppermute(pick(part, (xx + d) % XN, 1), BOTH, shift(dx=d)))  18.5 us
    all_gather x1, blocking collectives, on_device(): lax.all_gather(names.reshape(PLANE, ZN * CAP), 'row', axis_index_groups=P...  18.4 us
    all_to_all x1, blocking collectives, on_device(): sums = lax.all_to_all(sums, 'row', 0, 0, axis_index_groups=PILLARS)  17.4 us
    dot_general x11, matrix products, dot_t(): lax.dot_general(a, b, (((0,), (0,)), ((), ())), preferred_element_type=F32)  16.7 us
    all_to_all x1, blocking collectives, on_device(): spread = lax.all_to_all(spread, 'row', 0, 0, axis_index_groups=PILLARS)  14 us
    all_to_all x1, waiting for transfers between devices, on_device(): lax.all_to_all(back.reshape(PLANE, ZN * CAP, width), 'row', 0, 0, axis_in...  12.3 us
    all_to_all x1, starting transfers between devices, on_device(): lax.all_to_all(sent, 'row', 0, 0, axis_index_groups=PLANES)  11.8 us
  transfers between devices with their start and end apart: 14, of which 9 were waited for; matrix products, arithmetic and copies ran while one was open for 8% of the time, Pallas kernels for 0%

profile of v1, /device:TPU:1, one launch (start us, length us, event | category | flops | bytes accessed | tf_op | source)
XLA Modules:
  0.0 188.4 jit_solution(2526061023568887937)
XLA Ops:
  0.7 1.5 convolution_convert_fusion.13
  2.8 2.0 %collective-permute-start = (bf16[96,512]{1,0:T(8,128)(2,1)}, bf16[96,512]{1,0:T(8,128)(2,1)}, u32[]{:S(2)}, u32[]{:S(2)}) collective-permute-start(bf16[96,512]{1,0:T(8,128)(2,1)} %get-tuple-element.17), channel_id=1, source_target_pairs={{0,1},{1,2},{2,3},{3,4},{4,5},{5,6},{6,7},{7,8},{8,9},{9,10},{10,1... | collective-permute-start | bytes 294920 | tf_op jit(solution)/shard_map/ppermute | solution.py:102
  4.9 1.9 %collective-permute-start.1 = (bf16[96,512]{1,0:T(8,128)(2,1)}, bf16[96,512]{1,0:T(8,128)(2,1)}, u32[]{:S(2)}, u32[]{:S(2)}) collective-permute-start(bf16[96,512]{1,0:T(8,128)(2,1)} %get-tuple-element.16), channel_id=1, source_target_pairs={{1,0},{2,1},{3,2},{4,3},{5,4},{6,5},{7,6},{8,7},{9,8},{10,9},{11,1... | collective-permute-start | bytes 294920 | tf_op jit(solution)/shard_map/ppermute | solution.py:103
  7.8 2.4 %iota_compare_fusion.1 = pred[2304,384]{1,0:T(32,128)(4,1)} fusion(s32[2304]{0:T(1024)} %param.19), kind=kLoop, calls=%fused_computation.9 | loop fusion | flops 884736 | bytes 893952 | tf_op jit(solution)/shard_map/eq | solution.py:45
  10.3 2.2 %iota_compare_fusion = pred[2304,576]{1,0:T(32,128)(4,1)} fusion(s32[2304]{0:T(1024)S(1)} %copy-done.24), kind=kLoop, calls=%fused_computation.1 | loop fusion | flops 1327104 | bytes 1336320 | tf_op jit(solution)/shard_map/eq | solution.py:45
  16.1 4.2 %fusion.2 = f32[2304,512]{1,0:T(8,128)S(1)} fusion(pred[2304,384]{1,0:T(32,128)(4,1)} %iota_compare_fusion.1, pred[2304,576]{1,0:T(32,128)(4,1)} %iota_compare_fusion, bf16[384,512]{1,0:T(8,128)(2,1)S(1)} %convolution_convert_fusion.11, bf16[576,512]{1,0:T(8,128)(2,1)S(1)} %convolution_convert_fusion.5), kind=kOutput, calls=%fused_computation.10 | convolution fusion | flops 2269102080 | bytes 7913472 | tf_op jit(solution)/shard_map/dot_general | solution.py:33
  20.4 2.2 %fusion.15 = bf16[384,512]{1,0:T(8,128)(2,1)S(1)} fusion(f32[2304,512]{1,0:T(8,128)S(1)} %fusion.2, pred[2304]{0:T(1024)(128)(4,1)S(1)} %iota_compare_fusion.19, s32[2304]{0:T(1024)S(1)} %copy-done.25), kind=kOutput, calls=%fused_computation.40 | convolution fusion | flops 914128896 | bytes 5123328 | tf_op jit(solution)/shard_map/dot_general | solution.py:37
  22.9 1.5 add_convert_fusion
  25.2 1.6 convolution_convert_fusion.4
  26.8 11.8 %all-to-all-start = ((bf16[8,96,512]{2,1,0:T(8,128)(2,1)}), bf16[8,96,512]{2,1,0:T(8,128)(2,1)}, u32[]{:S(2)}, u32[]{:S(2)}) async-start(bf16[8,96,512]{2,1,0:T(8,128)(2,1)} %bitcast.77), calls=%async_computation | async-start | bytes 1572864 | tf_op jit(solution)/shard_map/all_to_all | solution.py:140
  39.0 18.4 %all_gather.3 = s32[8,8,96]{2,1,0:T(8,128)S(1)} all-gather(s32[1,8,96]{2,1,0:T(8,128)S(1)} %sub.39), channel_id=1, replica_groups={{0,4,8,12,16,20,24,28},{32,36,40,44,48,52,56,60},{64,68,72,76,80,84,88,..., dimensions={0}, use_global_device_ids=true | all-gather | bytes 27648 | tf_op jit(solution)/shard_map/all_gather | solution.py:113
  57.7 1.7 convolution_convert_fusion.12
  59.4 17.4 %all_to_all.25 = bf16[8,32,512]{2,1,0:T(8,128)(2,1)S(1)} all-to-all(bf16[8,32,512]{2,1,0:T(8,128)(2,1)S(1)} %bitcast.78), channel_id=1, replica_groups={{0,32,64,96,128,160,192,224},{4,36,68,100,132,164,196,228},{8,40,72,104..., dimensions={0} | all-to-all | bytes 524288 | tf_op jit(solution)/shard_map/all_to_all | solution.py:142
  78.8 14.0 %all_to_all.26 = bf16[8,32,512]{2,1,0:T(8,128)(2,1)S(1)} all-to-all(bf16[8,32,512]{2,1,0:T(8,128)(2,1)S(1)} %broadcast_in_dim.18), channel_id=1, replica_groups={{0,32,64,96,128,160,192,224},{4,36,68,100,132,164,196,228},{8,40,72,104..., dimensions={0} | all-to-all | bytes 524288 | tf_op jit(solution)/shard_map/all_to_all | solution.py:155
  94.2 4.6 %all-to-all-start.3 = ((bf16[8,96,512]{2,1,0:T(8,128)(2,1)}), bf16[8,96,512]{2,1,0:T(8,128)(2,1)S(1)}, u32[]{:S(2)}, u32[]{:S(2)}) async-start(bf16[8,96,512]{2,1,0:T(8,128)(2,1)} %bitcast.5), calls=%async_computation.3 | async-start | bytes 1572864 | tf_op jit(solution)/shard_map/all_to_all | solution.py:157
  98.9 12.3 %all-to-all-done.3 = bf16[8,96,512]{2,1,0:T(8,128)(2,1)S(1)} async-done(((bf16[8,96,512]{2,1,0:T(8,128)(2,1)}), bf16[8,96,512]{2,1,0:T(8,128)(2,1)S(1)}, u32[]{:S(2)}, u32[]{:S(2)}) %all-to-all-start.3) | async-done | bytes 786464 | tf_op jit(solution)/shard_map/all_to_all | solution.py:157
  111.2 2.8 %multiply_convert_fusion = (bf16[384,512]{1,0:T(8,128)(2,1)S(1)}, f32[384,512]{1,0:T(8,128)}) fusion(f32[384,512]{1,0:T(8,128)} %get-tuple-element.21, bf16[768,512]{1,0:T(8,128)(2,1)S(1)} %bitcast.76, s32[384]{0:T(512)S(1)} %copy-done.30, bf16[384,512]{1,0:T(8,128)(2,1)} %param.28), kind=kOutput, calls=%fused_computation.58 | convolution fusion | flops 304840704 | bytes 3147264 | tf_op jit(solution)/shard_map/dot_general | solution.py:33
  114.7 1.5 convolution_convert_fusion.2
  116.2 7.2 %fusion = bf16[2304,512]{1,0:T(8,128)(2,1)} fusion(f32[2304,512]{1,0:T(8,128)} %copy-done.34, pred[2304]{0:T(1024)(128)(4,1)S(1)} %iota_compare_fusion.19, s32[2304]{0:T(1024)S(1)} %copy-done.25, bf16[512,512]{1,0:T(8,128)(2,1)} %param.25, bf16[384,1024]{1,0:T(8,128)(2,1)} %convolution_convert_fusion.2), kind=kOutput, calls=%fused_computation.6 | convolution fusion | flops 1122533376 | bytes 8006912 | tf_op jit(solution)/shard_map/dot_general | solution.py:33
  123.4 6.1 %fusion.9 = bf16[960,512]{1,0:T(8,128)(2,1)S(1)} fusion(bf16[2304,512]{1,0:T(8,128)(2,1)} %fusion, pred[2304,384]{1,0:T(32,128)(4,1)} %iota_compare_fusion.1, pred[2304,576]{1,0:T(32,128)(4,1)S(1)} %copy-done.8), kind=kOutput, calls=%fused_computation.21 | convolution fusion | flops 2267627520 | bytes 5554176 | tf_op jit(solution)/shard_map/dot_general | solution.py:37
  133.3 1.9 copy.57
  136.0 3.8 %collective-permute-done.4 = bf16[32,56,512]{2,0,1:T(8,128)(2,1)} collective-permute-done((bf16[32,56,512]{2,0,1:T(8,128)(2,1)}, bf16[32,56,512]{2,0,1:T(8,128)(2,1)}, u32[]{:S(2)}, u32[]{:S(2)}) %collective-permute-start.4) | collective-permute-done | bytes 1835040 | tf_op jit(solution)/shard_map/ppermute | solution.py:61
  139.8 2.3 %fusion.1 = bf16[32,56,512]{2,0,1:T(8,128)(2,1)S(1)} fusion(bf16[32,56,512]{2,0,1:T(8,128)(2,1)} %collective-permute-done.4, bf16[32,1,56,512]{3,2,1,0:T(8,128)(2,1)S(1)} %get-tuple-element.5), kind=kLoop, calls=%fused_computation.8 | loop fusion | flops 3670016 | bytes 5505024 | tf_op jit(solution)/shard_map/convert_element_type | solution.py:62
  145.3 2.3 %collective-permute-start.3 = (bf16[96,512]{1,0:T(8,128)(2,1)}, bf16[96,512]{1,0:T(8,128)(2,1)}, u32[]{:S(2)}, u32[]{:S(2)}) collective-permute-start(bf16[96,512]{1,0:T(8,128)(2,1)} %get-tuple-element.11), channel_id=1, source_target_pairs={{1,0},{2,1},{3,2},{4,3},{5,4},{6,5},{7,6},{8,7},{9,8},{10,9},{11,1... | collective-permute-start | bytes 294920 | tf_op jit(solution)/shard_map/ppermute | solution.py:177
  147.6 8.0 %collective-permute-done.7 = bf16[32,14,512]{2,0,1:T(8,128)(2,1)S(1)} collective-permute-done((bf16[32,14,512]{2,0,1:T(8,128)(2,1)S(1)}, bf16[32,14,512]{2,0,1:T(8,128)(2,1)S(1)}, u32[]{:S(2)}, u32[]{:S(2)}) %collective-permute-start.7) | collective-permute-done | bytes 458784 | tf_op jit(solution)/shard_map/ppermute | solution.py:66
  155.6 5.8 %collective-permute-done.6 = bf16[32,14,512]{2,0,1:T(8,128)(2,1)S(1)} collective-permute-done((bf16[32,14,512]{2,0,1:T(8,128)(2,1)S(1)}, bf16[32,14,512]{2,0,1:T(8,128)(2,1)S(1)}, u32[]{:S(2)}, u32[]{:S(2)}) %collective-permute-start.6) | collective-permute-done | bytes 458784 | tf_op jit(solution)/shard_map/ppermute | solution.py:66
  161.5 4.6 %collective-permute-done.5 = bf16[32,14,512]{2,0,1:T(8,128)(2,1)S(1)} collective-permute-done((bf16[32,14,512]{2,0,1:T(8,128)(2,1)S(1)}, bf16[32,14,512]{2,0,1:T(8,128)(2,1)S(1)}, u32[]{:S(2)}, u32[]{:S(2)}) %collective-permute-start.5) | collective-permute-done | bytes 458784 | tf_op jit(solution)/shard_map/ppermute | solution.py:66
  167.8 2.7 %collective-permute-start.9 = (bf16[8,14,512]{2,0,1:T(8,128)(2,1)S(1)}, bf16[8,14,512]{2,0,1:T(8,128)(2,1)S(1)}, u32[]{:S(2)}, u32[]{:S(2)}) collective-permute-start(bf16[8,14,512]{2,0,1:T(8,128)(2,1)S(1)} %bitcast.80), channel_id=1, source_target_pairs={{0,24},{1,25},{2,26},{3,27},{4,28},{5,29},{6,30},{7,31},{8,0},{9,1... | collective-permute-start | bytes 344072 | tf_op jit(solution)/shard_map/ppermute | solution.py:70
  173.3 2.3 %collective-permute-done.9 = bf16[8,14,512]{2,0,1:T(8,128)(2,1)S(1)} collective-permute-done((bf16[8,14,512]{2,0,1:T(8,128)(2,1)S(1)}, bf16[8,14,512]{2,0,1:T(8,128)(2,1)S(1)}, u32[]{:S(2)}, u32[]{:S(2)}) %collective-permute-start.9) | collective-permute-done | bytes 114720 | tf_op jit(solution)/shard_map/ppermute | solution.py:70
  176.5 3.4 %all-to-all-start.4 = ((bf16[8,14,512]{2,1,0:T(8,128)(2,1)}), bf16[8,14,512]{2,1,0:T(8,128)(2,1)S(1)}, u32[]{:S(2)}, u32[]{:S(2)}) async-start(bf16[8,14,512]{2,1,0:T(8,128)(2,1)} %copy.41), calls=%async_computation.4 | async-start | bytes 262144 | tf_op jit(solution)/shard_map/all_to_all | solution.py:72
  179.9 2.1 %fusion.14 = bf16[384,512]{1,0:T(8,128)(2,1)} fusion(f32[384,512]{1,0:T(8,128)S(1)} %convolution_add_fusion, bf16[96,512]{1,0:T(8,128)(2,1)} %collective-permute-done.3, bf16[96,512]{1,0:T(8,128)(2,1)} %collective-permute-done.2, s32[192]{0:T(256)S(1)} %copy-done.27), kind=kOutput, calls=%fused_computation.36 | convolution fusion | flops 76357632 | bytes 1377024 | tf_op jit(solution)/shard_map/dot_general | solution.py:37
  182.0 5.8 %all-to-all-done.4 = bf16[8,14,512]{2,1,0:T(8,128)(2,1)S(1)} async-done(((bf16[8,14,512]{2,1,0:T(8,128)(2,1)}), bf16[8,14,512]{2,1,0:T(8,128)(2,1)S(1)}, u32[]{:S(2)}, u32[]{:S(2)}) %all-to-all-start.4) | async-done | bytes 114720 | tf_op jit(solution)/shard_map/all_to_all | solution.py:72
  (133 shorter events, 24.2 us)
Async XLA Ops:
  0.6 22.3 %copy-start = (bf16[1024,512]{1,0:T(8,128)(2,1)S(1)}, bf16[1024,512]{1,0:T(8,128)(2,1)}, u32[]{:S(2)}) copy-start(bf16[1024,512]{1,0:T(8,128)(2,1)} %param.26) | copy-start | bytes 3145732
  0.6 11.8 %copy-start.2 = (bf16[384,512]{1,0:T(8,128)(2,1)S(1)}, bf16[384,512]{1,0:T(8,128)(2,1)}, u32[]{:S(2)}) copy-start(bf16[384,512]{1,0:T(8,128)(2,1)} %param.15) | copy-start | bytes 1179652
  0.7 9.6 %copy-start.24 = (s32[2304]{0:T(1024)S(1)}, s32[2304]{0:T(1024)}, u32[]{:S(2)}) copy-start(s32[2304]{0:T(1024)} %param.18) | copy-start | bytes 27652
  0.7 11.8 %copy-start.3 = (bf16[512,512]{1,0:T(8,128)(2,1)S(1)}, bf16[512,512]{1,0:T(8,128)(2,1)}, u32[]{:S(2)}) copy-start(bf16[512,512]{1,0:T(8,128)(2,1)} %param.24) | copy-start | bytes 1572868
  2.1 11.3 %copy-start.26 = (s32[384,1]{0,1:T(1,128)S(1)}, s32[384,1]{0,1:T(1,128)}, u32[]{:S(2)}) copy-start(s32[384,1]{0,1:T(1,128)} %param.21) | copy-start | bytes 4612
  2.8 10.9 %copy-start.28 = (s32[384]{0:T(512)S(1)}, s32[384]{0:T(512)}, u32[]{:S(2)}) copy-start(s32[384]{0:T(512)} %param.22) | copy-start | bytes 4612
  2.8 11.0 %collective-permute-start = (bf16[96,512]{1,0:T(8,128)(2,1)}, bf16[96,512]{1,0:T(8,128)(2,1)}, u32[]{:S(2)}, u32[]{:S(2)}) collective-permute-start(bf16[96,512]{1,0:T(8,128)(2,1)} %get-tuple-element.17), channel_id=1, source_target_pairs={{0,1},{1,2},{2,3},{3,4},{4,5},{5,6},{6,7},{7,8},{8,9},{9,10},{10,1... | collective-permute-start | bytes 294920 | tf_op jit(solution)/shard_map/ppermute | solution.py:102
  4.9 10.8 %copy-start.5 = (bf16[512,512]{1,0:T(8,128)(2,1)S(1)}, bf16[512,512]{1,0:T(8,128)(2,1)}, u32[]{:S(2)}) copy-start(bf16[512,512]{1,0:T(8,128)(2,1)} %param.23) | copy-start | bytes 1572868
  4.9 9.8 %collective-permute-start.1 = (bf16[96,512]{1,0:T(8,128)(2,1)}, bf16[96,512]{1,0:T(8,128)(2,1)}, u32[]{:S(2)}, u32[]{:S(2)}) collective-permute-start(bf16[96,512]{1,0:T(8,128)(2,1)} %get-tuple-element.16), channel_id=1, source_target_pairs={{1,0},{2,1},{3,2},{4,3},{5,4},{6,5},{7,6},{8,7},{9,8},{10,9},{11,1... | collective-permute-start | bytes 294920 | tf_op jit(solution)/shard_map/ppermute | solution.py:103
  13.8 24.8 %copy-start.29 = (s32[384]{0:T(512)}, s32[384]{0:T(512)S(1)}, u32[]{:S(2)}) copy-start(s32[384]{0:T(512)S(1)} %fusion.55) | copy-start | bytes 4612
  15.6 4.7 %copy-start.6 = (bf16[576,512]{1,0:T(8,128)(2,1)}, bf16[576,512]{1,0:T(8,128)(2,1)S(1)}, u32[]{:S(2)}) copy-start(bf16[576,512]{1,0:T(8,128)(2,1)S(1)} %constant_dynamic-update-slice_fusion) | copy-start | bytes 1769476
  16.1 4.2 %copy-start.25 = (s32[2304]{0:T(1024)S(1)}, s32[2304]{0:T(1024)}, u32[]{:S(2)}) copy-start(s32[2304]{0:T(1024)} %param.19) | copy-start | bytes 27652
  26.8 50.0 %copy-start.1 = (bf16[1024,512]{1,0:T(8,128)(2,1)S(1)}, bf16[1024,512]{1,0:T(8,128)(2,1)}, u32[]{:S(2)}) copy-start(bf16[1024,512]{1,0:T(8,128)(2,1)} %param.27) | copy-start | bytes 3145732
  26.8 50.0 %copy-start.19 = (bf16[32,512]{1,0:T(8,128)(2,1)S(1)}, bf16[32,512]{1,0:T(8,128)(2,1)}, u32[]{:S(2)}) copy-start(bf16[32,512]{1,0:T(8,128)(2,1)} %param.16) | copy-start | bytes 98308
  26.8 51.0 %copy-start.20 = (bf16[32,512]{1,0:T(8,128)(2,1)S(1)}, bf16[32,512]{1,0:T(8,128)(2,1)}, u32[]{:S(2)}) copy-start(bf16[32,512]{1,0:T(8,128)(2,1)} %param.29) | copy-start | bytes 98308
  26.8 30.9 %all-to-all-start = ((bf16[8,96,512]{2,1,0:T(8,128)(2,1)}), bf16[8,96,512]{2,1,0:T(8,128)(2,1)}, u32[]{:S(2)}, u32[]{:S(2)}) async-start(bf16[8,96,512]{2,1,0:T(8,128)(2,1)} %bitcast.77), calls=%async_computation | async-start | bytes 1572864 | tf_op jit(solution)/shard_map/all_to_all | solution.py:140
  77.8 33.4 %copy-start.30 = (s32[384]{0:T(512)S(1)}, s32[384]{0:T(512)}, u32[]{:S(2)}) copy-start(s32[384]{0:T(512)} %copy-done.29) | copy-start | bytes 4612
  94.2 16.9 %all-to-all-start.3 = ((bf16[8,96,512]{2,1,0:T(8,128)(2,1)}), bf16[8,96,512]{2,1,0:T(8,128)(2,1)S(1)}, u32[]{:S(2)}, u32[]{:S(2)}) async-start(bf16[8,96,512]{2,1,0:T(8,128)(2,1)} %bitcast.5), calls=%async_computation.3 | async-start | bytes 1572864 | tf_op jit(solution)/shard_map/all_to_all | solution.py:157
  116.2 7.2 %copy-start.8 = (pred[2304,576]{1,0:T(32,128)(4,1)S(1)}, pred[2304,576]{1,0:T(32,128)(4,1)}, u32[]{:S(2)}) copy-start(pred[2304,576]{1,0:T(32,128)(4,1)} %iota_compare_fusion) | copy-start | bytes 3981316
  123.4 6.1 %copy-start.7 = (bf16[576,512]{1,0:T(8,128)(2,1)S(1)}, bf16[576,512]{1,0:T(8,128)(2,1)}, u32[]{:S(2)}) copy-start(bf16[576,512]{1,0:T(8,128)(2,1)} %copy-done.6) | copy-start | bytes 1769476
  135.1 4.6 %collective-permute-start.4 = (bf16[32,56,512]{2,0,1:T(8,128)(2,1)}, bf16[32,56,512]{2,0,1:T(8,128)(2,1)}, u32[]{:S(2)}, u32[]{:S(2)}) collective-permute-start(bf16[32,56,512]{2,0,1:T(8,128)(2,1)} %bitcast.67), channel_id=1, source_target_pairs={{0,4},{1,5},{2,6},{3,7},{4,0},{5,1},{6,2},{7,3},{8,12},{9,13},{10,... | collective-permute-start | bytes 5505032 | tf_op jit(solution)/shard_map/ppermute | solution.py:61
  142.3 13.4 %collective-permute-start.7 = (bf16[32,14,512]{2,0,1:T(8,128)(2,1)S(1)}, bf16[32,14,512]{2,0,1:T(8,128)(2,1)S(1)}, u32[]{:S(2)}, u32[]{:S(2)}) collective-permute-start(bf16[32,14,512]{2,0,1:T(8,128)(2,1)S(1)} %get-tuple-element.8), channel_id=1, source_target_pairs={{0,2},{1,3},{2,0},{3,1},{4,6},{5,7},{6,4},{7,5},{8,10},{9,11},{10,... | collective-permute-start | bytes 1376264 | tf_op jit(solution)/shard_map/ppermute | solution.py:66
  142.4 19.1 %collective-permute-start.6 = (bf16[32,14,512]{2,0,1:T(8,128)(2,1)S(1)}, bf16[32,14,512]{2,0,1:T(8,128)(2,1)S(1)}, u32[]{:S(2)}, u32[]{:S(2)}) collective-permute-start(bf16[32,14,512]{2,0,1:T(8,128)(2,1)S(1)} %get-tuple-element.9), channel_id=1, source_target_pairs={{0,3},{1,0},{2,1},{3,2},{4,7},{5,4},{6,5},{7,6},{8,11},{9,8},{10,9... | collective-permute-start | bytes 1376264 | tf_op jit(solution)/shard_map/ppermute | solution.py:66
  142.7 23.5 %collective-permute-start.5 = (bf16[32,14,512]{2,0,1:T(8,128)(2,1)S(1)}, bf16[32,14,512]{2,0,1:T(8,128)(2,1)S(1)}, u32[]{:S(2)}, u32[]{:S(2)}) collective-permute-start(bf16[32,14,512]{2,0,1:T(8,128)(2,1)S(1)} %get-tuple-element.7), channel_id=1, source_target_pairs={{0,1},{1,2},{2,3},{3,0},{4,5},{5,6},{6,7},{7,4},{8,9},{9,10},{10,1... | collective-permute-start | bytes 1376264 | tf_op jit(solution)/shard_map/ppermute | solution.py:66
  145.3 34.6 %collective-permute-start.3 = (bf16[96,512]{1,0:T(8,128)(2,1)}, bf16[96,512]{1,0:T(8,128)(2,1)}, u32[]{:S(2)}, u32[]{:S(2)}) collective-permute-start(bf16[96,512]{1,0:T(8,128)(2,1)} %get-tuple-element.11), channel_id=1, source_target_pairs={{1,0},{2,1},{3,2},{4,3},{5,4},{6,5},{7,6},{8,7},{9,8},{10,9},{11,1... | collective-permute-start | bytes 294920 | tf_op jit(solution)/shard_map/ppermute | solution.py:177
  147.6 32.3 %collective-permute-start.2 = (bf16[96,512]{1,0:T(8,128)(2,1)}, bf16[96,512]{1,0:T(8,128)(2,1)}, u32[]{:S(2)}, u32[]{:S(2)}) collective-permute-start(bf16[96,512]{1,0:T(8,128)(2,1)} %get-tuple-element.10), channel_id=1, source_target_pairs={{0,1},{1,2},{2,3},{3,4},{4,5},{5,6},{6,7},{7,8},{8,9},{9,10},{10,1... | collective-permute-start | bytes 294920 | tf_op jit(solution)/shard_map/ppermute | solution.py:176
  166.5 4.0 %copy-start.4 = (bf16[512,512]{1,0:T(8,128)(2,1)S(1)}, bf16[512,512]{1,0:T(8,128)(2,1)}, u32[]{:S(2)}) copy-start(bf16[512,512]{1,0:T(8,128)(2,1)} %param.24) | copy-start | bytes 1572868
  167.6 5.7 %collective-permute-start.10 = (bf16[8,14,512]{2,0,1:T(8,128)(2,1)S(1)}, bf16[8,14,512]{2,0,1:T(8,128)(2,1)S(1)}, u32[]{:S(2)}, u32[]{:S(2)}) collective-permute-start(bf16[8,14,512]{2,0,1:T(8,128)(2,1)S(1)} %bitcast.79), channel_id=1, source_target_pairs={{0,16},{1,17},{2,18},{3,19},{4,20},{5,21},{6,22},{7,23},{8,24},{9,... | collective-permute-start | bytes 344072 | tf_op jit(solution)/shard_map/ppermute | solution.py:70
  167.8 7.8 %collective-permute-start.9 = (bf16[8,14,512]{2,0,1:T(8,128)(2,1)S(1)}, bf16[8,14,512]{2,0,1:T(8,128)(2,1)S(1)}, u32[]{:S(2)}, u32[]{:S(2)}) collective-permute-start(bf16[8,14,512]{2,0,1:T(8,128)(2,1)S(1)} %bitcast.80), channel_id=1, source_target_pairs={{0,24},{1,25},{2,26},{3,27},{4,28},{5,29},{6,30},{7,31},{8,0},{9,1... | collective-permute-start | bytes 344072 | tf_op jit(solution)/shard_map/ppermute | solution.py:70
  170.5 5.3 %collective-permute-start.8 = (bf16[8,14,512]{2,0,1:T(8,128)(2,1)S(1)}, bf16[8,14,512]{2,0,1:T(8,128)(2,1)S(1)}, u32[]{:S(2)}, u32[]{:S(2)}) collective-permute-start(bf16[8,14,512]{2,0,1:T(8,128)(2,1)S(1)} %bitcast.81), channel_id=1, source_target_pairs={{0,8},{1,9},{2,10},{3,11},{4,12},{5,13},{6,14},{7,15},{8,16},{9,17... | collective-permute-start | bytes 344072 | tf_op jit(solution)/shard_map/ppermute | solution.py:70
  170.6 9.3 %copy-start.27 = (s32[192]{0:T(256)S(1)}, s32[192]{0:T(256)}, u32[]{:S(2)}) copy-start(s32[192]{0:T(256)} %param.17) | copy-start | bytes 2308
  176.5 11.3 %all-to-all-start.4 = ((bf16[8,14,512]{2,1,0:T(8,128)(2,1)}), bf16[8,14,512]{2,1,0:T(8,128)(2,1)S(1)}, u32[]{:S(2)}, u32[]{:S(2)}) async-start(bf16[8,14,512]{2,1,0:T(8,128)(2,1)} %copy.41), calls=%async_computation.4 | async-start | bytes 262144 | tf_op jit(solution)/shard_map/all_to_all | solution.py:72
  (17 other events, 32.0 us)

commit v2 on v1

v2 whole, which is shorter than its diff:
```python
import jax
import jax.numpy as jnp
from jax import lax
from jax.experimental import pallas as pl
from jax.experimental.pallas import tpu as pltpu
from jax.sharding import PartitionSpec as P

BF = jnp.bfloat16
F32 = jnp.float32
BOTH = ("row", "col")
CAP = 12
ZN, YN, CN, XN = 8, 4, 2, 4
PLANE = YN * CN
NODES, RIM, EXT, MIDS, WIDTH, EDGES = 384, 96, 576, 32, 512, 2304
SLOTS = ZN * CAP
CARRY = 112
STEP = 768
DST = 640
ENDS = DST + NODES
TALL = 14
HELD = 16


def place(z, y, c, x):
    return ((z * YN + y) * CN + c) * XN + x


def shift(dz=0, dy=0, dc=0, dx=0):
    return [
        (place(z, y, c, x), place((z + dz) % ZN, (y + dy) % YN, (c + dc) % CN, (x + dx) % XN))
        for z in range(ZN)
        for y in range(YN)
        for c in range(CN)
        for x in range(XN)
    ]


PLANES = [[z * PLANE + i for i in range(PLANE)] for z in range(ZN)]
PILLARS = [[z * PLANE + i for z in range(ZN)] for i in range(PLANE)]
SHEETS = [
    [place(z, y, c, x) for y in range(YN) for x in range(XN)] for z in range(ZN) for c in range(CN)
]


def dot(a, b):
    return jnp.dot(a, b, preferred_element_type=F32)


def dot_t(a, b):
    return lax.dot_general(a, b, (((0,), (0,)), ((), ())), preferred_element_type=F32)


def dot_nt(a, b):
    return lax.dot_general(a, b, (((1,), (1,)), ((), ())), preferred_element_type=F32)


def iota(shape, axis):
    return lax.broadcasted_iota(jnp.int32, shape, axis)


def ones(mask):
    return jnp.where(mask, 1.0, 0.0).astype(BF)


def across(row):
    return jnp.transpose(jnp.broadcast_to(row, (128, 128)))


def down(row, count, start=0):
    return ones(iota((count, row.shape[1]), 0) + start == row)


def silu_pair(u):
    s = 0.5 * jnp.tanh(0.5 * u) + 0.5
    return u * s, s * (1.0 + u * (1.0 - s))


def bf(*shape):
    return jax.ShapeDtypeStruct(shape, BF)


def f32(*shape):
    return jax.ShapeDtypeStruct(shape, F32)


def i32(*shape):
    return jax.ShapeDtypeStruct(shape, jnp.int32)


def run(body, outs, args, kinds, scratch=(), copies=0, mib=16, flops=0):
    spaces = {"s": pltpu.SMEM, "v": pltpu.VMEM, "h": pltpu.HBM}
    moved = sum(a.size * a.dtype.itemsize for a in list(args) + list(outs))
    took, gave = kinds.split(">")
    scratch = list(scratch)
    if copies:
        scratch.append(pltpu.SemaphoreType.DMA((copies,)))
    return pl.pallas_call(
        body,
        out_shape=list(outs),
        in_specs=[pl.BlockSpec(memory_space=spaces[k]) for k in took],
        out_specs=[pl.BlockSpec(memory_space=spaces[k]) for k in gave],
        scratch_shapes=scratch,
        compiler_params=pltpu.CompilerParams(vmem_limit_bytes=mib << 20),
        cost_estimate=pl.CostEstimate(flops=flops, bytes_accessed=moved, transcendentals=0),
    )(*args)


def fetch(sems, *pairs):
    copies = [pltpu.make_async_copy(a, b, sems.at[i]) for i, (a, b) in enumerate(pairs)]
    for copy in copies:
        copy.start()
    return copies


def piece(line, start, size):
    return line[pl.ds(start, size)].reshape(1, size)


def send_body(index_far, latent_far, low, high, index, latent, sems):
    for copy in fetch(sems, (index_far, index), (latent_far, latent)):
        copy.wait()
    row = jnp.concatenate([piece(index, 0, 128), piece(index, 128, 64)], axis=1)
    rows = dot_t(down(row, NODES), latent[...]).astype(BF)
    low[...] = rows[:RIM]
    high[...] = rows[RIM:]


def local_body(
    dest_far, latent_far, w_src_far, w_dst_far, near, mine, spot, dest, latent, w_src, w_dst, sems
):
    copies = fetch(
        sems, (dest_far, dest), (latent_far, latent), (w_src_far, w_src), (w_dst_far, w_dst)
    )
    copies[0].wait()
    for j in range(NODES // 128):
        row = dest[:, 128 * j : 128 * (j + 1)]
        rank = jnp.zeros((1, 128), F32)
        for b in range(j + 1):
            same = across(dest[:, 128 * b : 128 * (b + 1)]) == row
            if b == j:
                same = same & (iota((128, 128), 0) < iota((128, 128), 1))
            rank = rank + jnp.sum(jnp.where(same, 1.0, 0.0), axis=0, keepdims=True)
        spot[:, 128 * j : 128 * (j + 1)] = (
            (row & (PLANE - 1)) * SLOTS + (row >> 3) * CAP + rank.astype(jnp.int32)
        )
    for copy in copies[1:]:
        copy.wait()
    near[...] = dot(latent[...], w_src[...]).astype(BF)
    mine[...] = dot(latent[...], w_dst[...]).astype(BF)


def live_row(row, count, start):
    return jnp.where(iota(row.shape, 1) + start < count, row, -1)


def forward_body(
    count,
    src_far,
    dst_far,
    near_far,
    mine_far,
    w_src_far,
    lower_far,
    upper_far,
    w_msg_far,
    w_node_far,
    latent_far,
    spot_far,
    node_far,
    fine_out_far,
    sent_far,
    node_slope_far,
    slope_far,
    gathered_far,
    aggregate_far,
    src,
    dst,
    mine,
    w_src,
    lower,
    upper,
    w_msg,
    w_node,
    latent,
    spot,
    node,
    fine_out,
    sent,
    node_slope,
    edge_slope,
    gathered,
    aggregate,
    table,
    ends,
    sems,
    out_sems,
):
    near = table.at[:NODES, :]
    copies = fetch(
        sems,
        (src_far, src),
        (dst_far, dst),
        (w_src_far, w_src),
        (lower_far, lower),
        (upper_far, upper),
        (near_far, near),
        (mine_far, mine),
        (w_msg_far, w_msg),
        (w_node_far, w_node),
        (latent_far, latent),
        (spot_far, spot),
        (node_far, node),
    )
    stores = []

    def store(here, there):
        stores.append(pltpu.make_async_copy(here, there, out_sems.at[len(stores)]))
        stores[-1].start()

    table[EXT:DST, :] = jnp.zeros((DST - EXT, WIDTH), BF)
    for copy in copies[:7]:
        copy.wait()
    table[DST:, :] = mine[...]
    table[NODES : NODES + RIM, :] = dot(lower[...], w_src[...]).astype(BF)
    table[NODES + RIM : EXT, :] = dot(upper[...], w_src[...]).astype(BF)
    lane = iota((128, 128), 1)
    total = jnp.zeros((NODES, WIDTH), F32)
    for start in range(0, EDGES, STEP):
        for at in range(start, start + STEP, 128):
            source, target = across(piece(src, at, 128)), across(piece(dst, at, 128))
            for j in range(0, DST, 128):
                ends[at : at + 128, j : j + 128] = ones(source == lane + j)
            for j in range(0, NODES, 128):
                ends[at : at + 128, DST + j : DST + j + 128] = ones(target == lane + j)
        act, slope = silu_pair(dot(ends[start : start + STEP, :], table[...]))
        here = pl.ds(start, STEP)
        edge_slope[here, :] = slope.astype(BF)
        store(edge_slope.at[here, :], slope_far.at[here, :])
        row = live_row(piece(dst, start, STEP), count[0], start)
        total = total + dot(down(row, NODES), act.astype(BF))
    gathered[...] = total.astype(BF)
    store(gathered, gathered_far)
    for copy in copies[7:]:
        copy.wait()
    aggregate[...] = dot(gathered[...], w_msg[...]).astype(BF)
    store(aggregate, aggregate_far)
    update = dot(latent[...], w_node[:WIDTH, :]) + dot(aggregate[...], w_node[WIDTH:, :])
    lift, slope = silu_pair(update)
    node_slope[...] = slope
    store(node_slope, node_slope_far)
    fine_out[...] = (latent[...].astype(F32) + lift).astype(BF)
    store(fine_out, fine_out_far)
    names = jnp.broadcast_to((piece(node, 0, NODES) + 1).astype(F32), (16, NODES)).astype(BF)
    for i in range(PLANE):
        offset = spot[...] - i * SLOTS
        to_slot = ones((iota((128, NODES), 0) == offset) & (offset < SLOTS))
        sent[i] = dot(to_slot[:CARRY], fine_out[...]).astype(BF)
        sent[i, SLOTS:CARRY, :128] = dot_nt(names, to_slot).astype(BF)
        if i % 4 == 3:
            store(sent.at[pl.ds(i - 3, 4)], sent_far.at[pl.ds(i - 3, 4)])
    for copy in stores:
        copy.wait()


def sum_body(got, sums, owner):
    total = jnp.zeros((ZN * MIDS, WIDTH), F32)
    level = iota((1, 128), 1)
    base = jnp.zeros((1, 128), jnp.int32)
    for z in range(1, ZN):
        base = base + jnp.where(level >= z * CAP, MIDS, 0)
    for i in range(PLANE):
        name = got[i, SLOTS:CARRY, :128][:1].astype(F32).astype(jnp.int32)
        name = jnp.where((name > 0) & (level < SLOTS), name - 1 + base, -1)
        owner[i : i + 1, :] = name
        total = total + dot(down(name, ZN * MIDS)[:, :CARRY], got[i])
    for z in range(ZN):
        sums[z] = total[z * MIDS : (z + 1) * MIDS].astype(BF)


def mid_body(
    got,
    latent_far,
    cot_far,
    w_mid_far,
    mid_out,
    grad_mid,
    spread,
    up_agg,
    mid_back,
    latent,
    cot,
    w_mid,
    sems,
):
    copies = fetch(sems, (latent_far, latent), (cot_far, cot), (w_mid_far, w_mid))
    total = got[0].astype(F32)
    for z in range(1, ZN):
        total = total + got[z].astype(F32)
    agg = (0.25 * total).astype(BF)
    up_agg[...] = agg
    for copy in copies:
        copy.wait()
    update = dot(latent[...], w_mid[:WIDTH, :]) + dot(agg, w_mid[WIDTH:, :])
    lift, slope = silu_pair(update)
    mid_out[...] = (latent[...].astype(F32) + lift).astype(BF)
    back = (cot[...].astype(F32) * slope).astype(BF)
    mid_back[...] = back
    grad = dot_nt(back, w_mid[:WIDTH, :]).astype(BF).astype(F32)
    grad_mid[...] = (cot[...].astype(F32) + grad).astype(BF)
    grad = dot_nt(back, w_mid[WIDTH:, :]).astype(BF).astype(F32)
    grad = (0.25 * grad).astype(BF)
    for z in range(ZN):
        spread[z] = grad


def spread_body(owner, got, back):
    rows = jnp.concatenate([got[z] for z in range(ZN)], axis=0)
    for i in range(PLANE):
        back[i] = dot_t(down(owner[i : i + 1, :], ZN * MIDS), rows)[:SLOTS].astype(BF)


def part_cores(flat, first, pairs, stage):
    for pair in range(first, first + pairs):
        for c in range(CN):
            rows = [flat[pl.ds(224 * pair + 112 * h + 56 * c, 56), :] for h in range(2)]
            rows = jnp.concatenate(rows, axis=0).astype(BF)
            stage[c, 112 * pair : 112 * (pair + 1), :] = rows


def backward_body(
    count,
    core,
    spot_far,
    back_far,
    cot_far,
    node_slope_far,
    w_node_far,
    w_msg_far,
    dst_far,
    gathered_far,
    latent_far,
    aggregate_far,
    mid_far,
    mid_back_far,
    up_agg_far,
    src_far,
    slope_far,
    lower_far,
    upper_far,
    w_src_far,
    w_dst_far,
    direct_far,
    low_far,
    high_far,
    keep_far,
    send_far,
    spot,
    back,
    cot,
    node_slope,
    w_node,
    w_msg,
    dst,
    gathered,
    latent,
    aggregate,
    mid,
    mid_back,
    up_agg,
    src,
    edge_slope,
    lower,
    upper,
    w_src,
    w_dst,
    node_back,
    grad_agg,
    grad_gathered,
    grad_ends,
    rims,
    direct,
    targets,
    total,
    flat,
    stage,
    sems,
    out_sems,
):
    copies = fetch(
        sems,
        (spot_far, spot),
        (back_far, back),
        (cot_far, cot),
        (node_slope_far, node_slope),
        (w_node_far, w_node),
        (w_msg_far, w_msg),
        (dst_far, dst),
        (gathered_far, gathered),
        (latent_far, latent),
        (aggregate_far, aggregate),
        (mid_far, mid),
        (mid_back_far, mid_back),
        (up_agg_far, up_agg),
        (src_far, src),
        (slope_far, edge_slope),
        (lower_far, lower),
        (upper_far, upper),
        (w_src_far, w_src),
        (w_dst_far, w_dst),
    )
    stores = []

    def store(here, there):
        stores.append(pltpu.make_async_copy(here, there, out_sems.at[len(stores)]))
        stores[-1].start()

    mine = core[0]
    for copy in copies[:2]:
        copy.wait()
    up = jnp.zeros((NODES, WIDTH), F32)
    for i in range(PLANE):
        up = up + dot_t(down(spot[...], SLOTS, i * SLOTS), back[i])
    for copy in copies[2:4]:
        copy.wait()
    cot_sum = (cot[...].astype(F32) + up).astype(BF).astype(F32)
    node_back[...] = (cot_sum * node_slope[...]).astype(BF)
    copies[4].wait()
    grad_agg[...] = dot_nt(node_back[...], w_node[WIDTH:, :]).astype(BF)
    copies[5].wait()
    grad_gathered[...] = dot_nt(grad_agg[...], w_msg[...]).astype(BF)
    direct[...] = cot_sum + dot_nt(node_back[...], w_node[:WIDTH, :]).astype(BF).astype(F32)

    for copy in copies[6:13]:
        copy.wait()
    flat[1024:1536, :] = dot_t(gathered[...], grad_agg[...])
    flat[1536:2048, :] = dot_t(latent[...], node_back[...])
    flat[2048:2560, :] = dot_t(aggregate[...], node_back[...])
    flat[2560:3072, :] = dot_t(mid[...], mid_back[...])
    flat[3072:, :] = dot_t(up_agg[...], mid_back[...])
    part_cores(flat, 5, 11, stage)
    rest = pl.ds(560, 1232)
    store(stage.at[mine, rest], keep_far.at[rest])
    store(stage.at[1 - mine, rest], send_far.at[rest])

    for copy in copies[13:]:
        copy.wait()
    lane = iota((128, 128), 1)
    for start in range(0, EDGES, STEP):
        for at in range(start, start + STEP, 128):
            target = across(piece(dst, at, 128))
            for j in range(0, NODES, 128):
                targets[at : at + 128, j : j + 128] = ones(target == lane + j)
        grad = dot(targets[start : start + STEP, :], grad_gathered[...])
        grad = (grad * edge_slope[start : start + STEP, :].astype(F32)).astype(BF)
        from_src = dot(down(live_row(piece(src, start, STEP), count[0], start), EXT), grad)
        from_dst = dot(down(live_row(piece(dst, start, STEP), count[0], start), NODES), grad)
        if start == 0:
            total[:EXT, :] = from_src
            total[EXT:, :] = from_dst
        else:
            total[:EXT, :] += from_src
            total[EXT:, :] += from_dst
    grad_ends[...] = total[...].astype(BF)
    rims[...] = dot_nt(grad_ends[NODES:EXT, :], w_src[...]).astype(BF)
    store(rims.at[pl.ds(0, RIM)], low_far)
    store(rims.at[pl.ds(RIM, RIM)], high_far)

    grad = dot_t(lower[...], grad_ends[NODES : NODES + RIM, :])
    grad = grad + dot_t(upper[...], grad_ends[NODES + RIM : EXT, :])
    flat[:512, :] = grad + dot_t(latent[...], grad_ends[:NODES, :])
    flat[512:1024, :] = dot_t(latent[...], grad_ends[EXT:, :])
    part_cores(flat, 0, 5, stage)
    head = pl.ds(0, 560)
    store(stage.at[mine, head], keep_far.at[head])
    store(stage.at[1 - mine, head], send_far.at[head])
    grad = dot_nt(grad_ends[:NODES, :], w_src[...]) + dot_nt(grad_ends[EXT:, :], w_dst[...])
    direct[...] += grad
    store(direct, direct_far)
    for copy in stores:
        copy.wait()


def sheet_body(keep, got, out, rows, held):
    for pair in range(2 * ZN):
        at = 112 * pair
        rows[pair] = keep[at : at + 112, :].astype(F32) + got[at : at + 112, :].astype(F32)
        for h in range(2):
            for x in range(XN):
                to = (2 * (pair % 2) + h) * XN + x
                start = 14 * (pair // 2)
                held[to, start : start + 14, :] = rows[pair, 56 * h + 14 * x : 56 * h + 14 * x + 14, :]
    for to in range(YN * XN):
        out[to] = held[to].astype(BF)


def pillar_body(got, out, rows):
    total = got[0].astype(F32)
    for i in range(1, YN * XN):
        total = total + got[i].astype(F32)
    rows[:112, :] = total
    rows[112:, :] = jnp.zeros((16, WIDTH), F32)
    for z in range(ZN):
        out[z] = rows[14 * z : 14 * z + 16, :].astype(BF)


def last_body(got, out):
    total = got[0].astype(F32)
    for z in range(1, ZN):
        total = total + got[z].astype(F32)
    for r in range(TALL):
        for j in range(WIDTH // 128):
            out[4 * r + j : 4 * r + j + 1, :] = total[r : r + 1, 128 * j : 128 * (j + 1)]


def final_body(direct, from_low, from_high, index_far, grad_fine, index, sems):
    (copy,) = fetch(sems, (index_far, index))
    copy.wait()
    row = jnp.concatenate([piece(index, 0, 128), piece(index, 128, 64)], axis=1)
    total = direct[...] + dot(down(row[:, :RIM], NODES), from_low[...])
    total = total + dot(down(row[:, RIM:], NODES), from_high[...])
    grad_fine[...] = total.astype(BF)


def on_device(
    fine_latent,
    mid_latent,
    send_index,
    edge_src,
    edge_dst,
    edge_count,
    up_row,
    up_node,
    w_src,
    w_dst,
    w_msg,
    w_node,
    w_mid,
    cot_fine,
    cot_mid,
):
    core = (lax.axis_index("row") % CN).astype(jnp.int32).reshape(1)
    dest = up_row.reshape(1, NODES)
    ahead = [(i, (i + 1) % 256) for i in range(256)]
    behind = [(j, i) for i, j in ahead]
    line = lambda n: pltpu.VMEM((n,), jnp.int32)
    hold = lambda *shape: pltpu.VMEM(shape, BF)
    wide = lambda *shape: pltpu.VMEM(shape, F32)
    rim, fine, mid = bf(RIM, WIDTH), bf(NODES, WIDTH), bf(MIDS, WIDTH)

    low, high = run(
        send_body,
        (rim, rim),
        (send_index, fine_latent),
        "hh>vv",
        (line(2 * RIM), hold(NODES, WIDTH)),
        copies=2,
        mib=60,
    )
    lower = lax.ppermute(high, BOTH, ahead)
    upper = lax.ppermute(low, BOTH, behind)
    near, mine, spot = run(
        local_body,
        (fine, fine, i32(1, NODES)),
        (dest, fine_latent, w_src, w_dst),
        "hhhh>vvv",
        (pltpu.VMEM((1, NODES), jnp.int32), hold(NODES, WIDTH), hold(WIDTH, WIDTH))
        + (hold(WIDTH, WIDTH),),
        copies=4,
        mib=60,
        flops=4 * NODES * WIDTH * WIDTH,
    )
    dma = pltpu.SemaphoreType.DMA
    fine_out, sent, node_slope, edge_slope, gathered, aggregate = run(
        forward_body,
        (fine, bf(PLANE, CARRY, WIDTH), f32(NODES, WIDTH), bf(EDGES, WIDTH), fine, fine),
        (edge_count, edge_src, edge_dst, near, mine, w_src, lower, upper, w_msg, w_node)
        + (fine_latent, spot, up_node),
        "s" + 12 * "h" + ">hhhhhh",
        (line(EDGES), line(EDGES), hold(NODES, WIDTH), hold(WIDTH, WIDTH), hold(RIM, WIDTH))
        + (hold(RIM, WIDTH), hold(WIDTH, WIDTH), hold(2 * WIDTH, WIDTH), hold(NODES, WIDTH))
        + (pltpu.VMEM((1, NODES), jnp.int32), line(NODES), hold(NODES, WIDTH))
        + (hold(PLANE, CARRY, WIDTH), wide(NODES, WIDTH), hold(EDGES, WIDTH))
        + (hold(NODES, WIDTH), hold(NODES, WIDTH), hold(ENDS, WIDTH), hold(EDGES, ENDS))
        + (dma((12,)), dma((9,))),
        mib=60,
        flops=4 * 10**9,
    )
    got = lax.all_to_all(sent, "row", 0, 0, axis_index_groups=PLANES)
    sums, owner = run(sum_body, (bf(ZN, MIDS, WIDTH), i32(PLANE, 128)), (got,), "v>vv")
    got = lax.all_to_all(sums, "row", 0, 0, axis_index_groups=PILLARS)
    mid_out, grad_mid, spread, up_agg, mid_back = run(
        mid_body,
        (mid, mid, bf(ZN, MIDS, WIDTH), mid, mid),
        (got, mid_latent, cot_mid, w_mid),
        "vhhh>vvvvv",
        (hold(MIDS, WIDTH), hold(MIDS, WIDTH), hold(2 * WIDTH, WIDTH)),
        copies=3,
    )
    got = lax.all_to_all(spread, "row", 0, 0, axis_index_groups=PILLARS)
    (back,) = run(spread_body, (bf(PLANE, SLOTS, WIDTH),), (owner, got), "vv>v")
    back = lax.all_to_all(back, "row", 0, 0, axis_index_groups=PLANES)
    direct, low, high, keep, send = run(
        backward_body,
        (f32(NODES, WIDTH), rim, rim, bf(1792, WIDTH), bf(1792, WIDTH)),
        (edge_count, core, spot, back, cot_fine, node_slope, w_node, w_msg, edge_dst, gathered)
        + (fine_latent, aggregate, mid_latent, mid_back, up_agg, edge_src, edge_slope, lower)
        + (upper, w_src, w_dst),
        "ss" + 19 * "h" + ">hhhhh",
        (pltpu.VMEM((1, NODES), jnp.int32), hold(PLANE, SLOTS, WIDTH), hold(NODES, WIDTH))
        + (wide(NODES, WIDTH), hold(2 * WIDTH, WIDTH), hold(WIDTH, WIDTH), line(EDGES))
        + (hold(NODES, WIDTH), hold(NODES, WIDTH), hold(NODES, WIDTH), hold(MIDS, WIDTH))
        + (hold(MIDS, WIDTH), hold(MIDS, WIDTH), line(EDGES), hold(EDGES, WIDTH))
        + (hold(RIM, WIDTH), hold(RIM, WIDTH), hold(WIDTH, WIDTH), hold(WIDTH, WIDTH))
        + (hold(NODES, WIDTH), hold(NODES, WIDTH), hold(NODES, WIDTH))
        + (hold(EXT + NODES, WIDTH), hold(2 * RIM, WIDTH), wide(NODES, WIDTH))
        + (hold(EDGES, NODES), wide(EXT + NODES, WIDTH), wide(3584, WIDTH))
        + (hold(CN, 1792, WIDTH), dma((19,)), dma((7,))),
        mib=60,
        flops=5 * 10**9,
    )
    from_low = lax.ppermute(high, BOTH, ahead)
    from_high = lax.ppermute(low, BOTH, behind)
    got = lax.ppermute(send, BOTH, shift(dc=1))
    (grad_fine,) = run(
        final_body,
        (fine,),
        (direct, from_low, from_high, send_index),
        "vvvh>v",
        (line(2 * RIM),),
        copies=1,
        flops=2 * 10**8,
    )
    sheet = YN * XN
    (part,) = run(
        sheet_body,
        (bf(sheet, 112, WIDTH),),
        (keep, got),
        "vv>v",
        (wide(2 * ZN, 112, WIDTH), wide(sheet, 112, WIDTH)),
        mib=24,
    )
    part = lax.all_to_all(part, BOTH, 0, 0, axis_index_groups=SHEETS)
    (part,) = run(
        pillar_body, (bf(ZN, HELD, WIDTH),), (part,), "v>v", (wide(128, WIDTH),)
    )
    part = lax.all_to_all(part, "row", 0, 0, axis_index_groups=PILLARS)
    (weight_grads,) = run(last_body, (f32(56, 128),), (part,), "v>v")
    return fine_out, mid_out, grad_fine, grad_mid, weight_grads.reshape(-1)


def solution(mesh):
    rows, line = P(BOTH, None), P(BOTH)
    return jax.shard_map(
        on_device,
        mesh=mesh,
        in_specs=(rows, rows, line, line, line, line, rows, line)
        + (P(),) * 5
        + (rows, rows),
        out_specs=(rows, rows, rows, rows, line),
        check_vma=False,
    )
```

time: 190 us -> 162 us (0.85)
  the two profiles are of different devices: /device:TPU:1 before, /device:TPU:127 now
where the time goes in v2:
time: 162 us; the launch traced here: 161 us
  blocking collectives  67 us (41%)
  Pallas kernels  32.5 us (20%)
  waiting for transfers between devices  30 us (19%)
  starting transfers between devices  26.8 us (17%)
  local copies, waits for them, and re-layouts  3.74 us (2%)
    pallas_call x11, Pallas kernels, run(): pl.pallas_call(body, out_shape=list(outs), in_specs=[pl.BlockSpec(memory_...  32.5 us
    all_to_all x1, blocking collectives, on_device(): part = lax.all_to_all(part, BOTH, 0, 0, axis_index_groups=SHEETS)  27.1 us
    all_to_all x1, blocking collectives, on_device(): got = lax.all_to_all(sent, 'row', 0, 0, axis_index_groups=PLANES)  16.5 us
    all_to_all x1, blocking collectives, on_device(): got = lax.all_to_all(sums, 'row', 0, 0, axis_index_groups=PILLARS)  11.8 us
    all_to_all x1, blocking collectives, on_device(): got = lax.all_to_all(spread, 'row', 0, 0, axis_index_groups=PILLARS)  11.6 us
    all_to_all x1, waiting for transfers between devices, on_device(): back = lax.all_to_all(back, 'row', 0, 0, axis_index_groups=PLANES)  10.6 us
    all_to_all x1, starting transfers between devices, on_device(): back = lax.all_to_all(back, 'row', 0, 0, axis_index_groups=PLANES)  8.56 us
    ppermute x1, waiting for transfers between devices, on_device(): from_high = lax.ppermute(low, BOTH, behind)  7.83 us
  transfers between devices with their start and end apart: 7, of which 5 were waited for; matrix products, arithmetic and copies ran while one was open for 0% of the time, Pallas kernels for 2%

profile of v2, /device:TPU:127, one launch (start us, length us, event | category | flops | bytes accessed | tf_op | source)
XLA Modules:
  0.0 161.5 jit_solution(7805330429262557755)
XLA Ops:
  0.6 2.0 %shard_map.183 = (bf16[96,512]{1,0:T(8,128)(2,1)}, bf16[96,512]{1,0:T(8,128)(2,1)}) custom-call(s32[192]{0:T(256)} %index_far.3, bf16[384,512]{1,0:T(8,128)(2,1)} %latent_far.9), custom_call_target="tpu_custom_call" | custom-call | bytes 590592 | tf_op jit(solution)/shard_map/pallas_call | solution.py:97
  2.6 3.1 %collective-permute-start = (bf16[96,512]{1,0:T(8,128)(2,1)}, bf16[96,512]{1,0:T(8,128)(2,1)S(1)}, u32[]{:S(2)}, u32[]{:S(2)}) collective-permute-start(bf16[96,512]{1,0:T(8,128)(2,1)} %get-tuple-element.30), channel_id=1, source_target_pairs={{0,1},{1,2},{2,3},{3,4},{4,5},{5,6},{6,7},{7,8},{8,9},{9,10},{10,1... | collective-permute-start | bytes 294920 | tf_op jit(solution)/shard_map/ppermute | solution.py:559
  6.3 2.7 %shard_map.182 = (bf16[384,512]{1,0:T(8,128)(2,1)}, bf16[384,512]{1,0:T(8,128)(2,1)}, s32[1,384]{1,0:T(1,128)}) custom-call(s32[1,384]{1,0:T(1,128)} %bitcast.4, bf16[384,512]{1,0:T(8,128)(2,1)} %latent_far.9, bf16[512,512]{1,0:T(8,128)(2,1)} %w_src_far.5, bf16[512,512]{1,0:T(8,128)(2,1)} %w_dst_far.3), custom_call_target="tpu_custom_call" | custom-call | flops 402653184 | bytes 2231296 | tf_op jit(solution)/shard_map/pallas_call | solution.py:97
  9.0 6.3 %collective-permute-done.1.upper_far = bf16[96,512]{1,0:T(8,128)(2,1)S(1)} collective-permute-done((bf16[96,512]{1,0:T(8,128)(2,1)}, bf16[96,512]{1,0:T(8,128)(2,1)S(1)}, u32[]{:S(2)}, u32[]{:S(2)}) %collective-permute-start.1) | collective-permute-done | bytes 98336 | tf_op jit(solution)/shard_map/ppermute | solution.py:560
  15.4 0.6 copy-done.10
  16.0 9.6 %shard_map.184 = (bf16[384,512]{1,0:T(8,128)(2,1)}, bf16[8,112,512]{2,1,0:T(8,128)(2,1)}, f32[384,512]{1,0:T(8,128)}, bf16[2304,512]{1,0:T(8,128)(2,1)}, bf16[38...) custom-call(s32[1]{0:T(128)S(6)} %copy.20.count, s32[2304]{0:T(1024)} %src_far.3, s32[2304]{0:T(1024)} %dst_far.3, ...), custom_call_target="tpu_custom_call" | custom-call | flops 4000000000 | bytes 8737796 | tf_op jit(solution)/shard_map/pallas_call | solution.py:97
  25.5 0.0 copy-start.1
  25.6 0.0 copy-start.3
  25.6 0.0 copy-start.4
  25.6 16.5 %all_to_all.30.got = bf16[8,112,512]{2,1,0:T(8,128)(2,1)S(1)} all-to-all(bf16[8,112,512]{2,1,0:T(8,128)(2,1)} %get-tuple-element.34), channel_id=1, replica_groups={{0,4,8,12,16,20,24,28},{32,36,40,44,48,52,56,60},{64,68,72,76,80,84,88,..., dimensions={0} | all-to-all | bytes 1835008 | tf_op jit(solution)/shard_map/all_to_all | solution.py:588
  42.1 0.7 shard_map.185
  42.8 11.8 %all_to_all.31.got = bf16[8,32,512]{2,1,0:T(8,128)(2,1)S(1)} all-to-all(bf16[8,32,512]{2,1,0:T(8,128)(2,1)S(1)} %get-tuple-element.35), channel_id=1, replica_groups={{0,32,64,96,128,160,192,224},{4,36,68,100,132,164,196,228},{8,40,72,104..., dimensions={0} | all-to-all | bytes 524288 | tf_op jit(solution)/shard_map/all_to_all | solution.py:590
  54.6 1.4 shard_map.186
  56.0 0.6 copy-done.6
  56.6 11.6 %all_to_all.32.got = bf16[8,32,512]{2,1,0:T(8,128)(2,1)S(1)} all-to-all(bf16[8,32,512]{2,1,0:T(8,128)(2,1)S(1)} %get-tuple-element.38), channel_id=1, replica_groups={{0,32,64,96,128,160,192,224},{4,36,68,100,132,164,196,228},{8,40,72,104..., dimensions={0} | all-to-all | bytes 524288 | tf_op jit(solution)/shard_map/all_to_all | solution.py:599
  68.2 1.4 shard_map.187
  69.5 8.6 %all-to-all-start.3 = ((bf16[8,96,512]{2,1,0:T(8,128)(2,1)}), bf16[8,96,512]{2,1,0:T(8,128)(2,1)S(1)}, u32[]{:S(2)}, u32[]{:S(2)}) async-start(bf16[8,96,512]{2,1,0:T(8,128)(2,1)} %shard_map.187), calls=%async_computation.3 | async-start | bytes 1572864 | tf_op jit(solution)/shard_map/all_to_all | solution.py:601
  78.1 10.6 %all-to-all-done.3.back_far = bf16[8,96,512]{2,1,0:T(8,128)(2,1)S(1)} async-done(((bf16[8,96,512]{2,1,0:T(8,128)(2,1)}), bf16[8,96,512]{2,1,0:T(8,128)(2,1)S(1)}, u32[]{:S(2)}, u32[]{:S(2)}) %all-to-all-start.3) | async-done | bytes 786464 | tf_op jit(solution)/shard_map/all_to_all | solution.py:601
  88.6 1.0 copy-done.8
  89.6 11.2 %shard_map.188 = (f32[384,512]{1,0:T(8,128)}, bf16[96,512]{1,0:T(8,128)(2,1)}, bf16[96,512]{1,0:T(8,128)(2,1)}, bf16[1792,512]{1,0:T(8,128)(2,1)}, bf16[1792,512]{1,0:T(8,128)(2,1)}) custom-call(s32[1]{0:T(128)S(6)} %copy.20.count, s32[1]{0:T(128)} %bitcast.1.core, s32[1,384]{1,0:T(1,128)} %get-tuple-element.32.spot_far, bf16[8,96,512]{2,1,0:T(8,128)(2,1)} %copy-done.8, ...), custom_call_target="tpu_custom_call" | custom-call | flops 5000000000 | bytes 13094408 | tf_op jit(solution)/shard_map/pallas_call | solution.py:97
  100.9 1.0 collective-permute-start.4
  101.8 3.6 %collective-permute-done.4.got = bf16[1792,512]{1,0:T(8,128)(2,1)S(1)} collective-permute-done((bf16[1792,512]{1,0:T(8,128)(2,1)}, bf16[1792,512]{1,0:T(8,128)(2,1)S(1)}, u32[]{:S(2)}, u32[]{:S(2)}) %collective-permute-start.4) | collective-permute-done | bytes 1835040 | tf_op jit(solution)/shard_map/ppermute | solution.py:623
  105.4 1.5 copy-done
  106.9 0.9 shard_map.190
  107.9 27.1 %all_to_all.33.got = bf16[16,112,512]{2,1,0:T(8,128)(2,1)S(1)} all-to-all(bf16[16,112,512]{2,1,0:T(8,128)(2,1)S(1)} %shard_map.190), channel_id=1, replica_groups={{0,1,2,3,8,9,10,11,16,17,18,19,24,25,26,27},{4,5,6,7,12,13,14,15,20,21,..., dimensions={0} | all-to-all | bytes 3670016 | tf_op jit(solution)/shard_map/all_to_all | solution.py:642
  135.0 1.0 shard_map.191
  136.0 6.6 %all-to-all-start.5 = ((bf16[8,16,512]{2,1,0:T(8,128)(2,1)}), bf16[8,16,512]{2,1,0:T(8,128)(2,1)S(1)}, u32[]{:S(2)}, u32[]{:S(2)}) async-start(bf16[8,16,512]{2,1,0:T(8,128)(2,1)} %shard_map.191), calls=%async_computation.5 | async-start | bytes 262144 | tf_op jit(solution)/shard_map/all_to_all | solution.py:646
  142.6 7.7 %collective-permute-start.2 = (bf16[96,512]{1,0:T(8,128)(2,1)S(1)}, bf16[96,512]{1,0:T(8,128)(2,1)S(1)}, u32[]{:S(2)}, u32[]{:S(2)}) collective-permute-start(bf16[96,512]{1,0:T(8,128)(2,1)S(1)} %copy-done.12), channel_id=1, source_target_pairs={{0,1},{1,2},{2,3},{3,4},{4,5},{5,6},{6,7},{7,8},{8,9},{9,10},{10,1... | collective-permute-start | bytes 294920 | tf_op jit(solution)/shard_map/ppermute | solution.py:621
  150.2 1.6 %collective-permute-done.2.from_low = bf16[96,512]{1,0:T(8,128)(2,1)S(1)} collective-permute-done((bf16[96,512]{1,0:T(8,128)(2,1)S(1)}, bf16[96,512]{1,0:T(8,128)(2,1)S(1)}, u32[]{:S(2)}, u32[]{:S(2)}) %collective-permute-start.2) | collective-permute-done | bytes 98336 | tf_op jit(solution)/shard_map/ppermute | solution.py:621
  151.9 7.8 %collective-permute-done.3.from_high = bf16[96,512]{1,0:T(8,128)(2,1)S(1)} collective-permute-done((bf16[96,512]{1,0:T(8,128)(2,1)S(1)}, bf16[96,512]{1,0:T(8,128)(2,1)S(1)}, u32[]{:S(2)}, u32[]{:S(2)}) %collective-permute-start.3) | collective-permute-done | bytes 98336 | tf_op jit(solution)/shard_map/ppermute | solution.py:622
  159.7 1.1 shard_map.189
  160.8 0.6 shard_map.192
  (23 shorter events, 0.0 us)
Async XLA Ops:
  2.6 6.4 %collective-permute-start = (bf16[96,512]{1,0:T(8,128)(2,1)}, bf16[96,512]{1,0:T(8,128)(2,1)S(1)}, u32[]{:S(2)}, u32[]{:S(2)}) collective-permute-start(bf16[96,512]{1,0:T(8,128)(2,1)} %get-tuple-element.30), channel_id=1, source_target_pairs={{0,1},{1,2},{2,3},{3,4},{4,5},{5,6},{6,7},{7,8},{8,9},{9,10},{10,1... | collective-permute-start | bytes 294920 | tf_op jit(solution)/shard_map/ppermute | solution.py:559
  5.7 9.7 %collective-permute-start.1 = (bf16[96,512]{1,0:T(8,128)(2,1)}, bf16[96,512]{1,0:T(8,128)(2,1)S(1)}, u32[]{:S(2)}, u32[]{:S(2)}) collective-permute-start(bf16[96,512]{1,0:T(8,128)(2,1)} %get-tuple-element.31), channel_id=1, source_target_pairs={{1,0},{2,1},{3,2},{4,3},{5,4},{6,5},{7,6},{8,7},{9,8},{10,9},{11,1... | collective-permute-start | bytes 294920 | tf_op jit(solution)/shard_map/ppermute | solution.py:560
  9.0 6.3 %copy-start.9 = (bf16[96,512]{1,0:T(8,128)(2,1)}, bf16[96,512]{1,0:T(8,128)(2,1)S(1)}, u32[]{:S(2)}) copy-start(bf16[96,512]{1,0:T(8,128)(2,1)S(1)} %collective-permute-done.lower_far) | copy-start | bytes 294916
  15.3 0.6 copy-start.10
  25.5 29.1 %copy-start.1 = (bf16[1024,512]{1,0:T(8,128)(2,1)S(1)}, bf16[1024,512]{1,0:T(8,128)(2,1)}, u32[]{:S(2)}) copy-start(bf16[1024,512]{1,0:T(8,128)(2,1)} %w_mid_far.1) | copy-start | bytes 3145732
  25.6 29.0 %copy-start.3 = (bf16[32,512]{1,0:T(8,128)(2,1)S(1)}, bf16[32,512]{1,0:T(8,128)(2,1)}, u32[]{:S(2)}) copy-start(bf16[32,512]{1,0:T(8,128)(2,1)} %cot_far.2) | copy-start | bytes 98308
  25.6 29.0 %copy-start.4 = (bf16[32,512]{1,0:T(8,128)(2,1)S(1)}, bf16[32,512]{1,0:T(8,128)(2,1)}, u32[]{:S(2)}) copy-start(bf16[32,512]{1,0:T(8,128)(2,1)} %mid_far.1) | copy-start | bytes 98308
  56.0 0.6 copy-start.6
  56.6 11.6 %copy-start.7 = (bf16[32,512]{1,0:T(8,128)(2,1)}, bf16[32,512]{1,0:T(8,128)(2,1)S(1)}, u32[]{:S(2)}) copy-start(bf16[32,512]{1,0:T(8,128)(2,1)S(1)} %get-tuple-element.42.mid_back_far) | copy-start | bytes 98308
  69.5 19.1 %all-to-all-start.3 = ((bf16[8,96,512]{2,1,0:T(8,128)(2,1)}), bf16[8,96,512]{2,1,0:T(8,128)(2,1)S(1)}, u32[]{:S(2)}, u32[]{:S(2)}) async-start(bf16[8,96,512]{2,1,0:T(8,128)(2,1)} %shard_map.187), calls=%async_computation.3 | async-start | bytes 1572864 | tf_op jit(solution)/shard_map/all_to_all | solution.py:601
  88.6 1.0 copy-start.8
  100.9 4.6 %collective-permute-start.4 = (bf16[1792,512]{1,0:T(8,128)(2,1)}, bf16[1792,512]{1,0:T(8,128)(2,1)S(1)}, u32[]{:S(2)}, u32[]{:S(2)}) collective-permute-start(bf16[1792,512]{1,0:T(8,128)(2,1)} %get-tuple-element.50), channel_id=1, source_target_pairs={{0,4},{1,5},{2,6},{3,7},{4,0},{5,1},{6,2},{7,3},{8,12},{9,13},{10,... | collective-permute-start | bytes 5505032 | tf_op jit(solution)/shard_map/ppermute | solution.py:623
  105.4 1.5 copy-start
  135.0 7.6 %copy-start.12 = (bf16[96,512]{1,0:T(8,128)(2,1)S(1)}, bf16[96,512]{1,0:T(8,128)(2,1)}, u32[]{:S(2)}) copy-start(bf16[96,512]{1,0:T(8,128)(2,1)} %get-tuple-element.46) | copy-start | bytes 294916
  135.0 15.2 %copy-start.11 = (bf16[96,512]{1,0:T(8,128)(2,1)S(1)}, bf16[96,512]{1,0:T(8,128)(2,1)}, u32[]{:S(2)}) copy-start(bf16[96,512]{1,0:T(8,128)(2,1)} %get-tuple-element.47) | copy-start | bytes 294916
  135.0 24.7 %copy-start.2 = (f32[384,512]{1,0:T(8,128)S(1)}, f32[384,512]{1,0:T(8,128)}, u32[]{:S(2)}) copy-start(f32[384,512]{1,0:T(8,128)} %get-tuple-element.45.direct) | copy-start | bytes 2359300
  135.0 24.7 %copy-start.5 = (s32[192]{0:T(256)S(1)}, s32[192]{0:T(256)}, u32[]{:S(2)}) copy-start(s32[192]{0:T(256)} %index_far.3) | copy-start | bytes 2308
  136.0 24.8 %all-to-all-start.5 = ((bf16[8,16,512]{2,1,0:T(8,128)(2,1)}), bf16[8,16,512]{2,1,0:T(8,128)(2,1)S(1)}, u32[]{:S(2)}, u32[]{:S(2)}) async-start(bf16[8,16,512]{2,1,0:T(8,128)(2,1)} %shard_map.191), calls=%async_computation.5 | async-start | bytes 262144 | tf_op jit(solution)/shard_map/all_to_all | solution.py:646
  142.6 9.3 %collective-permute-start.2 = (bf16[96,512]{1,0:T(8,128)(2,1)S(1)}, bf16[96,512]{1,0:T(8,128)(2,1)S(1)}, u32[]{:S(2)}, u32[]{:S(2)}) collective-permute-start(bf16[96,512]{1,0:T(8,128)(2,1)S(1)} %copy-done.12), channel_id=1, source_target_pairs={{0,1},{1,2},{2,3},{3,4},{4,5},{5,6},{6,7},{7,8},{8,9},{9,10},{10,1... | collective-permute-start | bytes 294920 | tf_op jit(solution)/shard_map/ppermute | solution.py:621
  150.2 9.5 %collective-permute-start.3 = (bf16[96,512]{1,0:T(8,128)(2,1)S(1)}, bf16[96,512]{1,0:T(8,128)(2,1)S(1)}, u32[]{:S(2)}, u32[]{:S(2)}) collective-permute-start(bf16[96,512]{1,0:T(8,128)(2,1)S(1)} %copy-done.11), channel_id=1, source_target_pairs={{1,0},{2,1},{3,2},{4,3},{5,4},{6,5},{7,6},{8,7},{9,8},{10,9},{11,1... | collective-permute-start | bytes 294920 | tf_op jit(solution)/shard_map/ppermute | solution.py:622

commit v3 on v2

--- a/solution.py
+++ b/solution.py
@@ -40,6 +40,13 @@
 SHEETS = [
     [place(z, y, c, x) for y in range(YN) for x in range(XN)] for z in range(ZN) for c in range(CN)
 ]
+
+
+PEERS = ((0, 0), (2, 0), (2, 1), (1, 0), (1, 1), (3, 0), (3, 1), (0, 1))
+
+
+def peer(me, dy, dc):
+    return (((me >> 1) + dy) & (YN - 1)) * CN + ((me & 1) ^ dc)
 
 
 def dot(a, b):
@@ -155,6 +162,7 @@
 
 def forward_body(
     count,
+    place_at,
     src_far,
     dst_far,
     near_far,
@@ -168,33 +176,16 @@
     spot_far,
     node_far,
     fine_out_far,
-    sent_far,
     node_slope_far,
     slope_far,
     gathered_far,
     aggregate_far,
-    src,
-    dst,
-    mine,
-    w_src,
-    lower,
-    upper,
-    w_msg,
-    w_node,
-    latent,
-    spot,
-    node,
-    fine_out,
-    sent,
-    node_slope,
-    edge_slope,
-    gathered,
-    aggregate,
-    table,
-    ends,
-    sems,
-    out_sems,
+    *rest,
 ):
+    sent_far, rest = rest[:PLANE], rest[PLANE:]
+    src, dst, mine, w_src, lower, upper, w_msg, w_node, latent, spot, node = rest[:11]
+    fine_out, sent, node_slope, edge_slope, gathered, aggregate = rest[11:17]
+    table, ends, sems, out_sems = rest[17:]
     near = table.at[:NODES, :]
     copies = fetch(
         sems,
@@ -218,11 +209,8 @@
         stores[-1].start()
 
     table[EXT:DST, :] = jnp.zeros((DST - EXT, WIDTH), BF)
-    for copy in copies[:7]:
-        copy.wait()
-    table[DST:, :] = mine[...]
-    table[NODES : NODES + RIM, :] = dot(lower[...], w_src[...]).astype(BF)
-    table[NODES + RIM : EXT, :] = dot(upper[...], w_src[...]).astype(BF)
+    for copy in copies[:2]:
+        copy.wait()
     lane = iota((128, 128), 1)
     total = jnp.zeros((NODES, WIDTH), F32)
     for start in range(0, EDGES, STEP):
@@ -232,6 +220,12 @@
                 ends[at : at + 128, j : j + 128] = ones(source == lane + j)
             for j in range(0, NODES, 128):
                 ends[at : at + 128, DST + j : DST + j + 128] = ones(target == lane + j)
+        if start == 0:
+            for copy in copies[2:7]:
+                copy.wait()
+            table[DST:, :] = mine[...]
+            table[NODES : NODES + RIM, :] = dot(lower[...], w_src[...]).astype(BF)
+            table[NODES + RIM : EXT, :] = dot(upper[...], w_src[...]).astype(BF)
         act, slope = silu_pair(dot(ends[start : start + STEP, :], table[...]))
         here = pl.ds(start, STEP)
         edge_slope[here, :] = slope.astype(BF)
@@ -251,28 +245,28 @@
     fine_out[...] = (latent[...].astype(F32) + lift).astype(BF)
     store(fine_out, fine_out_far)
     names = jnp.broadcast_to((piece(node, 0, NODES) + 1).astype(F32), (16, NODES)).astype(BF)
-    for i in range(PLANE):
-        offset = spot[...] - i * SLOTS
+    for i, (dy, dc) in enumerate(PEERS):
+        offset = spot[...] - peer(place_at[0], dy, dc) * SLOTS
         to_slot = ones((iota((128, NODES), 0) == offset) & (offset < SLOTS))
         sent[i] = dot(to_slot[:CARRY], fine_out[...]).astype(BF)
         sent[i, SLOTS:CARRY, :128] = dot_nt(names, to_slot).astype(BF)
-        if i % 4 == 3:
-            store(sent.at[pl.ds(i - 3, 4)], sent_far.at[pl.ds(i - 3, 4)])
+        store(sent.at[i], sent_far[i])
     for copy in stores:
         copy.wait()
 
 
-def sum_body(got, sums, owner):
+def sum_body(*refs):
+    got, (sums, owner) = refs[:PLANE], refs[PLANE:]
     total = jnp.zeros((ZN * MIDS, WIDTH), F32)
     level = iota((1, 128), 1)
     base = jnp.zeros((1, 128), jnp.int32)
     for z in range(1, ZN):
         base = base + jnp.where(level >= z * CAP, MIDS, 0)
     for i in range(PLANE):
-        name = got[i, SLOTS:CARRY, :128][:1].astype(F32).astype(jnp.int32)
+        name = got[i][SLOTS:CARRY, :128][:1].astype(F32).astype(jnp.int32)
         name = jnp.where((name > 0) & (level < SLOTS), name - 1 + base, -1)
         owner[i : i + 1, :] = name
-        total = total + dot(down(name, ZN * MIDS)[:, :CARRY], got[i])
+        total = total + dot(down(name, ZN * MIDS)[:, :CARRY], got[i][...])
     for z in range(ZN):
         sums[z] = total[z * MIDS : (z + 1) * MIDS].astype(BF)
 
@@ -282,14 +276,18 @@
     latent_far,
     cot_far,
     w_mid_far,
-    mid_out,
-    grad_mid,
     spread,
-    up_agg,
-    mid_back,
+    mid_out_far,
+    grad_mid_far,
+    up_agg_far,
+    mid_back_far,
     latent,
     cot,
     w_mid,
+    mid_out,
+    grad_mid,
+    up_agg,
+    mid_back,
     sems,
 ):
     copies = fetch(sems, (latent_far, latent), (cot_far, cot), (w_mid_far, w_mid))
@@ -305,18 +303,29 @@
     mid_out[...] = (latent[...].astype(F32) + lift).astype(BF)
     back = (cot[...].astype(F32) * slope).astype(BF)
     mid_back[...] = back
+    stores = [
+        pltpu.make_async_copy(up_agg, up_agg_far, sems.at[3]),
+        pltpu.make_async_copy(mid_out, mid_out_far, sems.at[4]),
+        pltpu.make_async_copy(mid_back, mid_back_far, sems.at[5]),
+        pltpu.make_async_copy(grad_mid, grad_mid_far, sems.at[6]),
+    ]
+    for copy in stores[:3]:
+        copy.start()
     grad = dot_nt(back, w_mid[:WIDTH, :]).astype(BF).astype(F32)
     grad_mid[...] = (cot[...].astype(F32) + grad).astype(BF)
+    stores[3].start()
     grad = dot_nt(back, w_mid[WIDTH:, :]).astype(BF).astype(F32)
     grad = (0.25 * grad).astype(BF)
     for z in range(ZN):
         spread[z] = grad
-
-
-def spread_body(owner, got, back):
+    for copy in stores:
+        copy.wait()
+
+
+def spread_body(owner, got, *back):
     rows = jnp.concatenate([got[z] for z in range(ZN)], axis=0)
     for i in range(PLANE):
-        back[i] = dot_t(down(owner[i : i + 1, :], ZN * MIDS), rows)[:SLOTS].astype(BF)
+        back[i][...] = dot_t(down(owner[i : i + 1, :], ZN * MIDS), rows)[:SLOTS].astype(BF)
 
 
 def part_cores(flat, first, pairs, stage):
@@ -329,9 +338,11 @@
 
 def backward_body(
     count,
-    core,
+    place_at,
+    *refs,
+):
+    (
     spot_far,
-    back_far,
     cot_far,
     node_slope_far,
     w_node_far,
@@ -349,47 +360,17 @@
     upper_far,
     w_src_far,
     w_dst_far,
-    direct_far,
-    low_far,
-    high_far,
-    keep_far,
-    send_far,
-    spot,
-    back,
-    cot,
-    node_slope,
-    w_node,
-    w_msg,
-    dst,
-    gathered,
-    latent,
-    aggregate,
-    mid,
-    mid_back,
-    up_agg,
-    src,
-    edge_slope,
-    lower,
-    upper,
-    w_src,
-    w_dst,
-    node_back,
-    grad_agg,
-    grad_gathered,
-    grad_ends,
-    rims,
-    direct,
-    targets,
-    total,
-    flat,
-    stage,
-    sems,
-    out_sems,
-):
+    ) = refs[:18]
+    back_far, refs = refs[18 : 18 + PLANE], refs[18 + PLANE :]
+    direct_far, low_far, high_far, keep_far, send_far = refs[:5]
+    spot, back, cot, node_slope, w_node, w_msg, dst, gathered, latent, aggregate = refs[5:15]
+    mid, mid_back, up_agg, src, edge_slope, lower, upper, w_src, w_dst = refs[15:24]
+    node_back, grad_agg, grad_gathered, grad_ends, rims, direct = refs[24:30]
+    targets, total, flat, stage, sems, out_sems = refs[30:]
     copies = fetch(
         sems,
         (spot_far, spot),
-        (back_far, back),
+        *[(back_far[i], back.at[i]) for i in range(PLANE)],
         (cot_far, cot),
         (node_slope_far, node_slope),
         (w_node_far, w_node),
@@ -414,12 +395,14 @@
         stores.append(pltpu.make_async_copy(here, there, out_sems.at[len(stores)]))
         stores[-1].start()
 
-    mine = core[0]
-    for copy in copies[:2]:
-        copy.wait()
+    mine = place_at[0] & 1
+    for copy in copies[:9]:
+        copy.wait()
+    copies = copies[7:]
     up = jnp.zeros((NODES, WIDTH), F32)
-    for i in range(PLANE):
-        up = up + dot_t(down(spot[...], SLOTS, i * SLOTS), back[i])
+    for i, (dy, dc) in enumerate(PEERS):
+        offset = spot[...] - peer(place_at[0], dy, dc) * SLOTS
+        up = up + dot_t(down(offset, SLOTS), back[i])
     for copy in copies[2:4]:
         copy.wait()
     cot_sum = (cot[...].astype(F32) + up).astype(BF).astype(F32)
@@ -493,7 +476,25 @@
         out[to] = held[to].astype(BF)
 
 
-def pillar_body(got, out, rows):
+def pillar_body(
+    got,
+    low_far,
+    high_far,
+    direct_far,
+    index_far,
+    out,
+    grad_fine_far,
+    low,
+    high,
+    direct,
+    index,
+    grad_fine,
+    rows,
+    sems,
+):
+    copies = fetch(
+        sems, (index_far, index), (low_far, low), (high_far, high), (direct_far, direct)
+    )
     total = got[0].astype(F32)
     for i in range(1, YN * XN):
         total = total + got[i].astype(F32)
@@ -501,6 +502,15 @@
     rows[112:, :] = jnp.zeros((16, WIDTH), F32)
     for z in range(ZN):
         out[z] = rows[14 * z : 14 * z + 16, :].astype(BF)
+    for copy in copies:
+        copy.wait()
+    row = jnp.concatenate([piece(index, 0, 128), piece(index, 128, 64)], axis=1)
+    total = direct[...] + dot(down(row[:, :RIM], NODES), low[...])
+    total = total + dot(down(row[:, RIM:], NODES), high[...])
+    grad_fine[...] = total.astype(BF)
+    copy = pltpu.make_async_copy(grad_fine, grad_fine_far, sems.at[4])
+    copy.start()
+    copy.wait()
 
 
 def last_body(got, out):
@@ -509,16 +519,8 @@
         total = total + got[z].astype(F32)
     for r in range(TALL):
         for j in range(WIDTH // 128):
-            out[4 * r + j : 4 * r + j + 1, :] = total[r : r + 1, 128 * j : 128 * (j + 1)]
-
-
-def final_body(direct, from_low, from_high, index_far, grad_fine, index, sems):
-    (copy,) = fetch(sems, (index_far, index))
-    copy.wait()
-    row = jnp.concatenate([piece(index, 0, 128), piece(index, 128, 64)], axis=1)
-    total = direct[...] + dot(down(row[:, :RIM], NODES), from_low[...])
-    total = total + dot(down(row[:, RIM:], NODES), from_high[...])
-    grad_fine[...] = total.astype(BF)
+            here = pl.ds(WIDTH * r + 128 * j, 128)
+            out[here] = total[r : r + 1, 128 * j : 128 * (j + 1)].reshape(128)
 
 
 def on_device(
@@ -538,7 +540,7 @@
     cot_fine,
     cot_mid,
 ):
-    core = (lax.axis_index("row") % CN).astype(jnp.int32).reshape(1)
+    place_at = (lax.axis_index("row") % PLANE).astype(jnp.int32).reshape(1)
     dest = up_row.reshape(1, NODES)
     ahead = [(i, (i + 1) % 256) for i in range(256)]
     behind = [(j, i) for i, j in ahead]
@@ -570,42 +572,47 @@
         flops=4 * NODES * WIDTH * WIDTH,
     )
     dma = pltpu.SemaphoreType.DMA
-    fine_out, sent, node_slope, edge_slope, gathered, aggregate = run(
+    fine_out, node_slope, edge_slope, gathered, aggregate, *sent = run(
         forward_body,
-        (fine, bf(PLANE, CARRY, WIDTH), f32(NODES, WIDTH), bf(EDGES, WIDTH), fine, fine),
-        (edge_count, edge_src, edge_dst, near, mine, w_src, lower, upper, w_msg, w_node)
+        (fine, f32(NODES, WIDTH), bf(EDGES, WIDTH), fine, fine) + PLANE * (bf(CARRY, WIDTH),),
+        (edge_count, place_at, edge_src, edge_dst, near, mine, w_src, lower, upper, w_msg, w_node)
         + (fine_latent, spot, up_node),
-        "s" + 12 * "h" + ">hhhhhh",
+        "ss" + 12 * "h" + ">" + 13 * "h",
         (line(EDGES), line(EDGES), hold(NODES, WIDTH), hold(WIDTH, WIDTH), hold(RIM, WIDTH))
         + (hold(RIM, WIDTH), hold(WIDTH, WIDTH), hold(2 * WIDTH, WIDTH), hold(NODES, WIDTH))
         + (pltpu.VMEM((1, NODES), jnp.int32), line(NODES), hold(NODES, WIDTH))
         + (hold(PLANE, CARRY, WIDTH), wide(NODES, WIDTH), hold(EDGES, WIDTH))
         + (hold(NODES, WIDTH), hold(NODES, WIDTH), hold(ENDS, WIDTH), hold(EDGES, ENDS))
-        + (dma((12,)), dma((9,))),
+        + (dma((12,)), dma((15,))),
         mib=60,
         flops=4 * 10**9,
     )
-    got = lax.all_to_all(sent, "row", 0, 0, axis_index_groups=PLANES)
-    sums, owner = run(sum_body, (bf(ZN, MIDS, WIDTH), i32(PLANE, 128)), (got,), "v>vv")
+    got = [sent[0]]
+    for (dy, dc), block in zip(PEERS[1:], sent[1:]):
+        got.append(lax.ppermute(block, BOTH, shift(dy=dy, dc=dc)))
+    sums, owner = run(sum_body, (bf(ZN, MIDS, WIDTH), i32(PLANE, 128)), got, 8 * "v" + ">vv")
     got = lax.all_to_all(sums, "row", 0, 0, axis_index_groups=PILLARS)
-    mid_out, grad_mid, spread, up_agg, mid_back = run(
+    spread, mid_out, grad_mid, up_agg, mid_back = run(
         mid_body,
-        (mid, mid, bf(ZN, MIDS, WIDTH), mid, mid),
+        (bf(ZN, MIDS, WIDTH), mid, mid, mid, mid),
         (got, mid_latent, cot_mid, w_mid),
-        "vhhh>vvvvv",
-        (hold(MIDS, WIDTH), hold(MIDS, WIDTH), hold(2 * WIDTH, WIDTH)),
-        copies=3,
+        "vhhh>vhhhh",
+        (hold(MIDS, WIDTH), hold(MIDS, WIDTH), hold(2 * WIDTH, WIDTH))
+        + 4 * (hold(MIDS, WIDTH),),
+        copies=7,
     )
     got = lax.all_to_all(spread, "row", 0, 0, axis_index_groups=PILLARS)
-    (back,) = run(spread_body, (bf(PLANE, SLOTS, WIDTH),), (owner, got), "vv>v")
-    back = lax.all_to_all(back, "row", 0, 0, axis_index_groups=PLANES)
+    blocks = run(spread_body, PLANE * (bf(SLOTS, WIDTH),), (owner, got), "vv>" + 8 * "v")
+    back = [blocks[0]]
+    for (dy, dc), block in zip(PEERS[1:], blocks[1:]):
+        back.append(lax.ppermute(block, BOTH, shift(dy=-dy, dc=-dc)))
     direct, low, high, keep, send = run(
         backward_body,
         (f32(NODES, WIDTH), rim, rim, bf(1792, WIDTH), bf(1792, WIDTH)),
-        (edge_count, core, spot, back, cot_fine, node_slope, w_node, w_msg, edge_dst, gathered)
+        (edge_count, place_at, spot, cot_fine, node_slope, w_node, w_msg, edge_dst, gathered)
         + (fine_latent, aggregate, mid_latent, mid_back, up_agg, edge_src, edge_slope, lower)
-        + (upper, w_src, w_dst),
-        "ss" + 19 * "h" + ">hhhhh",
+        + (upper, w_src, w_dst, *back),
+        "ss" + 26 * "h" + ">hhhhh",
         (pltpu.VMEM((1, NODES), jnp.int32), hold(PLANE, SLOTS, WIDTH), hold(NODES, WIDTH))
         + (wide(NODES, WIDTH), hold(2 * WIDTH, WIDTH), hold(WIDTH, WIDTH), line(EDGES))
         + (hold(NODES, WIDTH), hold(NODES, WIDTH), hold(NODES, WIDTH), hold(MIDS, WIDTH))
@@ -614,22 +621,13 @@
         + (hold(NODES, WIDTH), hold(NODES, WIDTH), hold(NODES, WIDTH))
         + (hold(EXT + NODES, WIDTH), hold(2 * RIM, WIDTH), wide(NODES, WIDTH))
         + (hold(EDGES, NODES), wide(EXT + NODES, WIDTH), wide(3584, WIDTH))
-        + (hold(CN, 1792, WIDTH), dma((19,)), dma((7,))),
+        + (hold(CN, 1792, WIDTH), dma((26,)), dma((7,))),
         mib=60,
         flops=5 * 10**9,
     )
     from_low = lax.ppermute(high, BOTH, ahead)
     from_high = lax.ppermute(low, BOTH, behind)
     got = lax.ppermute(send, BOTH, shift(dc=1))
-    (grad_fine,) = run(
-        final_body,
-        (fine,),
-        (direct, from_low, from_high, send_index),
-        "vvvh>v",
-        (line(2 * RIM),),
-        copies=1,
-        flops=2 * 10**8,
-    )
     sheet = YN * XN
     (part,) = run(
         sheet_body,
@@ -639,13 +637,21 @@
         (wide(2 * ZN, 112, WIDTH), wide(sheet, 112, WIDTH)),
         mib=24,
     )
+    part, from_low, from_high = lax.optimization_barrier((part, from_low, from_high))
     part = lax.all_to_all(part, BOTH, 0, 0, axis_index_groups=SHEETS)
-    (part,) = run(
-        pillar_body, (bf(ZN, HELD, WIDTH),), (part,), "v>v", (wide(128, WIDTH),)
+    part, grad_fine = run(
+        pillar_body,
+        (bf(ZN, HELD, WIDTH), fine),
+        (part, from_low, from_high, direct, send_index),
+        "vhhhh>vh",
+        (hold(RIM, WIDTH), hold(RIM, WIDTH), wide(NODES, WIDTH), line(2 * RIM))
+        + (hold(NODES, WIDTH), wide(128, WIDTH)),
+        copies=5,
+        mib=24,
     )
     part = lax.all_to_all(part, "row", 0, 0, axis_index_groups=PILLARS)
-    (weight_grads,) = run(last_body, (f32(56, 128),), (part,), "v>v")
-    return fine_out, mid_out, grad_fine, grad_mid, weight_grads.reshape(-1)
+    (weight_grads,) = run(last_body, (f32(TALL * WIDTH),), (part,), "v>v")
+    return fine_out, mid_out, grad_fine, grad_mid, weight_grads
 
 
 def solution(mesh):

time: 162 us -> 157 us (0.969)
  the two profiles are of different devices: /device:TPU:127 before, /device:TPU:1 now
where the time goes in v3:
time: 157 us; the launch traced here: 156 us
  blocking collectives  72.1 us (46%)
  starting transfers between devices  35.3 us (22%)
  Pallas kernels  31.4 us (20%)
  waiting for transfers between devices  11 us (7%)
  local copies, waits for them, and re-layouts  4.95 us (3%)
    all_to_all x1, blocking collectives, on_device(): part = lax.all_to_all(part, BOTH, 0, 0, axis_index_groups=SHEETS)  32.7 us
    pallas_call x10, Pallas kernels, run(): pl.pallas_call(body, out_shape=list(outs), in_specs=[pl.BlockSpec(memory_...  31.4 us
    ppermute x7, starting transfers between devices, on_device(): got.append(lax.ppermute(block, BOTH, shift(dy=dy, dc=dc)))  15.5 us
    all_to_all x1, blocking collectives, on_device(): got = lax.all_to_all(sums, 'row', 0, 0, axis_index_groups=PILLARS)  15.3 us
    ppermute x7, starting transfers between devices, on_device(): back.append(lax.ppermute(block, BOTH, shift(dy=-dy, dc=-dc)))  12.3 us
    all_to_all x1, blocking collectives, on_device(): got = lax.all_to_all(spread, 'row', 0, 0, axis_index_groups=PILLARS)  12 us
    all_to_all x1, blocking collectives, on_device(): part = lax.all_to_all(part, 'row', 0, 0, axis_index_groups=PILLARS)  12 us
    ppermute x7, waiting for transfers between devices, on_device(): back.append(lax.ppermute(block, BOTH, shift(dy=-dy, dc=-dc)))  5.67 us
  transfers between devices with their start and end apart: 19, of which 8 were waited for; matrix products, arithmetic and copies ran while one was open for 0% of the time, Pallas kernels for 2%

profile of v3, /device:TPU:1, one launch (start us, length us, event | category | flops | bytes accessed | tf_op | source)
XLA Modules:
  0.0 156.3 jit_solution(10893312509538493949)
XLA Ops:
  0.6 2.0 %shard_map.183 = (bf16[96,512]{1,0:T(8,128)(2,1)}, bf16[96,512]{1,0:T(8,128)(2,1)}) custom-call(s32[192]{0:T(256)} %index_far.3, bf16[384,512]{1,0:T(8,128)(2,1)} %refs_7_.1), custom_call_target="tpu_custom_call" | custom-call | bytes 590592 | tf_op jit(solution)/shard_map/pallas_call | solution.py:104
  2.6 2.1 %collective-permute-start = (bf16[96,512]{1,0:T(8,128)(2,1)}, bf16[96,512]{1,0:T(8,128)(2,1)S(1)}, u32[]{:S(2)}, u32[]{:S(2)}) collective-permute-start(bf16[96,512]{1,0:T(8,128)(2,1)} %get-tuple-element.50), channel_id=1, source_target_pairs={{0,1},{1,2},{2,3},{3,4},{4,5},{5,6},{6,7},{7,8},{8,9},{9,10},{10,1... | collective-permute-start | bytes 294920 | tf_op jit(solution)/shard_map/ppermute | solution.py:561
  4.7 1.9 %collective-permute-start.1 = (bf16[96,512]{1,0:T(8,128)(2,1)}, bf16[96,512]{1,0:T(8,128)(2,1)S(1)}, u32[]{:S(2)}, u32[]{:S(2)}) collective-permute-start(bf16[96,512]{1,0:T(8,128)(2,1)} %get-tuple-element.51), channel_id=1, source_target_pairs={{1,0},{2,1},{3,2},{4,3},{5,4},{6,5},{7,6},{8,7},{9,8},{10,9},{11,1... | collective-permute-start | bytes 294920 | tf_op jit(solution)/shard_map/ppermute | solution.py:562
  7.3 2.7 %shard_map.182 = (bf16[384,512]{1,0:T(8,128)(2,1)}, bf16[384,512]{1,0:T(8,128)(2,1)}, s32[1,384]{1,0:T(1,128)}) custom-call(s32[1,384]{1,0:T(1,128)} %bitcast.2, bf16[384,512]{1,0:T(8,128)(2,1)} %refs_7_.1, bf16[512,512]{1,0:T(8,128)(2,1)} %refs_16_.1, bf16[512,512]{1,0:T(8,128)(2,1)} %refs_17_.1), custom_call_target="tpu_custom_call" | custom-call | flops 402653184 | bytes 2231296 | tf_op jit(solution)/shard_map/pallas_call | solution.py:104
  10.7 9.3 %shard_map.184 = (bf16[384,512]{1,0:T(8,128)(2,1)}, f32[384,512]{1,0:T(8,128)}, bf16[2304,512]{1,0:T(8,128)(2,1)}, bf16[384,512]{1,0:T(8,128)(2,1)}, bf16[384,51...) custom-call(s32[1]{0:T(128)S(6)} %copy.20.count, ...), custom_call_target="tpu_custom_call" | custom-call | flops 4000000000 | bytes 8737800 | tf_op jit(solution)/shard_map/pallas_call | solution.py:104
  20.0 3.0 %collective-permute-start.2 = (bf16[112,512]{1,0:T(8,128)(2,1)}, bf16[112,512]{1,0:T(8,128)(2,1)S(1)}, u32[]{:S(2)}, u32[]{:S(2)}) collective-permute-start(bf16[112,512]{1,0:T(8,128)(2,1)} %get-tuple-element.55), channel_id=1, source_target_pairs={{0,16},{1,17},{2,18},{3,19},{4,20},{5,21},{6,22},{7,23},{8,24},{9,... | collective-permute-start | bytes 344072 | tf_op jit(solution)/shard_map/ppermute | solution.py:592
  23.1 7.8 %collective-permute-start.3 = (bf16[112,512]{1,0:T(8,128)(2,1)}, bf16[112,512]{1,0:T(8,128)(2,1)S(1)}, u32[]{:S(2)}, u32[]{:S(2)}) collective-permute-start(bf16[112,512]{1,0:T(8,128)(2,1)} %get-tuple-element.56), channel_id=1, source_target_pairs={{0,20},{1,21},{2,22},{3,23},{4,16},{5,17},{6,18},{7,19},{8,28},{9,... | collective-permute-start | bytes 344072 | tf_op jit(solution)/shard_map/ppermute | solution.py:592
  30.9 2.7 %collective-permute-start.6 = (bf16[112,512]{1,0:T(8,128)(2,1)}, bf16[112,512]{1,0:T(8,128)(2,1)S(1)}, u32[]{:S(2)}, u32[]{:S(2)}) collective-permute-start(bf16[112,512]{1,0:T(8,128)(2,1)} %get-tuple-element.59), channel_id=1, source_target_pairs={{0,24},{1,25},{2,26},{3,27},{4,28},{5,29},{6,30},{7,31},{8,0},{9,1... | collective-permute-start | bytes 344072 | tf_op jit(solution)/shard_map/ppermute | solution.py:592
  33.5 2.0 %collective-permute-start.7 = (bf16[112,512]{1,0:T(8,128)(2,1)}, bf16[112,512]{1,0:T(8,128)(2,1)S(1)}, u32[]{:S(2)}, u32[]{:S(2)}) collective-permute-start(bf16[112,512]{1,0:T(8,128)(2,1)} %get-tuple-element.60), channel_id=1, source_target_pairs={{0,28},{1,29},{2,30},{3,31},{4,24},{5,25},{6,26},{7,27},{8,4},{9,5... | collective-permute-start | bytes 344072 | tf_op jit(solution)/shard_map/ppermute | solution.py:592
  35.6 1.6 %collective-permute-done.3.refs_2_ = bf16[112,512]{1,0:T(8,128)(2,1)S(1)} collective-permute-done((bf16[112,512]{1,0:T(8,128)(2,1)}, bf16[112,512]{1,0:T(8,128)(2,1)S(1)}, u32[]{:S(2)}, u32[]{:S(2)}) %collective-permute-start.3) | collective-permute-done | bytes 114720 | tf_op jit(solution)/shard_map/ppermute | solution.py:592
  37.2 1.3 collective-permute-done.4.refs_3_
  38.4 1.8 %collective-permute-done.5.refs_4_ = bf16[112,512]{1,0:T(8,128)(2,1)S(1)} collective-permute-done((bf16[112,512]{1,0:T(8,128)(2,1)}, bf16[112,512]{1,0:T(8,128)(2,1)S(1)}, u32[]{:S(2)}, u32[]{:S(2)}) %collective-permute-start.5) | collective-permute-done | bytes 114720 | tf_op jit(solution)/shard_map/ppermute | solution.py:592
  40.3 0.9 copy-done.3
  41.2 0.7 shard_map.185
  41.8 15.3 %all_to_all.20.got = bf16[8,32,512]{2,1,0:T(8,128)(2,1)S(1)} all-to-all(bf16[8,32,512]{2,1,0:T(8,128)(2,1)S(1)} %get-tuple-element.62), channel_id=1, replica_groups={{0,32,64,96,128,160,192,224},{4,36,68,100,132,164,196,228},{8,40,72,104..., dimensions={0} | all-to-all | bytes 524288 | tf_op jit(solution)/shard_map/all_to_all | solution.py:594
  57.2 1.6 shard_map.186
  59.4 12.0 %all_to_all.21.got = bf16[8,32,512]{2,1,0:T(8,128)(2,1)S(1)} all-to-all(bf16[8,32,512]{2,1,0:T(8,128)(2,1)S(1)} %get-tuple-element.71), channel_id=1, replica_groups={{0,32,64,96,128,160,192,224},{4,36,68,100,132,164,196,228},{8,40,72,104..., dimensions={0} | all-to-all | bytes 524288 | tf_op jit(solution)/shard_map/all_to_all | solution.py:604
  72.5 5.9 %collective-permute-start.9 = (bf16[96,512]{1,0:T(8,128)(2,1)S(1)}, bf16[96,512]{1,0:T(8,128)(2,1)S(1)}, u32[]{:S(2)}, u32[]{:S(2)}) collective-permute-start(bf16[96,512]{1,0:T(8,128)(2,1)S(1)} %get-tuple-element.73), channel_id=1, source_target_pairs={{0,16},{1,17},{2,18},{3,19},{4,20},{5,21},{6,22},{7,23},{8,24},{9,... | collective-permute-start | bytes 294920 | tf_op jit(solution)/shard_map/ppermute | solution.py:608
  78.4 0.7 collective-permute-start.10
  79.1 3.3 %collective-permute-start.11 = (bf16[96,512]{1,0:T(8,128)(2,1)S(1)}, bf16[96,512]{1,0:T(8,128)(2,1)S(1)}, u32[]{:S(2)}, u32[]{:S(2)}) collective-permute-start(bf16[96,512]{1,0:T(8,128)(2,1)S(1)} %get-tuple-element.75), channel_id=1, source_target_pairs={{0,24},{1,25},{2,26},{3,27},{4,28},{5,29},{6,30},{7,31},{8,0},{9,1... | collective-permute-start | bytes 294920 | tf_op jit(solution)/shard_map/ppermute | solution.py:608
  82.5 1.8 %collective-permute-start.14 = (bf16[96,512]{1,0:T(8,128)(2,1)S(1)}, bf16[96,512]{1,0:T(8,128)(2,1)S(1)}, u32[]{:S(2)}, u32[]{:S(2)}) collective-permute-start(bf16[96,512]{1,0:T(8,128)(2,1)S(1)} %get-tuple-element.78), channel_id=1, source_target_pairs={{0,12},{1,13},{2,14},{3,15},{4,8},{5,9},{6,10},{7,11},{8,20},{9,21... | collective-permute-start | bytes 294920 | tf_op jit(solution)/shard_map/ppermute | solution.py:608
  84.3 0.9 collective-permute-done.10.refs_20_
  85.9 2.6 %collective-permute-done.12.refs_22_ = bf16[96,512]{1,0:T(8,128)(2,1)S(1)} collective-permute-done((bf16[96,512]{1,0:T(8,128)(2,1)S(1)}, bf16[96,512]{1,0:T(8,128)(2,1)S(1)}, u32[]{:S(2)}, u32[]{:S(2)}) %collective-permute-start.12) | collective-permute-done | bytes 98336 | tf_op jit(solution)/shard_map/ppermute | solution.py:608
  88.4 2.1 %collective-permute-done.14.refs_24_ = bf16[96,512]{1,0:T(8,128)(2,1)S(1)} collective-permute-done((bf16[96,512]{1,0:T(8,128)(2,1)S(1)}, bf16[96,512]{1,0:T(8,128)(2,1)S(1)}, u32[]{:S(2)}, u32[]{:S(2)}) %collective-permute-start.14) | collective-permute-done | bytes 98336 | tf_op jit(solution)/shard_map/ppermute | solution.py:608
  91.2 11.3 %shard_map.188 = (f32[384,512]{1,0:T(8,128)}, bf16[96,512]{1,0:T(8,128)(2,1)}, bf16[96,512]{1,0:T(8,128)(2,1)}, bf16[1792,512]{1,0:T(8,128)(2,1)}, bf16[1792,512]{1,0:T(8,128)(2,1)}) custom-call(s32[1]{0:T(128)S(6)} %copy.20.count, s32[1]{0:T(128)} %bitcast.place_at, s32[1,384]{1,0:T(1,128)} %get-tuple-element.52.spot_far.refs_0_, bf16[384,512]{1,0:T(8,128)(2,1)} %refs_1_.1, ...), custom_call_target="tpu_custom_call" | custom-call | flops 5000000000 | bytes 13094408 | tf_op jit(solution)/shard_map/pallas_call | solution.py:104
  103.0 3.0 %collective-permute-start.18 = (bf16[96,512]{1,0:T(8,128)(2,1)}, bf16[96,512]{1,0:T(8,128)(2,1)S(1)}, u32[]{:S(2)}, u32[]{:S(2)}) collective-permute-start(bf16[96,512]{1,0:T(8,128)(2,1)} %get-tuple-element.83), channel_id=1, source_target_pairs={{1,0},{2,1},{3,2},{4,3},{5,4},{6,5},{7,6},{8,7},{9,8},{10,9},{11,1... | collective-permute-start | bytes 294920 | tf_op jit(solution)/shard_map/ppermute | solution.py:629
  106.0 0.7 collective-permute-done.16.got
  106.6 1.5 copy-done
  108.1 0.9 shard_map.189
  109.1 32.7 %all_to_all.22.got = bf16[16,112,512]{2,1,0:T(8,128)(2,1)S(1)} all-to-all(bf16[16,112,512]{2,1,0:T(8,128)(2,1)S(1)} %shard_map.189), channel_id=1, replica_groups={{0,1,2,3,8,9,10,11,16,17,18,19,24,25,26,27},{4,5,6,7,12,13,14,15,20,21,..., dimensions={0} | all-to-all | bytes 3670016 | tf_op jit(solution)/shard_map/all_to_all | solution.py:641
  141.9 1.8 %shard_map.190 = (bf16[8,16,512]{2,1,0:T(8,128)(2,1)S(1)}, bf16[384,512]{1,0:T(8,128)(2,1)}) custom-call(bf16[16,112,512]{2,1,0:T(8,128)(2,1)S(1)} %all_to_all.22.got, bf16[96,512]{1,0:T(8,128)(2,1)S(1)} %collective-permute-done.17.low_far, bf16[96,512]{1,0:T(8,128)(2,1)S(1)} %collective-permute-done.18.high_far, f32[384,512]{1,0:T(8,128)S(1)} %copy-done.2, ...), custom_call_target="tpu_custom_call" | custom-call | bytes 3343104 | tf_op jit(solution)/shard_map/pallas_call | solution.py:104
  143.7 12.0 %all_to_all.23.got = bf16[8,16,512]{2,1,0:T(8,128)(2,1)S(1)} all-to-all(bf16[8,16,512]{2,1,0:T(8,128)(2,1)S(1)} %get-tuple-element.90), channel_id=1, replica_groups={{0,32,64,96,128,160,192,224},{4,36,68,100,132,164,196,228},{8,40,72,104..., dimensions={0} | all-to-all | bytes 262144 | tf_op jit(solution)/shard_map/all_to_all | solution.py:652
  (58 shorter events, 4.9 us)
Async XLA Ops:
  2.6 7.4 %collective-permute-start = (bf16[96,512]{1,0:T(8,128)(2,1)}, bf16[96,512]{1,0:T(8,128)(2,1)S(1)}, u32[]{:S(2)}, u32[]{:S(2)}) collective-permute-start(bf16[96,512]{1,0:T(8,128)(2,1)} %get-tuple-element.50), channel_id=1, source_target_pairs={{0,1},{1,2},{2,3},{3,4},{4,5},{5,6},{6,7},{7,8},{8,9},{9,10},{10,1... | collective-permute-start | bytes 294920 | tf_op jit(solution)/shard_map/ppermute | solution.py:561
  4.7 5.3 %collective-permute-start.1 = (bf16[96,512]{1,0:T(8,128)(2,1)}, bf16[96,512]{1,0:T(8,128)(2,1)S(1)}, u32[]{:S(2)}, u32[]{:S(2)}) collective-permute-start(bf16[96,512]{1,0:T(8,128)(2,1)} %get-tuple-element.51), channel_id=1, source_target_pairs={{1,0},{2,1},{3,2},{4,3},{5,4},{6,5},{7,6},{8,7},{9,8},{10,9},{11,1... | collective-permute-start | bytes 294920 | tf_op jit(solution)/shard_map/ppermute | solution.py:562
  10.7 46.5 %copy-start.4 = (bf16[32,512]{1,0:T(8,128)(2,1)S(1)}, bf16[32,512]{1,0:T(8,128)(2,1)}, u32[]{:S(2)}) copy-start(bf16[32,512]{1,0:T(8,128)(2,1)} %cot_far.1) | copy-start | bytes 98308
  10.7 46.5 %copy-start.5 = (bf16[32,512]{1,0:T(8,128)(2,1)S(1)}, bf16[32,512]{1,0:T(8,128)(2,1)}, u32[]{:S(2)}) copy-start(bf16[32,512]{1,0:T(8,128)(2,1)} %refs_9_.1) | copy-start | bytes 98308
  20.0 37.2 %copy-start.1 = (bf16[1024,512]{1,0:T(8,128)(2,1)S(1)}, bf16[1024,512]{1,0:T(8,128)(2,1)}, u32[]{:S(2)}) copy-start(bf16[1024,512]{1,0:T(8,128)(2,1)} %w_mid_far.1) | copy-start | bytes 3145732
  20.0 13.5 %collective-permute-start.2 = (bf16[112,512]{1,0:T(8,128)(2,1)}, bf16[112,512]{1,0:T(8,128)(2,1)S(1)}, u32[]{:S(2)}, u32[]{:S(2)}) collective-permute-start(bf16[112,512]{1,0:T(8,128)(2,1)} %get-tuple-element.55), channel_id=1, source_target_pairs={{0,16},{1,17},{2,18},{3,19},{4,20},{5,21},{6,22},{7,23},{8,24},{9,... | collective-permute-start | bytes 344072 | tf_op jit(solution)/shard_map/ppermute | solution.py:592
  23.1 14.1 %collective-permute-start.3 = (bf16[112,512]{1,0:T(8,128)(2,1)}, bf16[112,512]{1,0:T(8,128)(2,1)S(1)}, u32[]{:S(2)}, u32[]{:S(2)}) collective-permute-start(bf16[112,512]{1,0:T(8,128)(2,1)} %get-tuple-element.56), channel_id=1, source_target_pairs={{0,20},{1,21},{2,22},{3,23},{4,16},{5,17},{6,18},{7,19},{8,28},{9,... | collective-permute-start | bytes 344072 | tf_op jit(solution)/shard_map/ppermute | solution.py:592
  30.8 7.6 %collective-permute-start.4 = (bf16[112,512]{1,0:T(8,128)(2,1)}, bf16[112,512]{1,0:T(8,128)(2,1)S(1)}, u32[]{:S(2)}, u32[]{:S(2)}) collective-permute-start(bf16[112,512]{1,0:T(8,128)(2,1)} %get-tuple-element.57), channel_id=1, source_target_pairs={{0,8},{1,9},{2,10},{3,11},{4,12},{5,13},{6,14},{7,15},{8,16},{9,17... | collective-permute-start | bytes 344072 | tf_op jit(solution)/shard_map/ppermute | solution.py:592
  30.8 9.4 %collective-permute-start.5 = (bf16[112,512]{1,0:T(8,128)(2,1)}, bf16[112,512]{1,0:T(8,128)(2,1)S(1)}, u32[]{:S(2)}, u32[]{:S(2)}) collective-permute-start(bf16[112,512]{1,0:T(8,128)(2,1)} %get-tuple-element.58), channel_id=1, source_target_pairs={{0,12},{1,13},{2,14},{3,15},{4,8},{5,9},{6,10},{7,11},{8,20},{9,21... | collective-permute-start | bytes 344072 | tf_op jit(solution)/shard_map/ppermute | solution.py:592
  30.9 9.4 %collective-permute-start.6 = (bf16[112,512]{1,0:T(8,128)(2,1)}, bf16[112,512]{1,0:T(8,128)(2,1)S(1)}, u32[]{:S(2)}, u32[]{:S(2)}) collective-permute-start(bf16[112,512]{1,0:T(8,128)(2,1)} %get-tuple-element.59), channel_id=1, source_target_pairs={{0,24},{1,25},{2,26},{3,27},{4,28},{5,29},{6,30},{7,31},{8,0},{9,1... | collective-permute-start | bytes 344072 | tf_op jit(solution)/shard_map/ppermute | solution.py:592
  33.5 6.7 %collective-permute-start.7 = (bf16[112,512]{1,0:T(8,128)(2,1)}, bf16[112,512]{1,0:T(8,128)(2,1)S(1)}, u32[]{:S(2)}, u32[]{:S(2)}) collective-permute-start(bf16[112,512]{1,0:T(8,128)(2,1)} %get-tuple-element.60), channel_id=1, source_target_pairs={{0,28},{1,29},{2,30},{3,31},{4,24},{5,25},{6,26},{7,27},{8,4},{9,5... | collective-permute-start | bytes 344072 | tf_op jit(solution)/shard_map/ppermute | solution.py:592
  37.2 3.1 %collective-permute-start.8 = (bf16[112,512]{1,0:T(8,128)(2,1)}, bf16[112,512]{1,0:T(8,128)(2,1)S(1)}, u32[]{:S(2)}, u32[]{:S(2)}) collective-permute-start(bf16[112,512]{1,0:T(8,128)(2,1)} %get-tuple-element.61), channel_id=1, source_target_pairs={{0,4},{1,5},{2,6},{3,7},{4,0},{5,1},{6,2},{7,3},{8,12},{9,13},{10,... | collective-permute-start | bytes 344072 | tf_op jit(solution)/shard_map/ppermute | solution.py:592
  40.3 0.9 copy-start.3
  59.4 12.0 %copy-start.9 = (bf16[32,512]{1,0:T(8,128)(2,1)}, bf16[32,512]{1,0:T(8,128)(2,1)S(1)}, u32[]{:S(2)}) copy-start(bf16[32,512]{1,0:T(8,128)(2,1)S(1)} %get-tuple-element.67.refs_10_) | copy-start | bytes 98308
  72.5 9.9 %collective-permute-start.9 = (bf16[96,512]{1,0:T(8,128)(2,1)S(1)}, bf16[96,512]{1,0:T(8,128)(2,1)S(1)}, u32[]{:S(2)}, u32[]{:S(2)}) collective-permute-start(bf16[96,512]{1,0:T(8,128)(2,1)S(1)} %get-tuple-element.73), channel_id=1, source_target_pairs={{0,16},{1,17},{2,18},{3,19},{4,20},{5,21},{6,22},{7,23},{8,24},{9,... | collective-permute-start | bytes 294920 | tf_op jit(solution)/shard_map/ppermute | solution.py:608
  78.4 6.7 %collective-permute-start.10 = (bf16[96,512]{1,0:T(8,128)(2,1)S(1)}, bf16[96,512]{1,0:T(8,128)(2,1)S(1)}, u32[]{:S(2)}, u32[]{:S(2)}) collective-permute-start(bf16[96,512]{1,0:T(8,128)(2,1)S(1)} %get-tuple-element.74), channel_id=1, source_target_pairs={{0,20},{1,21},{2,22},{3,23},{4,16},{5,17},{6,18},{7,19},{8,28},{9,... | collective-permute-start | bytes 294920 | tf_op jit(solution)/shard_map/ppermute | solution.py:608
  79.1 6.7 %collective-permute-start.11 = (bf16[96,512]{1,0:T(8,128)(2,1)S(1)}, bf16[96,512]{1,0:T(8,128)(2,1)S(1)}, u32[]{:S(2)}, u32[]{:S(2)}) collective-permute-start(bf16[96,512]{1,0:T(8,128)(2,1)S(1)} %get-tuple-element.75), channel_id=1, source_target_pairs={{0,24},{1,25},{2,26},{3,27},{4,28},{5,29},{6,30},{7,31},{8,0},{9,1... | collective-permute-start | bytes 294920 | tf_op jit(solution)/shard_map/ppermute | solution.py:608
  82.4 6.0 %collective-permute-start.12 = (bf16[96,512]{1,0:T(8,128)(2,1)S(1)}, bf16[96,512]{1,0:T(8,128)(2,1)S(1)}, u32[]{:S(2)}, u32[]{:S(2)}) collective-permute-start(bf16[96,512]{1,0:T(8,128)(2,1)S(1)} %get-tuple-element.76), channel_id=1, source_target_pairs={{0,28},{1,29},{2,30},{3,31},{4,24},{5,25},{6,26},{7,27},{8,4},{9,5... | collective-permute-start | bytes 294920 | tf_op jit(solution)/shard_map/ppermute | solution.py:608
  82.4 6.0 %collective-permute-start.13 = (bf16[96,512]{1,0:T(8,128)(2,1)S(1)}, bf16[96,512]{1,0:T(8,128)(2,1)S(1)}, u32[]{:S(2)}, u32[]{:S(2)}) collective-permute-start(bf16[96,512]{1,0:T(8,128)(2,1)S(1)} %get-tuple-element.77), channel_id=1, source_target_pairs={{0,8},{1,9},{2,10},{3,11},{4,12},{5,13},{6,14},{7,15},{8,16},{9,17... | collective-permute-start | bytes 294920 | tf_op jit(solution)/shard_map/ppermute | solution.py:608
  82.4 8.1 %copy-start.12 = (bf16[96,512]{1,0:T(8,128)(2,1)}, bf16[96,512]{1,0:T(8,128)(2,1)S(1)}, u32[]{:S(2)}) copy-start(bf16[96,512]{1,0:T(8,128)(2,1)S(1)} %collective-permute-done.9.refs_19_) | copy-start | bytes 294916
  82.5 8.0 %collective-permute-start.14 = (bf16[96,512]{1,0:T(8,128)(2,1)S(1)}, bf16[96,512]{1,0:T(8,128)(2,1)S(1)}, u32[]{:S(2)}, u32[]{:S(2)}) collective-permute-start(bf16[96,512]{1,0:T(8,128)(2,1)S(1)} %get-tuple-element.78), channel_id=1, source_target_pairs={{0,12},{1,13},{2,14},{3,15},{4,8},{5,9},{6,10},{7,11},{8,20},{9,21... | collective-permute-start | bytes 294920 | tf_op jit(solution)/shard_map/ppermute | solution.py:608
  85.1 5.4 %copy-start.13 = (bf16[96,512]{1,0:T(8,128)(2,1)}, bf16[96,512]{1,0:T(8,128)(2,1)S(1)}, u32[]{:S(2)}) copy-start(bf16[96,512]{1,0:T(8,128)(2,1)S(1)} %collective-permute-done.10.refs_20_) | copy-start | bytes 294916
  85.1 5.4 %collective-permute-start.15 = (bf16[96,512]{1,0:T(8,128)(2,1)S(1)}, bf16[96,512]{1,0:T(8,128)(2,1)S(1)}, u32[]{:S(2)}, u32[]{:S(2)}) collective-permute-start(bf16[96,512]{1,0:T(8,128)(2,1)S(1)} %get-tuple-element.79), channel_id=1, source_target_pairs={{0,4},{1,5},{2,6},{3,7},{4,0},{5,1},{6,2},{7,3},{8,12},{9,13},{10,... | collective-permute-start | bytes 294920 | tf_op jit(solution)/shard_map/ppermute | solution.py:608
  85.8 4.7 %copy-start.14 = (bf16[96,512]{1,0:T(8,128)(2,1)}, bf16[96,512]{1,0:T(8,128)(2,1)S(1)}, u32[]{:S(2)}) copy-start(bf16[96,512]{1,0:T(8,128)(2,1)S(1)} %collective-permute-done.11.refs_21_) | copy-start | bytes 294916
  88.4 2.1 %copy-start.15 = (bf16[96,512]{1,0:T(8,128)(2,1)}, bf16[96,512]{1,0:T(8,128)(2,1)S(1)}, u32[]{:S(2)}) copy-start(bf16[96,512]{1,0:T(8,128)(2,1)S(1)} %collective-permute-done.12.refs_22_) | copy-start | bytes 294916
  88.4 2.1 %copy-start.16 = (bf16[96,512]{1,0:T(8,128)(2,1)}, bf16[96,512]{1,0:T(8,128)(2,1)S(1)}, u32[]{:S(2)}) copy-start(bf16[96,512]{1,0:T(8,128)(2,1)S(1)} %collective-permute-done.13.refs_23_) | copy-start | bytes 294916
  102.5 4.1 %collective-permute-start.16 = (bf16[1792,512]{1,0:T(8,128)(2,1)}, bf16[1792,512]{1,0:T(8,128)(2,1)S(1)}, u32[]{:S(2)}, u32[]{:S(2)}) collective-permute-start(bf16[1792,512]{1,0:T(8,128)(2,1)} %get-tuple-element.81), channel_id=1, source_target_pairs={{0,4},{1,5},{2,6},{3,7},{4,0},{5,1},{6,2},{7,3},{8,12},{9,13},{10,... | collective-permute-start | bytes 5505032 | tf_op jit(solution)/shard_map/ppermute | solution.py:630
  103.0 6.1 %collective-permute-start.17 = (bf16[96,512]{1,0:T(8,128)(2,1)}, bf16[96,512]{1,0:T(8,128)(2,1)S(1)}, u32[]{:S(2)}, u32[]{:S(2)}) collective-permute-start(bf16[96,512]{1,0:T(8,128)(2,1)} %get-tuple-element.82), channel_id=1, source_target_pairs={{0,1},{1,2},{2,3},{3,4},{4,5},{5,6},{6,7},{7,8},{8,9},{9,10},{10,1... | collective-permute-start | bytes 294920 | tf_op jit(solution)/shard_map/ppermute | solution.py:628
  103.0 6.1 %collective-permute-start.18 = (bf16[96,512]{1,0:T(8,128)(2,1)}, bf16[96,512]{1,0:T(8,128)(2,1)S(1)}, u32[]{:S(2)}, u32[]{:S(2)}) collective-permute-start(bf16[96,512]{1,0:T(8,128)(2,1)} %get-tuple-element.83), channel_id=1, source_target_pairs={{1,0},{2,1},{3,2},{4,3},{5,4},{6,5},{7,6},{8,7},{9,8},{10,9},{11,1... | collective-permute-start | bytes 294920 | tf_op jit(solution)/shard_map/ppermute | solution.py:629
  106.6 1.5 copy-start
  109.1 32.8 %copy-start.2 = (f32[384,512]{1,0:T(8,128)S(1)}, f32[384,512]{1,0:T(8,128)}, u32[]{:S(2)}) copy-start(f32[384,512]{1,0:T(8,128)} %get-tuple-element.87.direct_far) | copy-start | bytes 2359300
  109.1 32.8 %copy-start.6 = (s32[192]{0:T(256)S(1)}, s32[192]{0:T(256)}, u32[]{:S(2)}) copy-start(s32[192]{0:T(256)} %index_far.3) | copy-start | bytes 2308
  (6 other events, 3.9 us)

commit v4 on v3

--- a/solution.py
+++ b/solution.py
@@ -19,6 +19,7 @@
 ENDS = DST + NODES
 TALL = 14
 HELD = 16
+VMEM = 57_000_000
 
 
 def place(z, y, c, x):
@@ -94,11 +95,12 @@
     return jax.ShapeDtypeStruct(shape, jnp.int32)
 
 
-def run(body, outs, args, kinds, scratch=(), copies=0, mib=16, flops=0):
+def run(body, outs, args, kinds, scratch=(), copies=0, mib=16, room=0, flops=0):
     spaces = {"s": pltpu.SMEM, "v": pltpu.VMEM, "h": pltpu.HBM}
     moved = sum(a.size * a.dtype.itemsize for a in list(args) + list(outs))
     took, gave = kinds.split(">")
     scratch = list(scratch)
+    limit = VMEM - room if room else mib << 20
     if copies:
         scratch.append(pltpu.SemaphoreType.DMA((copies,)))
     return pl.pallas_call(
@@ -107,7 +109,7 @@
         in_specs=[pl.BlockSpec(memory_space=spaces[k]) for k in took],
         out_specs=[pl.BlockSpec(memory_space=spaces[k]) for k in gave],
         scratch_shapes=scratch,
-        compiler_params=pltpu.CompilerParams(vmem_limit_bytes=mib << 20),
+        compiler_params=pltpu.CompilerParams(vmem_limit_bytes=limit),
         cost_estimate=pl.CostEstimate(flops=flops, bytes_accessed=moved, transcendentals=0),
     )(*args)
 
@@ -180,6 +182,7 @@
     slope_far,
     gathered_far,
     aggregate_far,
+    rims_far,
     *rest,
 ):
     sent_far, rest = rest[:PLANE], rest[PLANE:]
@@ -223,6 +226,8 @@
         if start == 0:
             for copy in copies[2:7]:
                 copy.wait()
+            store(lower, rims_far.at[pl.ds(0, RIM)])
+            store(upper, rims_far.at[pl.ds(RIM, RIM)])
             table[DST:, :] = mine[...]
             table[NODES : NODES + RIM, :] = dot(lower[...], w_src[...]).astype(BF)
             table[NODES + RIM : EXT, :] = dot(upper[...], w_src[...]).astype(BF)
@@ -277,17 +282,15 @@
     cot_far,
     w_mid_far,
     spread,
+    up_agg,
+    mid_back,
     mid_out_far,
     grad_mid_far,
-    up_agg_far,
-    mid_back_far,
     latent,
     cot,
     w_mid,
     mid_out,
     grad_mid,
-    up_agg,
-    mid_back,
     sems,
 ):
     copies = fetch(sems, (latent_far, latent), (cot_far, cot), (w_mid_far, w_mid))
@@ -304,16 +307,13 @@
     back = (cot[...].astype(F32) * slope).astype(BF)
     mid_back[...] = back
     stores = [
-        pltpu.make_async_copy(up_agg, up_agg_far, sems.at[3]),
-        pltpu.make_async_copy(mid_out, mid_out_far, sems.at[4]),
-        pltpu.make_async_copy(mid_back, mid_back_far, sems.at[5]),
-        pltpu.make_async_copy(grad_mid, grad_mid_far, sems.at[6]),
+        pltpu.make_async_copy(mid_out, mid_out_far, sems.at[3]),
+        pltpu.make_async_copy(grad_mid, grad_mid_far, sems.at[4]),
     ]
-    for copy in stores[:3]:
-        copy.start()
+    stores[0].start()
     grad = dot_nt(back, w_mid[:WIDTH, :]).astype(BF).astype(F32)
     grad_mid[...] = (cot[...].astype(F32) + grad).astype(BF)
-    stores[3].start()
+    stores[1].start()
     grad = dot_nt(back, w_mid[WIDTH:, :]).astype(BF).astype(F32)
     grad = (0.25 * grad).astype(BF)
     for z in range(ZN):
@@ -328,12 +328,16 @@
         back[i][...] = dot_t(down(owner[i : i + 1, :], ZN * MIDS), rows)[:SLOTS].astype(BF)
 
 
-def part_cores(flat, first, pairs, stage):
+def part_cores(mine, flat, first, pairs, keep, send):
     for pair in range(first, first + pairs):
-        for c in range(CN):
-            rows = [flat[pl.ds(224 * pair + 112 * h + 56 * c, 56), :] for h in range(2)]
-            rows = jnp.concatenate(rows, axis=0).astype(BF)
-            stage[c, 112 * pair : 112 * (pair + 1), :] = rows
+        even, odd = [
+            jnp.concatenate(
+                [flat[pl.ds(224 * pair + 112 * h + 56 * c, 56), :] for h in range(2)], axis=0
+            )
+            for c in range(CN)
+        ]
+        keep[112 * pair : 112 * (pair + 1), :] = jnp.where(mine == 0, even, odd).astype(BF)
+        send[112 * pair : 112 * (pair + 1), :] = jnp.where(mine == 0, odd, even).astype(BF)
 
 
 def backward_body(
@@ -341,92 +345,29 @@
     place_at,
     *refs,
 ):
-    (
-    spot_far,
-    cot_far,
-    node_slope_far,
-    w_node_far,
-    w_msg_far,
-    dst_far,
-    gathered_far,
-    latent_far,
-    aggregate_far,
-    mid_far,
-    mid_back_far,
-    up_agg_far,
-    src_far,
-    slope_far,
-    lower_far,
-    upper_far,
-    w_src_far,
-    w_dst_far,
-    ) = refs[:18]
-    back_far, refs = refs[18 : 18 + PLANE], refs[18 + PLANE :]
-    direct_far, low_far, high_far, keep_far, send_far = refs[:5]
-    spot, back, cot, node_slope, w_node, w_msg, dst, gathered, latent, aggregate = refs[5:15]
-    mid, mid_back, up_agg, src, edge_slope, lower, upper, w_src, w_dst = refs[15:24]
-    node_back, grad_agg, grad_gathered, grad_ends, rims, direct = refs[24:30]
-    targets, total, flat, stage, sems, out_sems = refs[30:]
-    copies = fetch(
-        sems,
-        (spot_far, spot),
-        *[(back_far[i], back.at[i]) for i in range(PLANE)],
-        (cot_far, cot),
-        (node_slope_far, node_slope),
-        (w_node_far, w_node),
-        (w_msg_far, w_msg),
-        (dst_far, dst),
-        (gathered_far, gathered),
-        (latent_far, latent),
-        (aggregate_far, aggregate),
-        (mid_far, mid),
-        (mid_back_far, mid_back),
-        (up_agg_far, up_agg),
-        (src_far, src),
-        (slope_far, edge_slope),
-        (lower_far, lower),
-        (upper_far, upper),
-        (w_src_far, w_src),
-        (w_dst_far, w_dst),
-    )
-    stores = []
-
-    def store(here, there):
-        stores.append(pltpu.make_async_copy(here, there, out_sems.at[len(stores)]))
-        stores[-1].start()
-
+    spot, up_agg, mid_back, cot, node_slope, w_node, w_msg, dst, gathered, latent = refs[:10]
+    aggregate, mid, src, edge_slope, rims_in, w_src, w_dst = refs[10:17]
+    back, refs = refs[17 : 17 + PLANE], refs[17 + PLANE :]
+    direct, low, high, keep, send = refs[:5]
+    node_back, grad_agg, grad_gathered, grad_ends, targets, total, flat = refs[5:]
     mine = place_at[0] & 1
-    for copy in copies[:9]:
-        copy.wait()
-    copies = copies[7:]
     up = jnp.zeros((NODES, WIDTH), F32)
     for i, (dy, dc) in enumerate(PEERS):
         offset = spot[...] - peer(place_at[0], dy, dc) * SLOTS
-        up = up + dot_t(down(offset, SLOTS), back[i])
-    for copy in copies[2:4]:
-        copy.wait()
+        up = up + dot_t(down(offset, SLOTS), back[i][...])
     cot_sum = (cot[...].astype(F32) + up).astype(BF).astype(F32)
     node_back[...] = (cot_sum * node_slope[...]).astype(BF)
-    copies[4].wait()
     grad_agg[...] = dot_nt(node_back[...], w_node[WIDTH:, :]).astype(BF)
-    copies[5].wait()
     grad_gathered[...] = dot_nt(grad_agg[...], w_msg[...]).astype(BF)
     direct[...] = cot_sum + dot_nt(node_back[...], w_node[:WIDTH, :]).astype(BF).astype(F32)
 
-    for copy in copies[6:13]:
-        copy.wait()
     flat[1024:1536, :] = dot_t(gathered[...], grad_agg[...])
     flat[1536:2048, :] = dot_t(latent[...], node_back[...])
     flat[2048:2560, :] = dot_t(aggregate[...], node_back[...])
     flat[2560:3072, :] = dot_t(mid[...], mid_back[...])
     flat[3072:, :] = dot_t(up_agg[...], mid_back[...])
-    part_cores(flat, 5, 11, stage)
-    rest = pl.ds(560, 1232)
-    store(stage.at[mine, rest], keep_far.at[rest])
-    store(stage.at[1 - mine, rest], send_far.at[rest])
-
-    for copy in copies[13:]:
-        copy.wait()
+    part_cores(mine, flat, 5, 11, keep, send)
+
     lane = iota((128, 128), 1)
     for start in range(0, EDGES, STEP):
         for at in range(start, start + STEP, 128):
@@ -444,23 +385,15 @@
             total[:EXT, :] += from_src
             total[EXT:, :] += from_dst
     grad_ends[...] = total[...].astype(BF)
-    rims[...] = dot_nt(grad_ends[NODES:EXT, :], w_src[...]).astype(BF)
-    store(rims.at[pl.ds(0, RIM)], low_far)
-    store(rims.at[pl.ds(RIM, RIM)], high_far)
-
-    grad = dot_t(lower[...], grad_ends[NODES : NODES + RIM, :])
-    grad = grad + dot_t(upper[...], grad_ends[NODES + RIM : EXT, :])
+    rims = dot_nt(grad_ends[NODES:EXT, :], w_src[...]).astype(BF)
+    low[...] = rims[:RIM]
+    high[...] = rims[RIM:]
+    grad = dot_t(rims_in[...], grad_ends[NODES:EXT, :])
     flat[:512, :] = grad + dot_t(latent[...], grad_ends[:NODES, :])
     flat[512:1024, :] = dot_t(latent[...], grad_ends[EXT:, :])
-    part_cores(flat, 0, 5, stage)
-    head = pl.ds(0, 560)
-    store(stage.at[mine, head], keep_far.at[head])
-    store(stage.at[1 - mine, head], send_far.at[head])
+    part_cores(mine, flat, 0, 5, keep, send)
     grad = dot_nt(grad_ends[:NODES, :], w_src[...]) + dot_nt(grad_ends[EXT:, :], w_dst[...])
     direct[...] += grad
-    store(direct, direct_far)
-    for copy in stores:
-        copy.wait()
 
 
 def sheet_body(keep, got, out, rows, held):
@@ -480,21 +413,18 @@
     got,
     low_far,
     high_far,
-    direct_far,
+    direct,
     index_far,
     out,
     grad_fine_far,
     low,
     high,
-    direct,
     index,
     grad_fine,
     rows,
     sems,
 ):
-    copies = fetch(
-        sems, (index_far, index), (low_far, low), (high_far, high), (direct_far, direct)
-    )
+    copies = fetch(sems, (index_far, index), (low_far, low), (high_far, high))
     total = got[0].astype(F32)
     for i in range(1, YN * XN):
         total = total + got[i].astype(F32)
@@ -508,7 +438,7 @@
     total = direct[...] + dot(down(row[:, :RIM], NODES), low[...])
     total = total + dot(down(row[:, RIM:], NODES), high[...])
     grad_fine[...] = total.astype(BF)
-    copy = pltpu.make_async_copy(grad_fine, grad_fine_far, sems.at[4])
+    copy = pltpu.make_async_copy(grad_fine, grad_fine_far, sems.at[3])
     copy.start()
     copy.wait()
 
@@ -572,18 +502,18 @@
         flops=4 * NODES * WIDTH * WIDTH,
     )
     dma = pltpu.SemaphoreType.DMA
-    fine_out, node_slope, edge_slope, gathered, aggregate, *sent = run(
+    fine_out, node_slope, edge_slope, gathered, aggregate, rims_in, *sent = run(
         forward_body,
-        (fine, f32(NODES, WIDTH), bf(EDGES, WIDTH), fine, fine) + PLANE * (bf(CARRY, WIDTH),),
+        (fine, f32(NODES, WIDTH), bf(EDGES, WIDTH), fine, fine, bf(2 * RIM, WIDTH)) + PLANE * (bf(CARRY, WIDTH),),
         (edge_count, place_at, edge_src, edge_dst, near, mine, w_src, lower, upper, w_msg, w_node)
         + (fine_latent, spot, up_node),
-        "ss" + 12 * "h" + ">" + 13 * "h",
+        "ss" + 12 * "h" + ">" + 14 * "h",
         (line(EDGES), line(EDGES), hold(NODES, WIDTH), hold(WIDTH, WIDTH), hold(RIM, WIDTH))
         + (hold(RIM, WIDTH), hold(WIDTH, WIDTH), hold(2 * WIDTH, WIDTH), hold(NODES, WIDTH))
         + (pltpu.VMEM((1, NODES), jnp.int32), line(NODES), hold(NODES, WIDTH))
         + (hold(PLANE, CARRY, WIDTH), wide(NODES, WIDTH), hold(EDGES, WIDTH))
         + (hold(NODES, WIDTH), hold(NODES, WIDTH), hold(ENDS, WIDTH), hold(EDGES, ENDS))
-        + (dma((12,)), dma((15,))),
+        + (dma((12,)), dma((17,))),
         mib=60,
         flops=4 * 10**9,
     )
@@ -592,37 +522,30 @@
         got.append(lax.ppermute(block, BOTH, shift(dy=dy, dc=dc)))
     sums, owner = run(sum_body, (bf(ZN, MIDS, WIDTH), i32(PLANE, 128)), got, 8 * "v" + ">vv")
     got = lax.all_to_all(sums, "row", 0, 0, axis_index_groups=PILLARS)
-    spread, mid_out, grad_mid, up_agg, mid_back = run(
+    spread, up_agg, mid_back, mid_out, grad_mid = run(
         mid_body,
         (bf(ZN, MIDS, WIDTH), mid, mid, mid, mid),
         (got, mid_latent, cot_mid, w_mid),
-        "vhhh>vhhhh",
+        "vhhh>vvvhh",
         (hold(MIDS, WIDTH), hold(MIDS, WIDTH), hold(2 * WIDTH, WIDTH))
-        + 4 * (hold(MIDS, WIDTH),),
-        copies=7,
+        + 2 * (hold(MIDS, WIDTH),),
+        copies=5,
     )
     got = lax.all_to_all(spread, "row", 0, 0, axis_index_groups=PILLARS)
     blocks = run(spread_body, PLANE * (bf(SLOTS, WIDTH),), (owner, got), "vv>" + 8 * "v")
     back = [blocks[0]]
     for (dy, dc), block in zip(PEERS[1:], blocks[1:]):
         back.append(lax.ppermute(block, BOTH, shift(dy=-dy, dc=-dc)))
+    far = (cot_fine, node_slope, w_node, w_msg, edge_dst, gathered, fine_latent, aggregate)
+    far += (mid_latent, edge_src, edge_slope, rims_in, w_src, w_dst)
     direct, low, high, keep, send = run(
         backward_body,
         (f32(NODES, WIDTH), rim, rim, bf(1792, WIDTH), bf(1792, WIDTH)),
-        (edge_count, place_at, spot, cot_fine, node_slope, w_node, w_msg, edge_dst, gathered)
-        + (fine_latent, aggregate, mid_latent, mid_back, up_agg, edge_src, edge_slope, lower)
-        + (upper, w_src, w_dst, *back),
-        "ss" + 26 * "h" + ">hhhhh",
-        (pltpu.VMEM((1, NODES), jnp.int32), hold(PLANE, SLOTS, WIDTH), hold(NODES, WIDTH))
-        + (wide(NODES, WIDTH), hold(2 * WIDTH, WIDTH), hold(WIDTH, WIDTH), line(EDGES))
-        + (hold(NODES, WIDTH), hold(NODES, WIDTH), hold(NODES, WIDTH), hold(MIDS, WIDTH))
-        + (hold(MIDS, WIDTH), hold(MIDS, WIDTH), line(EDGES), hold(EDGES, WIDTH))
-        + (hold(RIM, WIDTH), hold(RIM, WIDTH), hold(WIDTH, WIDTH), hold(WIDTH, WIDTH))
-        + (hold(NODES, WIDTH), hold(NODES, WIDTH), hold(NODES, WIDTH))
-        + (hold(EXT + NODES, WIDTH), hold(2 * RIM, WIDTH), wide(NODES, WIDTH))
-        + (hold(EDGES, NODES), wide(EXT + NODES, WIDTH), wide(3584, WIDTH))
-        + (hold(CN, 1792, WIDTH), dma((26,)), dma((7,))),
-        mib=60,
+        (edge_count, place_at, spot, up_agg, mid_back, *far, *back),
+        "ss" + (3 + len(far) + PLANE) * "v" + ">vvvvv",
+        (hold(NODES, WIDTH), hold(NODES, WIDTH), hold(NODES, WIDTH), hold(EXT + NODES, WIDTH))
+        + (hold(EDGES, NODES), wide(EXT + NODES, WIDTH), wide(3584, WIDTH)),
+        room=17_000_000,
         flops=5 * 10**9,
     )
     from_low = lax.ppermute(high, BOTH, ahead)
@@ -643,10 +566,10 @@
         pillar_body,
         (bf(ZN, HELD, WIDTH), fine),
         (part, from_low, from_high, direct, send_index),
-        "vhhhh>vh",
-        (hold(RIM, WIDTH), hold(RIM, WIDTH), wide(NODES, WIDTH), line(2 * RIM))
+        "vhhvh>vh",
+        (hold(RIM, WIDTH), hold(RIM, WIDTH), line(2 * RIM))
         + (hold(NODES, WIDTH), wide(128, WIDTH)),
-        copies=5,
+        copies=4,
         mib=24,
     )
     part = lax.all_to_all(part, "row", 0, 0, axis_index_groups=PILLARS)

time: 157 us -> 152 us (0.968)
  Pallas kernels: 31.4 us -> 27.6 us
  local copies, waits for them, and re-layouts: 4.95 us -> 3.28 us
    pallas_call x10, Pallas kernels: 31.4 us -> 27.6 us  [run(): pl.pallas_call(body, out_shape=list(outs), in_specs=[pl.BlockSpec(memory_...]
    unnamed x38 -> x42, local copies, waits for them, and re-layouts: 4.95 us -> 3.28 us
  transfers between devices with their start and end apart: 19 -> 19, of which waited for: 8 -> 9; matrix products, arithmetic and copies ran while one was open for 0% -> 0% of each run, Pallas kernels for 2% -> 2%
where the time goes in v4:
time: 152 us
  blocking collectives  72.4 us (48%)
  starting transfers between devices  35.3 us (23%)
  Pallas kernels  27.6 us (18%)
  waiting for transfers between devices  11.8 us (8%)
  local copies, waits for them, and re-layouts  3.28 us (2%)
  between operations  1.61 us (1%)
    all_to_all x1, blocking collectives, on_device(): part = lax.all_to_all(part, BOTH, 0, 0, axis_index_groups=SHEETS)  33.3 us
    pallas_call x10, Pallas kernels, run(): pl.pallas_call(body, out_shape=list(outs), in_specs=[pl.BlockSpec(memory_...  27.6 us
    ppermute x7, starting transfers between devices, on_device(): got.append(lax.ppermute(block, BOTH, shift(dy=dy, dc=dc)))  15.5 us
    all_to_all x1, blocking collectives, on_device(): got = lax.all_to_all(sums, 'row', 0, 0, axis_index_groups=PILLARS)  15.3 us
    ppermute x7, starting transfers between devices, on_device(): back.append(lax.ppermute(block, BOTH, shift(dy=-dy, dc=-dc)))  12.4 us
    all_to_all x1, blocking collectives, on_device(): got = lax.all_to_all(spread, 'row', 0, 0, axis_index_groups=PILLARS)  12 us
    all_to_all x1, blocking collectives, on_device(): part = lax.all_to_all(part, 'row', 0, 0, axis_index_groups=PILLARS)  11.8 us
    ppermute x7, waiting for transfers between devices, on_device(): back.append(lax.ppermute(block, BOTH, shift(dy=-dy, dc=-dc)))  5.74 us
  transfers between devices with their start and end apart: 19, of which 9 were waited for; matrix products, arithmetic and copies ran while one was open for 0% of the time, Pallas kernels for 2%

profile of v4, /device:TPU:1, one launch (start us, length us, event | category | flops | bytes accessed | tf_op | source)
XLA Modules:
  0.0 152.1 jit_solution(17333435936425500419)
XLA Ops:
  0.6 2.0 %shard_map.183 = (bf16[96,512]{1,0:T(8,128)(2,1)}, bf16[96,512]{1,0:T(8,128)(2,1)}) custom-call(s32[192]{0:T(256)} %index_far.3, bf16[384,512]{1,0:T(8,128)(2,1)} %refs_9_.1), custom_call_target="tpu_custom_call" | custom-call | bytes 590592 | tf_op jit(solution)/shard_map/pallas_call | solution.py:106
  2.6 2.1 %collective-permute-start = (bf16[96,512]{1,0:T(8,128)(2,1)}, bf16[96,512]{1,0:T(8,128)(2,1)S(1)}, u32[]{:S(2)}, u32[]{:S(2)}) collective-permute-start(bf16[96,512]{1,0:T(8,128)(2,1)} %get-tuple-element.51), channel_id=1, source_target_pairs={{0,1},{1,2},{2,3},{3,4},{4,5},{5,6},{6,7},{7,8},{8,9},{9,10},{10,1... | collective-permute-start | bytes 294920 | tf_op jit(solution)/shard_map/ppermute | solution.py:491
  4.7 1.9 %collective-permute-start.1 = (bf16[96,512]{1,0:T(8,128)(2,1)}, bf16[96,512]{1,0:T(8,128)(2,1)S(1)}, u32[]{:S(2)}, u32[]{:S(2)}) collective-permute-start(bf16[96,512]{1,0:T(8,128)(2,1)} %get-tuple-element.52), channel_id=1, source_target_pairs={{1,0},{2,1},{3,2},{4,3},{5,4},{6,5},{7,6},{8,7},{9,8},{10,9},{11,1... | collective-permute-start | bytes 294920 | tf_op jit(solution)/shard_map/ppermute | solution.py:492
  7.3 2.7 %shard_map.182 = (bf16[384,512]{1,0:T(8,128)(2,1)}, bf16[384,512]{1,0:T(8,128)(2,1)}, s32[1,384]{1,0:T(1,128)}) custom-call(s32[1,384]{1,0:T(1,128)} %bitcast.2, bf16[384,512]{1,0:T(8,128)(2,1)} %refs_9_.1, bf16[512,512]{1,0:T(8,128)(2,1)} %refs_15_.1, bf16[512,512]{1,0:T(8,128)(2,1)} %refs_16_.1), custom_call_target="tpu_custom_call" | custom-call | flops 402653184 | bytes 2231296 | tf_op jit(solution)/shard_map/pallas_call | solution.py:106
  10.8 9.5 %shard_map.184 = (bf16[384,512]{1,0:T(8,128)(2,1)}, f32[384,512]{1,0:T(8,128)}, bf16[2304,512]{1,0:T(8,128)(2,1)}, bf16[384,512]{1,0:T(8,128)(2,1)}, bf16[384,51...) custom-call(s32[1]{0:T(128)S(6)} %copy.20.count, ...), custom_call_target="tpu_custom_call" | custom-call | flops 4000000000 | bytes 8934408 | tf_op jit(solution)/shard_map/pallas_call | solution.py:106
  20.3 3.0 %collective-permute-start.2 = (bf16[112,512]{1,0:T(8,128)(2,1)}, bf16[112,512]{1,0:T(8,128)(2,1)S(1)}, u32[]{:S(2)}, u32[]{:S(2)}) collective-permute-start(bf16[112,512]{1,0:T(8,128)(2,1)} %get-tuple-element.56), channel_id=1, source_target_pairs={{0,16},{1,17},{2,18},{3,19},{4,20},{5,21},{6,22},{7,23},{8,24},{9,... | collective-permute-start | bytes 344072 | tf_op jit(solution)/shard_map/ppermute | solution.py:522
  23.3 7.8 %collective-permute-start.3 = (bf16[112,512]{1,0:T(8,128)(2,1)}, bf16[112,512]{1,0:T(8,128)(2,1)S(1)}, u32[]{:S(2)}, u32[]{:S(2)}) collective-permute-start(bf16[112,512]{1,0:T(8,128)(2,1)} %get-tuple-element.57), channel_id=1, source_target_pairs={{0,20},{1,21},{2,22},{3,23},{4,16},{5,17},{6,18},{7,19},{8,28},{9,... | collective-permute-start | bytes 344072 | tf_op jit(solution)/shard_map/ppermute | solution.py:522
  31.1 2.7 %collective-permute-start.6 = (bf16[112,512]{1,0:T(8,128)(2,1)}, bf16[112,512]{1,0:T(8,128)(2,1)S(1)}, u32[]{:S(2)}, u32[]{:S(2)}) collective-permute-start(bf16[112,512]{1,0:T(8,128)(2,1)} %get-tuple-element.60), channel_id=1, source_target_pairs={{0,24},{1,25},{2,26},{3,27},{4,28},{5,29},{6,30},{7,31},{8,0},{9,1... | collective-permute-start | bytes 344072 | tf_op jit(solution)/shard_map/ppermute | solution.py:522
  33.8 2.0 %collective-permute-start.7 = (bf16[112,512]{1,0:T(8,128)(2,1)}, bf16[112,512]{1,0:T(8,128)(2,1)S(1)}, u32[]{:S(2)}, u32[]{:S(2)}) collective-permute-start(bf16[112,512]{1,0:T(8,128)(2,1)} %get-tuple-element.61), channel_id=1, source_target_pairs={{0,28},{1,29},{2,30},{3,31},{4,24},{5,25},{6,26},{7,27},{8,4},{9,5... | collective-permute-start | bytes 344072 | tf_op jit(solution)/shard_map/ppermute | solution.py:522
  35.8 1.6 %collective-permute-done.3.refs_2_ = bf16[112,512]{1,0:T(8,128)(2,1)S(1)} collective-permute-done((bf16[112,512]{1,0:T(8,128)(2,1)}, bf16[112,512]{1,0:T(8,128)(2,1)S(1)}, u32[]{:S(2)}, u32[]{:S(2)}) %collective-permute-start.3) | collective-permute-done | bytes 114720 | tf_op jit(solution)/shard_map/ppermute | solution.py:522
  37.4 1.3 collective-permute-done.4.refs_3_
  38.7 1.8 %collective-permute-done.5.refs_4_ = bf16[112,512]{1,0:T(8,128)(2,1)S(1)} collective-permute-done((bf16[112,512]{1,0:T(8,128)(2,1)}, bf16[112,512]{1,0:T(8,128)(2,1)S(1)}, u32[]{:S(2)}, u32[]{:S(2)}) %collective-permute-start.5) | collective-permute-done | bytes 114720 | tf_op jit(solution)/shard_map/ppermute | solution.py:522
  40.5 0.9 copy-done.2
  41.4 0.7 shard_map.185
  42.1 15.3 %all_to_all.20.got = bf16[8,32,512]{2,1,0:T(8,128)(2,1)S(1)} all-to-all(bf16[8,32,512]{2,1,0:T(8,128)(2,1)S(1)} %get-tuple-element.63), channel_id=1, replica_groups={{0,32,64,96,128,160,192,224},{4,36,68,100,132,164,196,228},{8,40,72,104..., dimensions={0} | all-to-all | bytes 524288 | tf_op jit(solution)/shard_map/all_to_all | solution.py:524
  57.5 1.4 shard_map.186
  58.8 12.0 %all_to_all.21.got = bf16[8,32,512]{2,1,0:T(8,128)(2,1)S(1)} all-to-all(bf16[8,32,512]{2,1,0:T(8,128)(2,1)S(1)} %get-tuple-element.73), channel_id=1, replica_groups={{0,32,64,96,128,160,192,224},{4,36,68,100,132,164,196,228},{8,40,72,104..., dimensions={0} | all-to-all | bytes 524288 | tf_op jit(solution)/shard_map/all_to_all | solution.py:534
  71.3 6.0 %collective-permute-start.9 = (bf16[96,512]{1,0:T(8,128)(2,1)S(1)}, bf16[96,512]{1,0:T(8,128)(2,1)S(1)}, u32[]{:S(2)}, u32[]{:S(2)}) collective-permute-start(bf16[96,512]{1,0:T(8,128)(2,1)S(1)} %get-tuple-element.75), channel_id=1, source_target_pairs={{0,16},{1,17},{2,18},{3,19},{4,20},{5,21},{6,22},{7,23},{8,24},{9,... | collective-permute-start | bytes 294920 | tf_op jit(solution)/shard_map/ppermute | solution.py:538
  77.3 0.7 collective-permute-start.10
  78.1 3.3 %collective-permute-start.11 = (bf16[96,512]{1,0:T(8,128)(2,1)S(1)}, bf16[96,512]{1,0:T(8,128)(2,1)S(1)}, u32[]{:S(2)}, u32[]{:S(2)}) collective-permute-start(bf16[96,512]{1,0:T(8,128)(2,1)S(1)} %get-tuple-element.77), channel_id=1, source_target_pairs={{0,24},{1,25},{2,26},{3,27},{4,28},{5,29},{6,30},{7,31},{8,0},{9,1... | collective-permute-start | bytes 294920 | tf_op jit(solution)/shard_map/ppermute | solution.py:538
  81.4 1.8 %collective-permute-start.14 = (bf16[96,512]{1,0:T(8,128)(2,1)S(1)}, bf16[96,512]{1,0:T(8,128)(2,1)S(1)}, u32[]{:S(2)}, u32[]{:S(2)}) collective-permute-start(bf16[96,512]{1,0:T(8,128)(2,1)S(1)} %get-tuple-element.80), channel_id=1, source_target_pairs={{0,12},{1,13},{2,14},{3,15},{4,8},{5,9},{6,10},{7,11},{8,20},{9,21... | collective-permute-start | bytes 294920 | tf_op jit(solution)/shard_map/ppermute | solution.py:538
  83.2 0.9 collective-permute-done.10.refs_19_
  84.8 2.6 %collective-permute-done.12.refs_21_ = bf16[96,512]{1,0:T(8,128)(2,1)S(1)} collective-permute-done((bf16[96,512]{1,0:T(8,128)(2,1)S(1)}, bf16[96,512]{1,0:T(8,128)(2,1)S(1)}, u32[]{:S(2)}, u32[]{:S(2)}) %collective-permute-start.12) | collective-permute-done | bytes 98336 | tf_op jit(solution)/shard_map/ppermute | solution.py:538
  87.4 2.0 %collective-permute-done.14.refs_23_ = bf16[96,512]{1,0:T(8,128)(2,1)S(1)} collective-permute-done((bf16[96,512]{1,0:T(8,128)(2,1)S(1)}, bf16[96,512]{1,0:T(8,128)(2,1)S(1)}, u32[]{:S(2)}, u32[]{:S(2)}) %collective-permute-start.14) | collective-permute-done | bytes 98336 | tf_op jit(solution)/shard_map/ppermute | solution.py:538
  89.6 1.7 %copy-done.14 = bf16[2304,512]{1,0:T(8,128)(2,1)S(1)} copy-done((bf16[2304,512]{1,0:T(8,128)(2,1)S(1)}, bf16[2304,512]{1,0:T(8,128)(2,1)}, u32[]{:S(2)}) %copy-start.14) | copy-done | bytes 2359320
  91.2 7.6 %shard_map.188 = (f32[384,512]{1,0:T(8,128)S(1)}, bf16[96,512]{1,0:T(8,128)(2,1)S(1)}, bf16[96,512]{1,0:T(8,128)(2,1)S(1)}, bf16[1792,512]{1,0:T(8,128)(2,1)S(1)}, bf16[1792,512]{1,0:T(8,128)(2,1)S(1)}) custom-call(s32[1]{0:T(128)S(6)} %copy.20.count, s32[1]{0:T(128)} %bitcast.place_at, s32[1,384]{1,0:T(1,128)S(1)} %copy-done.13, ...), custom_call_target="tpu_custom_call" | custom-call | flops 5000000000 | bytes 13094408 | tf_op jit(solution)/shard_map/pallas_call | solution.py:106
  99.3 3.0 %collective-permute-start.18 = (bf16[96,512]{1,0:T(8,128)(2,1)S(1)}, bf16[96,512]{1,0:T(8,128)(2,1)S(1)}, u32[]{:S(2)}, u32[]{:S(2)}) collective-permute-start(bf16[96,512]{1,0:T(8,128)(2,1)S(1)} %get-tuple-element.85), channel_id=1, source_target_pairs={{1,0},{2,1},{3,2},{4,3},{5,4},{6,5},{7,6},{8,7},{9,8},{10,9},{11,1... | collective-permute-start | bytes 294920 | tf_op jit(solution)/shard_map/ppermute | solution.py:552
  102.7 0.9 shard_map.189
  103.7 0.9 collective-permute-done.17.low_far
  104.6 33.3 %all_to_all.22.got = bf16[16,112,512]{2,1,0:T(8,128)(2,1)S(1)} all-to-all(bf16[16,112,512]{2,1,0:T(8,128)(2,1)S(1)} %shard_map.189), channel_id=1, replica_groups={{0,1,2,3,8,9,10,11,16,17,18,19,24,25,26,27},{4,5,6,7,12,13,14,15,20,21,..., dimensions={0} | all-to-all | bytes 3670016 | tf_op jit(solution)/shard_map/all_to_all | solution.py:564
  137.9 1.7 %shard_map.190 = (bf16[8,16,512]{2,1,0:T(8,128)(2,1)S(1)}, bf16[384,512]{1,0:T(8,128)(2,1)}) custom-call(bf16[16,112,512]{2,1,0:T(8,128)(2,1)S(1)} %all_to_all.22.got, bf16[96,512]{1,0:T(8,128)(2,1)S(1)} %collective-permute-done.17.low_far, bf16[96,512]{1,0:T(8,128)(2,1)S(1)} %collective-permute-done.18.high_far, f32[384,512]{1,0:T(8,128)S(1)} %get-tuple-element.89.direct, ...), custom_call_target="tpu_custom_call" | custom-call | bytes 3343104 | tf_op jit(solution)/shard_map/pallas_call | solution.py:106
  139.6 11.8 %all_to_all.23.got = bf16[8,16,512]{2,1,0:T(8,128)(2,1)S(1)} all-to-all(bf16[8,16,512]{2,1,0:T(8,128)(2,1)S(1)} %get-tuple-element.92), channel_id=1, replica_groups={{0,32,64,96,128,160,192,224},{4,36,68,100,132,164,196,228},{8,40,72,104..., dimensions={0} | all-to-all | bytes 262144 | tf_op jit(solution)/shard_map/all_to_all | solution.py:575
  (62 shorter events, 3.6 us)
Async XLA Ops:
  2.6 7.4 %collective-permute-start = (bf16[96,512]{1,0:T(8,128)(2,1)}, bf16[96,512]{1,0:T(8,128)(2,1)S(1)}, u32[]{:S(2)}, u32[]{:S(2)}) collective-permute-start(bf16[96,512]{1,0:T(8,128)(2,1)} %get-tuple-element.51), channel_id=1, source_target_pairs={{0,1},{1,2},{2,3},{3,4},{4,5},{5,6},{6,7},{7,8},{8,9},{9,10},{10,1... | collective-permute-start | bytes 294920 | tf_op jit(solution)/shard_map/ppermute | solution.py:491
  4.7 5.3 %collective-permute-start.1 = (bf16[96,512]{1,0:T(8,128)(2,1)}, bf16[96,512]{1,0:T(8,128)(2,1)S(1)}, u32[]{:S(2)}, u32[]{:S(2)}) collective-permute-start(bf16[96,512]{1,0:T(8,128)(2,1)} %get-tuple-element.52), channel_id=1, source_target_pairs={{1,0},{2,1},{3,2},{4,3},{5,4},{6,5},{7,6},{8,7},{9,8},{10,9},{11,1... | collective-permute-start | bytes 294920 | tf_op jit(solution)/shard_map/ppermute | solution.py:492
  10.7 78.8 %copy-start.6 = (bf16[1024,512]{1,0:T(8,128)(2,1)S(1)}, bf16[1024,512]{1,0:T(8,128)(2,1)}, u32[]{:S(2)}) copy-start(bf16[1024,512]{1,0:T(8,128)(2,1)} %refs_5_.1) | copy-start | bytes 3145732
  10.7 78.8 %copy-start.7 = (bf16[512,512]{1,0:T(8,128)(2,1)S(1)}, bf16[512,512]{1,0:T(8,128)(2,1)}, u32[]{:S(2)}) copy-start(bf16[512,512]{1,0:T(8,128)(2,1)} %refs_15_.1) | copy-start | bytes 1572868
  10.7 78.8 %copy-start.8 = (bf16[512,512]{1,0:T(8,128)(2,1)S(1)}, bf16[512,512]{1,0:T(8,128)(2,1)}, u32[]{:S(2)}) copy-start(bf16[512,512]{1,0:T(8,128)(2,1)} %refs_16_.1) | copy-start | bytes 1572868
  10.7 78.8 %copy-start.9 = (bf16[512,512]{1,0:T(8,128)(2,1)S(1)}, bf16[512,512]{1,0:T(8,128)(2,1)}, u32[]{:S(2)}) copy-start(bf16[512,512]{1,0:T(8,128)(2,1)} %refs_6_.1) | copy-start | bytes 1572868
  10.7 78.8 %copy-start.10 = (bf16[384,512]{1,0:T(8,128)(2,1)S(1)}, bf16[384,512]{1,0:T(8,128)(2,1)}, u32[]{:S(2)}) copy-start(bf16[384,512]{1,0:T(8,128)(2,1)} %refs_3_.1) | copy-start | bytes 1179652
  10.7 78.8 %copy-start.11 = (s32[2304]{0:T(1024)S(1)}, s32[2304]{0:T(1024)}, u32[]{:S(2)}) copy-start(s32[2304]{0:T(1024)} %refs_12_.1) | copy-start | bytes 27652
  10.7 78.8 %copy-start.12 = (s32[2304]{0:T(1024)S(1)}, s32[2304]{0:T(1024)}, u32[]{:S(2)}) copy-start(s32[2304]{0:T(1024)} %refs_7_.1) | copy-start | bytes 27652
  10.8 78.8 %copy-start.13 = (s32[1,384]{1,0:T(1,128)S(1)}, s32[1,384]{1,0:T(1,128)}, u32[]{:S(2)}) copy-start(s32[1,384]{1,0:T(1,128)} %get-tuple-element.53.spot_far.refs_0_) | copy-start | bytes 4612
  20.3 69.2 %copy-start.1 = (bf16[384,512]{1,0:T(8,128)(2,1)S(1)}, bf16[384,512]{1,0:T(8,128)(2,1)}, u32[]{:S(2)}) copy-start(bf16[384,512]{1,0:T(8,128)(2,1)} %refs_9_.1) | copy-start | bytes 1179652
  20.3 13.5 %collective-permute-start.2 = (bf16[112,512]{1,0:T(8,128)(2,1)}, bf16[112,512]{1,0:T(8,128)(2,1)S(1)}, u32[]{:S(2)}, u32[]{:S(2)}) collective-permute-start(bf16[112,512]{1,0:T(8,128)(2,1)} %get-tuple-element.56), channel_id=1, source_target_pairs={{0,16},{1,17},{2,18},{3,19},{4,20},{5,21},{6,22},{7,23},{8,24},{9,... | collective-permute-start | bytes 344072 | tf_op jit(solution)/shard_map/ppermute | solution.py:522
  23.3 14.1 %collective-permute-start.3 = (bf16[112,512]{1,0:T(8,128)(2,1)}, bf16[112,512]{1,0:T(8,128)(2,1)S(1)}, u32[]{:S(2)}, u32[]{:S(2)}) collective-permute-start(bf16[112,512]{1,0:T(8,128)(2,1)} %get-tuple-element.57), channel_id=1, source_target_pairs={{0,20},{1,21},{2,22},{3,23},{4,16},{5,17},{6,18},{7,19},{8,28},{9,... | collective-permute-start | bytes 344072 | tf_op jit(solution)/shard_map/ppermute | solution.py:522
  31.1 7.6 %collective-permute-start.4 = (bf16[112,512]{1,0:T(8,128)(2,1)}, bf16[112,512]{1,0:T(8,128)(2,1)S(1)}, u32[]{:S(2)}, u32[]{:S(2)}) collective-permute-start(bf16[112,512]{1,0:T(8,128)(2,1)} %get-tuple-element.58), channel_id=1, source_target_pairs={{0,8},{1,9},{2,10},{3,11},{4,12},{5,13},{6,14},{7,15},{8,16},{9,17... | collective-permute-start | bytes 344072 | tf_op jit(solution)/shard_map/ppermute | solution.py:522
  31.1 9.4 %collective-permute-start.5 = (bf16[112,512]{1,0:T(8,128)(2,1)}, bf16[112,512]{1,0:T(8,128)(2,1)S(1)}, u32[]{:S(2)}, u32[]{:S(2)}) collective-permute-start(bf16[112,512]{1,0:T(8,128)(2,1)} %get-tuple-element.59), channel_id=1, source_target_pairs={{0,12},{1,13},{2,14},{3,15},{4,8},{5,9},{6,10},{7,11},{8,20},{9,21... | collective-permute-start | bytes 344072 | tf_op jit(solution)/shard_map/ppermute | solution.py:522
  31.1 9.4 %collective-permute-start.6 = (bf16[112,512]{1,0:T(8,128)(2,1)}, bf16[112,512]{1,0:T(8,128)(2,1)S(1)}, u32[]{:S(2)}, u32[]{:S(2)}) collective-permute-start(bf16[112,512]{1,0:T(8,128)(2,1)} %get-tuple-element.60), channel_id=1, source_target_pairs={{0,24},{1,25},{2,26},{3,27},{4,28},{5,29},{6,30},{7,31},{8,0},{9,1... | collective-permute-start | bytes 344072 | tf_op jit(solution)/shard_map/ppermute | solution.py:522
  33.8 6.7 %collective-permute-start.7 = (bf16[112,512]{1,0:T(8,128)(2,1)}, bf16[112,512]{1,0:T(8,128)(2,1)S(1)}, u32[]{:S(2)}, u32[]{:S(2)}) collective-permute-start(bf16[112,512]{1,0:T(8,128)(2,1)} %get-tuple-element.61), channel_id=1, source_target_pairs={{0,28},{1,29},{2,30},{3,31},{4,24},{5,25},{6,26},{7,27},{8,4},{9,5... | collective-permute-start | bytes 344072 | tf_op jit(solution)/shard_map/ppermute | solution.py:522
  37.4 3.1 %collective-permute-start.8 = (bf16[112,512]{1,0:T(8,128)(2,1)}, bf16[112,512]{1,0:T(8,128)(2,1)S(1)}, u32[]{:S(2)}, u32[]{:S(2)}) collective-permute-start(bf16[112,512]{1,0:T(8,128)(2,1)} %get-tuple-element.62), channel_id=1, source_target_pairs={{0,4},{1,5},{2,6},{3,7},{4,0},{5,1},{6,2},{7,3},{8,12},{9,13},{10,... | collective-permute-start | bytes 344072 | tf_op jit(solution)/shard_map/ppermute | solution.py:522
  41.4 48.1 %copy-start.15 = (f32[384,512]{1,0:T(8,128)S(1)}, f32[384,512]{1,0:T(8,128)}, u32[]{:S(2)}) copy-start(f32[384,512]{1,0:T(8,128)} %get-tuple-element.67.refs_4_) | copy-start | bytes 2359300
  41.4 48.1 %copy-start.16 = (bf16[384,512]{1,0:T(8,128)(2,1)S(1)}, bf16[384,512]{1,0:T(8,128)(2,1)}, u32[]{:S(2)}) copy-start(bf16[384,512]{1,0:T(8,128)(2,1)} %get-tuple-element.68.refs_8_) | copy-start | bytes 1179652
  41.4 48.1 %copy-start.17 = (bf16[384,512]{1,0:T(8,128)(2,1)S(1)}, bf16[384,512]{1,0:T(8,128)(2,1)}, u32[]{:S(2)}) copy-start(bf16[384,512]{1,0:T(8,128)(2,1)} %get-tuple-element.69.refs_10_) | copy-start | bytes 1179652
  41.4 48.1 %copy-start.18 = (bf16[192,512]{1,0:T(8,128)(2,1)S(1)}, bf16[192,512]{1,0:T(8,128)(2,1)}, u32[]{:S(2)}) copy-start(bf16[192,512]{1,0:T(8,128)(2,1)} %get-tuple-element.71.refs_14_) | copy-start | bytes 589828
  71.3 10.0 %collective-permute-start.9 = (bf16[96,512]{1,0:T(8,128)(2,1)S(1)}, bf16[96,512]{1,0:T(8,128)(2,1)S(1)}, u32[]{:S(2)}, u32[]{:S(2)}) collective-permute-start(bf16[96,512]{1,0:T(8,128)(2,1)S(1)} %get-tuple-element.75), channel_id=1, source_target_pairs={{0,16},{1,17},{2,18},{3,19},{4,20},{5,21},{6,22},{7,23},{8,24},{9,... | collective-permute-start | bytes 294920 | tf_op jit(solution)/shard_map/ppermute | solution.py:538
  77.3 6.7 %collective-permute-start.10 = (bf16[96,512]{1,0:T(8,128)(2,1)S(1)}, bf16[96,512]{1,0:T(8,128)(2,1)S(1)}, u32[]{:S(2)}, u32[]{:S(2)}) collective-permute-start(bf16[96,512]{1,0:T(8,128)(2,1)S(1)} %get-tuple-element.76), channel_id=1, source_target_pairs={{0,20},{1,21},{2,22},{3,23},{4,16},{5,17},{6,18},{7,19},{8,28},{9,... | collective-permute-start | bytes 294920 | tf_op jit(solution)/shard_map/ppermute | solution.py:538
  78.1 6.7 %collective-permute-start.11 = (bf16[96,512]{1,0:T(8,128)(2,1)S(1)}, bf16[96,512]{1,0:T(8,128)(2,1)S(1)}, u32[]{:S(2)}, u32[]{:S(2)}) collective-permute-start(bf16[96,512]{1,0:T(8,128)(2,1)S(1)} %get-tuple-element.77), channel_id=1, source_target_pairs={{0,24},{1,25},{2,26},{3,27},{4,28},{5,29},{6,30},{7,31},{8,0},{9,1... | collective-permute-start | bytes 294920 | tf_op jit(solution)/shard_map/ppermute | solution.py:538
  81.4 6.0 %collective-permute-start.12 = (bf16[96,512]{1,0:T(8,128)(2,1)S(1)}, bf16[96,512]{1,0:T(8,128)(2,1)S(1)}, u32[]{:S(2)}, u32[]{:S(2)}) collective-permute-start(bf16[96,512]{1,0:T(8,128)(2,1)S(1)} %get-tuple-element.78), channel_id=1, source_target_pairs={{0,28},{1,29},{2,30},{3,31},{4,24},{5,25},{6,26},{7,27},{8,4},{9,5... | collective-permute-start | bytes 294920 | tf_op jit(solution)/shard_map/ppermute | solution.py:538
  81.4 6.0 %collective-permute-start.13 = (bf16[96,512]{1,0:T(8,128)(2,1)S(1)}, bf16[96,512]{1,0:T(8,128)(2,1)S(1)}, u32[]{:S(2)}, u32[]{:S(2)}) collective-permute-start(bf16[96,512]{1,0:T(8,128)(2,1)S(1)} %get-tuple-element.79), channel_id=1, source_target_pairs={{0,8},{1,9},{2,10},{3,11},{4,12},{5,13},{6,14},{7,15},{8,16},{9,17... | collective-permute-start | bytes 294920 | tf_op jit(solution)/shard_map/ppermute | solution.py:538
  81.4 8.1 %collective-permute-start.14 = (bf16[96,512]{1,0:T(8,128)(2,1)S(1)}, bf16[96,512]{1,0:T(8,128)(2,1)S(1)}, u32[]{:S(2)}, u32[]{:S(2)}) collective-permute-start(bf16[96,512]{1,0:T(8,128)(2,1)S(1)} %get-tuple-element.80), channel_id=1, source_target_pairs={{0,12},{1,13},{2,14},{3,15},{4,8},{5,9},{6,10},{7,11},{8,20},{9,21... | collective-permute-start | bytes 294920 | tf_op jit(solution)/shard_map/ppermute | solution.py:538
  84.1 5.4 %collective-permute-start.15 = (bf16[96,512]{1,0:T(8,128)(2,1)S(1)}, bf16[96,512]{1,0:T(8,128)(2,1)S(1)}, u32[]{:S(2)}, u32[]{:S(2)}) collective-permute-start(bf16[96,512]{1,0:T(8,128)(2,1)S(1)} %get-tuple-element.81), channel_id=1, source_target_pairs={{0,4},{1,5},{2,6},{3,7},{4,0},{5,1},{6,2},{7,3},{8,12},{9,13},{10,... | collective-permute-start | bytes 294920 | tf_op jit(solution)/shard_map/ppermute | solution.py:538
  98.8 3.9 %collective-permute-start.16 = (bf16[1792,512]{1,0:T(8,128)(2,1)S(1)}, bf16[1792,512]{1,0:T(8,128)(2,1)S(1)}, u32[]{:S(2)}, u32[]{:S(2)}) collective-permute-start(bf16[1792,512]{1,0:T(8,128)(2,1)S(1)} %get-tuple-element.83), channel_id=1, source_target_pairs={{0,4},{1,5},{2,6},{3,7},{4,0},{5,1},{6,2},{7,3},{8,12},{9,13},{10,... | collective-permute-start | bytes 5505032 | tf_op jit(solution)/shard_map/ppermute | solution.py:553
  99.3 5.3 %collective-permute-start.17 = (bf16[96,512]{1,0:T(8,128)(2,1)S(1)}, bf16[96,512]{1,0:T(8,128)(2,1)S(1)}, u32[]{:S(2)}, u32[]{:S(2)}) collective-permute-start(bf16[96,512]{1,0:T(8,128)(2,1)S(1)} %get-tuple-element.84), channel_id=1, source_target_pairs={{0,1},{1,2},{2,3},{3,4},{4,5},{5,6},{6,7},{7,8},{8,9},{9,10},{10,1... | collective-permute-start | bytes 294920 | tf_op jit(solution)/shard_map/ppermute | solution.py:551
  99.3 5.3 %collective-permute-start.18 = (bf16[96,512]{1,0:T(8,128)(2,1)S(1)}, bf16[96,512]{1,0:T(8,128)(2,1)S(1)}, u32[]{:S(2)}, u32[]{:S(2)}) collective-permute-start(bf16[96,512]{1,0:T(8,128)(2,1)S(1)} %get-tuple-element.85), channel_id=1, source_target_pairs={{1,0},{2,1},{3,2},{4,3},{5,4},{6,5},{7,6},{8,7},{9,8},{10,9},{11,1... | collective-permute-start | bytes 294920 | tf_op jit(solution)/shard_map/ppermute | solution.py:552
  (8 other events, 168.7 us)

commit v5 on v4

--- a/solution.py
+++ b/solution.py
@@ -340,17 +340,11 @@
         send[112 * pair : 112 * (pair + 1), :] = jnp.where(mine == 0, odd, even).astype(BF)
 
 
-def backward_body(
-    count,
-    place_at,
-    *refs,
-):
-    spot, up_agg, mid_back, cot, node_slope, w_node, w_msg, dst, gathered, latent = refs[:10]
-    aggregate, mid, src, edge_slope, rims_in, w_src, w_dst = refs[10:17]
-    back, refs = refs[17 : 17 + PLANE], refs[17 + PLANE :]
-    direct, low, high, keep, send = refs[:5]
-    node_back, grad_agg, grad_gathered, grad_ends, targets, total, flat = refs[5:]
-    mine = place_at[0] & 1
+def backward_body(count, place_at, *refs):
+    spot, cot, node_slope, w_node, w_msg, dst, src, edge_slope, w_src, w_dst = refs[:10]
+    back, refs = refs[10 : 10 + PLANE], refs[10 + PLANE :]
+    direct, low, high, node_back, grad_agg, grad_ends = refs[:6]
+    grad_gathered, targets, total = refs[6:]
     up = jnp.zeros((NODES, WIDTH), F32)
     for i, (dy, dc) in enumerate(PEERS):
         offset = spot[...] - peer(place_at[0], dy, dc) * SLOTS
@@ -360,14 +354,6 @@
     grad_agg[...] = dot_nt(node_back[...], w_node[WIDTH:, :]).astype(BF)
     grad_gathered[...] = dot_nt(grad_agg[...], w_msg[...]).astype(BF)
     direct[...] = cot_sum + dot_nt(node_back[...], w_node[:WIDTH, :]).astype(BF).astype(F32)
-
-    flat[1024:1536, :] = dot_t(gathered[...], grad_agg[...])
-    flat[1536:2048, :] = dot_t(latent[...], node_back[...])
-    flat[2048:2560, :] = dot_t(aggregate[...], node_back[...])
-    flat[2560:3072, :] = dot_t(mid[...], mid_back[...])
-    flat[3072:, :] = dot_t(up_agg[...], mid_back[...])
-    part_cores(mine, flat, 5, 11, keep, send)
-
     lane = iota((128, 128), 1)
     for start in range(0, EDGES, STEP):
         for at in range(start, start + STEP, 128):
@@ -388,12 +374,24 @@
     rims = dot_nt(grad_ends[NODES:EXT, :], w_src[...]).astype(BF)
     low[...] = rims[:RIM]
     high[...] = rims[RIM:]
+    grad = dot_nt(grad_ends[:NODES, :], w_src[...]) + dot_nt(grad_ends[EXT:, :], w_dst[...])
+    direct[...] += grad
+
+
+def weights_body(place_at, *refs):
+    up_agg, mid_back, gathered, latent, aggregate, mid, rims_in = refs[:7]
+    node_back, grad_agg, grad_ends, keep, send, flat = refs[7:]
+    mine = place_at[0] & 1
+    flat[1024:1536, :] = dot_t(gathered[...], grad_agg[...])
+    flat[1536:2048, :] = dot_t(latent[...], node_back[...])
+    flat[2048:2560, :] = dot_t(aggregate[...], node_back[...])
+    flat[2560:3072, :] = dot_t(mid[...], mid_back[...])
+    flat[3072:, :] = dot_t(up_agg[...], mid_back[...])
+    part_cores(mine, flat, 5, 11, keep, send)
     grad = dot_t(rims_in[...], grad_ends[NODES:EXT, :])
     flat[:512, :] = grad + dot_t(latent[...], grad_ends[:NODES, :])
     flat[512:1024, :] = dot_t(latent[...], grad_ends[EXT:, :])
     part_cores(mine, flat, 0, 5, keep, send)
-    grad = dot_nt(grad_ends[:NODES, :], w_src[...]) + dot_nt(grad_ends[EXT:, :], w_dst[...])
-    direct[...] += grad
 
 
 def sheet_body(keep, got, out, rows, held):
@@ -409,22 +407,7 @@
         out[to] = held[to].astype(BF)
 
 
-def pillar_body(
-    got,
-    low_far,
-    high_far,
-    direct,
-    index_far,
-    out,
-    grad_fine_far,
-    low,
-    high,
-    index,
-    grad_fine,
-    rows,
-    sems,
-):
-    copies = fetch(sems, (index_far, index), (low_far, low), (high_far, high))
+def pillar_body(got, out, rows):
     total = got[0].astype(F32)
     for i in range(1, YN * XN):
         total = total + got[i].astype(F32)
@@ -432,15 +415,13 @@
     rows[112:, :] = jnp.zeros((16, WIDTH), F32)
     for z in range(ZN):
         out[z] = rows[14 * z : 14 * z + 16, :].astype(BF)
-    for copy in copies:
-        copy.wait()
+
+
+def final_body(direct, low, high, index, grad_fine):
     row = jnp.concatenate([piece(index, 0, 128), piece(index, 128, 64)], axis=1)
     total = direct[...] + dot(down(row[:, :RIM], NODES), low[...])
     total = total + dot(down(row[:, RIM:], NODES), high[...])
     grad_fine[...] = total.astype(BF)
-    copy = pltpu.make_async_copy(grad_fine, grad_fine_far, sems.at[3])
-    copy.start()
-    copy.wait()
 
 
 def last_body(got, out):
@@ -536,20 +517,26 @@
     back = [blocks[0]]
     for (dy, dc), block in zip(PEERS[1:], blocks[1:]):
         back.append(lax.ppermute(block, BOTH, shift(dy=-dy, dc=-dc)))
-    far = (cot_fine, node_slope, w_node, w_msg, edge_dst, gathered, fine_latent, aggregate)
-    far += (mid_latent, edge_src, edge_slope, rims_in, w_src, w_dst)
-    direct, low, high, keep, send = run(
+    direct, low, high, node_back, grad_agg, grad_ends = run(
         backward_body,
-        (f32(NODES, WIDTH), rim, rim, bf(1792, WIDTH), bf(1792, WIDTH)),
-        (edge_count, place_at, spot, up_agg, mid_back, *far, *back),
-        "ss" + (3 + len(far) + PLANE) * "v" + ">vvvvv",
-        (hold(NODES, WIDTH), hold(NODES, WIDTH), hold(NODES, WIDTH), hold(EXT + NODES, WIDTH))
-        + (hold(EDGES, NODES), wide(EXT + NODES, WIDTH), wide(3584, WIDTH)),
+        (f32(NODES, WIDTH), rim, rim, fine, fine, bf(EXT + NODES, WIDTH)),
+        (edge_count, place_at, spot, cot_fine, node_slope, w_node, w_msg, edge_dst, edge_src)
+        + (edge_slope, w_src, w_dst, *back),
+        "ss" + 18 * "v" + ">" + 6 * "v",
+        (hold(NODES, WIDTH), hold(EDGES, NODES), wide(EXT + NODES, WIDTH)),
         room=17_000_000,
-        flops=5 * 10**9,
-    )
-    from_low = lax.ppermute(high, BOTH, ahead)
-    from_high = lax.ppermute(low, BOTH, behind)
+        flops=4 * 10**9,
+    )
+    keep, send = run(
+        weights_body,
+        (bf(1792, WIDTH), bf(1792, WIDTH)),
+        (place_at, up_agg, mid_back, gathered, fine_latent, aggregate, mid_latent, rims_in)
+        + (node_back, grad_agg, grad_ends),
+        "s" + 10 * "v" + ">vv",
+        (wide(3584, WIDTH),),
+        room=17_000_000,
+        flops=2 * 10**9,
+    )
     got = lax.ppermute(send, BOTH, shift(dc=1))
     sheet = YN * XN
     (part,) = run(
@@ -560,19 +547,19 @@
         (wide(2 * ZN, 112, WIDTH), wide(sheet, 112, WIDTH)),
         mib=24,
     )
-    part, from_low, from_high = lax.optimization_barrier((part, from_low, from_high))
     part = lax.all_to_all(part, BOTH, 0, 0, axis_index_groups=SHEETS)
-    part, grad_fine = run(
-        pillar_body,
-        (bf(ZN, HELD, WIDTH), fine),
-        (part, from_low, from_high, direct, send_index),
-        "vhhvh>vh",
-        (hold(RIM, WIDTH), hold(RIM, WIDTH), line(2 * RIM))
-        + (hold(NODES, WIDTH), wide(128, WIDTH)),
-        copies=4,
-        mib=24,
-    )
+    part, low, high = lax.optimization_barrier((part, low, high))
+    from_low = lax.ppermute(high, BOTH, ahead)
+    from_high = lax.ppermute(low, BOTH, behind)
+    (part,) = run(pillar_body, (bf(ZN, HELD, WIDTH),), (part,), "v>v", (wide(128, WIDTH),))
     part = lax.all_to_all(part, "row", 0, 0, axis_index_groups=PILLARS)
+    (grad_fine,) = run(
+        final_body,
+        (fine,),
+        (direct, from_low, from_high, send_index),
+        "vvvv>v",
+        flops=2 * 10**8,
+    )
     (weight_grads,) = run(last_body, (f32(TALL * WIDTH),), (part,), "v>v")
     return fine_out, mid_out, grad_fine, grad_mid, weight_grads
 

time: 152 us -> 150 us (0.987)
  the two profiles are of different devices: /device:TPU:1 before, /device:TPU:127 now
where the time goes in v5:
time: 150 us
  blocking collectives  52.4 us (35%)
  starting transfers between devices  35.3 us (24%)
  waiting for transfers between devices  29.4 us (20%)
  Pallas kernels  28.2 us (19%)
  local copies, waits for them, and re-layouts  2.76 us (2%)
  between operations  1.63 us (1%)
    pallas_call x12, Pallas kernels, run(): pl.pallas_call(body, out_shape=list(outs), in_specs=[pl.BlockSpec(memory_...  28.2 us
    all_to_all x1, blocking collectives, on_device(): part = lax.all_to_all(part, BOTH, 0, 0, axis_index_groups=SHEETS)  27.1 us
    all_to_all x1, blocking collectives, on_device(): got = lax.all_to_all(spread, 'row', 0, 0, axis_index_groups=PILLARS)  12.8 us
    all_to_all x1, blocking collectives, on_device(): got = lax.all_to_all(sums, 'row', 0, 0, axis_index_groups=PILLARS)  12.5 us
    ppermute x7, starting transfers between devices, on_device(): back.append(lax.ppermute(block, BOTH, shift(dy=-dy, dc=-dc)))  10 us
    ppermute x1, waiting for transfers between devices, on_device(): from_high = lax.ppermute(low, BOTH, behind)  7.83 us
    ppermute x1, starting transfers between devices, on_device(): from_low = lax.ppermute(high, BOTH, ahead)  7.65 us
    all_to_all x1, starting transfers between devices, on_device(): part = lax.all_to_all(part, 'row', 0, 0, axis_index_groups=PILLARS)  7.09 us
  transfers between devices with their start and end apart: 20, of which 12 were waited for; matrix products, arithmetic and copies ran while one was open for 0% of the time, Pallas kernels for 3%

profile of v5, /device:TPU:127, one launch (start us, length us, event | category | flops | bytes accessed | tf_op | source)
XLA Modules:
  0.0 149.6 jit_solution(5949418007096217370)
XLA Ops:
  0.6 2.0 %shard_map.183 = (bf16[96,512]{1,0:T(8,128)(2,1)}, bf16[96,512]{1,0:T(8,128)(2,1)}) custom-call(s32[192]{0:T(256)} %index.1, bf16[384,512]{1,0:T(8,128)(2,1)} %refs_3_.3), custom_call_target="tpu_custom_call" | custom-call | bytes 590592 | tf_op jit(solution)/shard_map/pallas_call | solution.py:106
  2.6 3.1 %collective-permute-start = (bf16[96,512]{1,0:T(8,128)(2,1)}, bf16[96,512]{1,0:T(8,128)(2,1)S(1)}, u32[]{:S(2)}, u32[]{:S(2)}) collective-permute-start(bf16[96,512]{1,0:T(8,128)(2,1)} %get-tuple-element.52), channel_id=1, source_target_pairs={{0,1},{1,2},{2,3},{3,4},{4,5},{5,6},{6,7},{7,8},{8,9},{9,10},{10,1... | collective-permute-start | bytes 294920 | tf_op jit(solution)/shard_map/ppermute | solution.py:472
  6.3 2.7 %shard_map.182 = (bf16[384,512]{1,0:T(8,128)(2,1)}, bf16[384,512]{1,0:T(8,128)(2,1)}, s32[1,384]{1,0:T(1,128)}) custom-call(s32[1,384]{1,0:T(1,128)} %bitcast.2, bf16[384,512]{1,0:T(8,128)(2,1)} %refs_3_.3, bf16[512,512]{1,0:T(8,128)(2,1)} %refs_8_.1, bf16[512,512]{1,0:T(8,128)(2,1)} %refs_9_.1), custom_call_target="tpu_custom_call" | custom-call | flops 402653184 | bytes 2231296 | tf_op jit(solution)/shard_map/pallas_call | solution.py:106
  9.1 6.3 %collective-permute-done.1.upper_far = bf16[96,512]{1,0:T(8,128)(2,1)S(1)} collective-permute-done((bf16[96,512]{1,0:T(8,128)(2,1)}, bf16[96,512]{1,0:T(8,128)(2,1)S(1)}, u32[]{:S(2)}, u32[]{:S(2)}) %collective-permute-start.1) | collective-permute-done | bytes 98336 | tf_op jit(solution)/shard_map/ppermute | solution.py:473
  16.1 9.5 %shard_map.184 = (bf16[384,512]{1,0:T(8,128)(2,1)}, f32[384,512]{1,0:T(8,128)}, bf16[2304,512]{1,0:T(8,128)(2,1)}, bf16[384,512]{1,0:T(8,128)(2,1)}, bf16[384,51...) custom-call(s32[1]{0:T(128)S(6)} %copy.20.count, ...), custom_call_target="tpu_custom_call" | custom-call | flops 4000000000 | bytes 8934408 | tf_op jit(solution)/shard_map/pallas_call | solution.py:106
  25.9 3.7 %collective-permute-start.5 = (bf16[112,512]{1,0:T(8,128)(2,1)}, bf16[112,512]{1,0:T(8,128)(2,1)S(1)}, u32[]{:S(2)}, u32[]{:S(2)}) collective-permute-start(bf16[112,512]{1,0:T(8,128)(2,1)} %get-tuple-element.60), channel_id=1, source_target_pairs={{0,12},{1,13},{2,14},{3,15},{4,8},{5,9},{6,10},{7,11},{8,20},{9,21... | collective-permute-start | bytes 344072 | tf_op jit(solution)/shard_map/ppermute | solution.py:503
  30.4 1.2 collective-permute-done.2.refs_1_
  31.6 1.5 %collective-permute-done.3.refs_2_ = bf16[112,512]{1,0:T(8,128)(2,1)S(1)} collective-permute-done((bf16[112,512]{1,0:T(8,128)(2,1)}, bf16[112,512]{1,0:T(8,128)(2,1)S(1)}, u32[]{:S(2)}, u32[]{:S(2)}) %collective-permute-start.3) | collective-permute-done | bytes 114720 | tf_op jit(solution)/shard_map/ppermute | solution.py:503
  33.2 1.6 %collective-permute-start.8 = (bf16[112,512]{1,0:T(8,128)(2,1)}, bf16[112,512]{1,0:T(8,128)(2,1)S(1)}, u32[]{:S(2)}, u32[]{:S(2)}) collective-permute-start(bf16[112,512]{1,0:T(8,128)(2,1)} %get-tuple-element.63), channel_id=1, source_target_pairs={{0,4},{1,5},{2,6},{3,7},{4,0},{5,1},{6,2},{7,3},{8,12},{9,13},{10,... | collective-permute-start | bytes 344072 | tf_op jit(solution)/shard_map/ppermute | solution.py:503
  36.4 2.5 %collective-permute-done.7.refs_6_ = bf16[112,512]{1,0:T(8,128)(2,1)S(1)} collective-permute-done((bf16[112,512]{1,0:T(8,128)(2,1)}, bf16[112,512]{1,0:T(8,128)(2,1)S(1)}, u32[]{:S(2)}, u32[]{:S(2)}) %collective-permute-start.7) | collective-permute-done | bytes 114720 | tf_op jit(solution)/shard_map/ppermute | solution.py:503
  38.9 0.9 copy-done.2
  40.5 12.5 %all_to_all.20.got = bf16[8,32,512]{2,1,0:T(8,128)(2,1)S(1)} all-to-all(bf16[8,32,512]{2,1,0:T(8,128)(2,1)S(1)} %get-tuple-element.64), channel_id=1, replica_groups={{0,32,64,96,128,160,192,224},{4,36,68,100,132,164,196,228},{8,40,72,104..., dimensions={0} | all-to-all | bytes 524288 | tf_op jit(solution)/shard_map/all_to_all | solution.py:505
  53.0 1.4 shard_map.186
  54.4 12.8 %all_to_all.21.got = bf16[8,32,512]{2,1,0:T(8,128)(2,1)S(1)} all-to-all(bf16[8,32,512]{2,1,0:T(8,128)(2,1)S(1)} %get-tuple-element.69), channel_id=1, replica_groups={{0,32,64,96,128,160,192,224},{4,36,68,100,132,164,196,228},{8,40,72,104..., dimensions={0} | all-to-all | bytes 524288 | tf_op jit(solution)/shard_map/all_to_all | solution.py:515
  67.7 5.2 %collective-permute-start.10 = (bf16[96,512]{1,0:T(8,128)(2,1)S(1)}, bf16[96,512]{1,0:T(8,128)(2,1)S(1)}, u32[]{:S(2)}, u32[]{:S(2)}) collective-permute-start(bf16[96,512]{1,0:T(8,128)(2,1)S(1)} %get-tuple-element.72), channel_id=1, source_target_pairs={{0,20},{1,21},{2,22},{3,23},{4,16},{5,17},{6,18},{7,19},{8,28},{9,... | collective-permute-start | bytes 294920 | tf_op jit(solution)/shard_map/ppermute | solution.py:519
  73.4 2.1 %collective-permute-start.13 = (bf16[96,512]{1,0:T(8,128)(2,1)S(1)}, bf16[96,512]{1,0:T(8,128)(2,1)S(1)}, u32[]{:S(2)}, u32[]{:S(2)}) collective-permute-start(bf16[96,512]{1,0:T(8,128)(2,1)S(1)} %get-tuple-element.75), channel_id=1, source_target_pairs={{0,8},{1,9},{2,10},{3,11},{4,12},{5,13},{6,14},{7,15},{8,16},{9,17... | collective-permute-start | bytes 294920 | tf_op jit(solution)/shard_map/ppermute | solution.py:519
  75.6 2.0 %collective-permute-start.14 = (bf16[96,512]{1,0:T(8,128)(2,1)S(1)}, bf16[96,512]{1,0:T(8,128)(2,1)S(1)}, u32[]{:S(2)}, u32[]{:S(2)}) collective-permute-start(bf16[96,512]{1,0:T(8,128)(2,1)S(1)} %get-tuple-element.76), channel_id=1, source_target_pairs={{0,12},{1,13},{2,14},{3,15},{4,8},{5,9},{6,10},{7,11},{8,20},{9,21... | collective-permute-start | bytes 294920 | tf_op jit(solution)/shard_map/ppermute | solution.py:519
  78.4 1.2 collective-permute-done.11.refs_13_
  79.6 1.4 collective-permute-done.12.refs_14_
  81.1 1.1 copy-done.19
  82.2 5.9 %shard_map.188 = (f32[384,512]{1,0:T(8,128)S(1)}, bf16[96,512]{1,0:T(8,128)(2,1)S(1)}, bf16[96,512]{1,0:T(8,128)(2,1)S(1)}, bf16[384,512]{1,0:T(8,128)(2,1)S(1)}...) custom-call(s32[1]{0:T(128)S(6)} %copy.20.count, s32[1]{0:T(128)} %bitcast.place_at, ...), custom_call_target="tpu_custom_call" | custom-call | flops 4000000000 | bytes 9719304 | tf_op jit(solution)/shard_map/pallas_call | solution.py:106
  88.2 2.0 %shard_map.189 = (bf16[1792,512]{1,0:T(8,128)(2,1)S(1)}, bf16[1792,512]{1,0:T(8,128)(2,1)S(1)}) custom-call(s32[1]{0:T(128)} %bitcast.place_at, bf16[32,512]{1,0:T(8,128)(2,1)S(1)} %get-tuple-element.79.refs_0_, bf16[32,512]{1,0:T(8,128)(2,1)S(1)} %get-tuple-element.80.refs_1_, bf16[384,512]{1,0:T(8,128)(2,1)S(1)} %copy-done.17, ...), custom_call_target="tpu_custom_call" | custom-call | flops 2000000000 | bytes 6914052 | tf_op jit(solution)/shard_map/pallas_call | solution.py:106
  90.2 1.0 collective-permute-start.16
  91.2 3.4 %collective-permute-done.16.got = bf16[1792,512]{1,0:T(8,128)(2,1)S(1)} collective-permute-done((bf16[1792,512]{1,0:T(8,128)(2,1)S(1)}, bf16[1792,512]{1,0:T(8,128)(2,1)S(1)}, u32[]{:S(2)}, u32[]{:S(2)}) %collective-permute-start.16) | collective-permute-done | bytes 1835040 | tf_op jit(solution)/shard_map/ppermute | solution.py:540
  94.6 1.0 shard_map.190
  95.5 27.1 %all_to_all.22.got = bf16[16,112,512]{2,1,0:T(8,128)(2,1)S(1)} all-to-all(bf16[16,112,512]{2,1,0:T(8,128)(2,1)S(1)} %shard_map.190), channel_id=1, replica_groups={{0,1,2,3,8,9,10,11,16,17,18,19,24,25,26,27},{4,5,6,7,12,13,14,15,20,21,..., dimensions={0} | all-to-all | bytes 3670016 | tf_op jit(solution)/shard_map/all_to_all | solution.py:550
  122.7 1.0 shard_map.192
  123.7 7.1 %all-to-all-start.3 = ((bf16[8,16,512]{2,1,0:T(8,128)(2,1)}), bf16[8,16,512]{2,1,0:T(8,128)(2,1)S(1)}, u32[]{:S(2)}, u32[]{:S(2)}) async-start(bf16[8,16,512]{2,1,0:T(8,128)(2,1)} %shard_map.192), calls=%async_computation.3 | async-start | bytes 262144 | tf_op jit(solution)/shard_map/all_to_all | solution.py:555
  130.8 7.7 %collective-permute-start.17 = (bf16[96,512]{1,0:T(8,128)(2,1)S(1)}, bf16[96,512]{1,0:T(8,128)(2,1)S(1)}, u32[]{:S(2)}, u32[]{:S(2)}) collective-permute-start(bf16[96,512]{1,0:T(8,128)(2,1)S(1)} %copy-done.12), channel_id=1, source_target_pairs={{0,1},{1,2},{2,3},{3,4},{4,5},{5,6},{6,7},{7,8},{8,9},{9,10},{10,1... | collective-permute-start | bytes 294920 | tf_op jit(solution)/shard_map/ppermute | solution.py:552
  138.4 1.6 %collective-permute-done.17.low = bf16[96,512]{1,0:T(8,128)(2,1)S(1)} collective-permute-done((bf16[96,512]{1,0:T(8,128)(2,1)S(1)}, bf16[96,512]{1,0:T(8,128)(2,1)S(1)}, u32[]{:S(2)}, u32[]{:S(2)}) %collective-permute-start.17) | collective-permute-done | bytes 98336 | tf_op jit(solution)/shard_map/ppermute | solution.py:552
  140.0 7.8 %collective-permute-done.18.high = bf16[96,512]{1,0:T(8,128)(2,1)S(1)} collective-permute-done((bf16[96,512]{1,0:T(8,128)(2,1)S(1)}, bf16[96,512]{1,0:T(8,128)(2,1)S(1)}, u32[]{:S(2)}, u32[]{:S(2)}) %collective-permute-start.18) | collective-permute-done | bytes 98336 | tf_op jit(solution)/shard_map/ppermute | solution.py:553
  147.9 1.1 shard_map.191
  (69 shorter events, 6.7 us)
Async XLA Ops:
  2.6 6.4 %collective-permute-start = (bf16[96,512]{1,0:T(8,128)(2,1)}, bf16[96,512]{1,0:T(8,128)(2,1)S(1)}, u32[]{:S(2)}, u32[]{:S(2)}) collective-permute-start(bf16[96,512]{1,0:T(8,128)(2,1)} %get-tuple-element.52), channel_id=1, source_target_pairs={{0,1},{1,2},{2,3},{3,4},{4,5},{5,6},{6,7},{7,8},{8,9},{9,10},{10,1... | collective-permute-start | bytes 294920 | tf_op jit(solution)/shard_map/ppermute | solution.py:472
  5.7 9.7 %collective-permute-start.1 = (bf16[96,512]{1,0:T(8,128)(2,1)}, bf16[96,512]{1,0:T(8,128)(2,1)S(1)}, u32[]{:S(2)}, u32[]{:S(2)}) collective-permute-start(bf16[96,512]{1,0:T(8,128)(2,1)} %get-tuple-element.53), channel_id=1, source_target_pairs={{1,0},{2,1},{3,2},{4,3},{5,4},{6,5},{7,6},{8,7},{9,8},{10,9},{11,1... | collective-permute-start | bytes 294920 | tf_op jit(solution)/shard_map/ppermute | solution.py:473
  16.0 37.0 %copy-start.3 = (bf16[32,512]{1,0:T(8,128)(2,1)S(1)}, bf16[32,512]{1,0:T(8,128)(2,1)}, u32[]{:S(2)}) copy-start(bf16[32,512]{1,0:T(8,128)(2,1)} %cot_far.1) | copy-start | bytes 98308
  16.0 37.0 %copy-start.4 = (bf16[32,512]{1,0:T(8,128)(2,1)S(1)}, bf16[32,512]{1,0:T(8,128)(2,1)}, u32[]{:S(2)}) copy-start(bf16[32,512]{1,0:T(8,128)(2,1)} %refs_5_.3) | copy-start | bytes 98308
  16.0 65.0 %copy-start.6 = (bf16[1024,512]{1,0:T(8,128)(2,1)S(1)}, bf16[1024,512]{1,0:T(8,128)(2,1)}, u32[]{:S(2)}) copy-start(bf16[1024,512]{1,0:T(8,128)(2,1)} %refs_3_.2) | copy-start | bytes 3145732
  16.0 65.0 %copy-start.7 = (bf16[512,512]{1,0:T(8,128)(2,1)S(1)}, bf16[512,512]{1,0:T(8,128)(2,1)}, u32[]{:S(2)}) copy-start(bf16[512,512]{1,0:T(8,128)(2,1)} %refs_8_.1) | copy-start | bytes 1572868
  16.0 65.0 %copy-start.8 = (bf16[512,512]{1,0:T(8,128)(2,1)S(1)}, bf16[512,512]{1,0:T(8,128)(2,1)}, u32[]{:S(2)}) copy-start(bf16[512,512]{1,0:T(8,128)(2,1)} %refs_9_.1) | copy-start | bytes 1572868
  16.0 65.0 %copy-start.9 = (bf16[512,512]{1,0:T(8,128)(2,1)S(1)}, bf16[512,512]{1,0:T(8,128)(2,1)}, u32[]{:S(2)}) copy-start(bf16[512,512]{1,0:T(8,128)(2,1)} %refs_4_.1) | copy-start | bytes 1572868
  16.0 65.0 %copy-start.10 = (bf16[384,512]{1,0:T(8,128)(2,1)S(1)}, bf16[384,512]{1,0:T(8,128)(2,1)}, u32[]{:S(2)}) copy-start(bf16[384,512]{1,0:T(8,128)(2,1)} %refs_1_.1) | copy-start | bytes 1179652
  16.0 65.0 %copy-start.13 = (s32[2304]{0:T(1024)S(1)}, s32[2304]{0:T(1024)}, u32[]{:S(2)}) copy-start(s32[2304]{0:T(1024)} %refs_6_.1) | copy-start | bytes 27652
  16.1 65.0 %copy-start.14 = (s32[2304]{0:T(1024)S(1)}, s32[2304]{0:T(1024)}, u32[]{:S(2)}) copy-start(s32[2304]{0:T(1024)} %refs_5_.2) | copy-start | bytes 27652
  16.1 65.0 %copy-start.15 = (s32[1,384]{1,0:T(1,128)S(1)}, s32[1,384]{1,0:T(1,128)}, u32[]{:S(2)}) copy-start(s32[1,384]{1,0:T(1,128)} %get-tuple-element.54.spot_far.refs_0_) | copy-start | bytes 4612
  25.6 27.4 %copy-start = (bf16[1024,512]{1,0:T(8,128)(2,1)S(1)}, bf16[1024,512]{1,0:T(8,128)(2,1)}, u32[]{:S(2)}) copy-start(bf16[1024,512]{1,0:T(8,128)(2,1)} %w_mid_far.1) | copy-start | bytes 3145732
  25.6 6.0 %collective-permute-start.2 = (bf16[112,512]{1,0:T(8,128)(2,1)}, bf16[112,512]{1,0:T(8,128)(2,1)S(1)}, u32[]{:S(2)}, u32[]{:S(2)}) collective-permute-start(bf16[112,512]{1,0:T(8,128)(2,1)} %get-tuple-element.57), channel_id=1, source_target_pairs={{0,16},{1,17},{2,18},{3,19},{4,20},{5,21},{6,22},{7,23},{8,24},{9,... | collective-permute-start | bytes 344072 | tf_op jit(solution)/shard_map/ppermute | solution.py:503
  25.7 7.5 %collective-permute-start.3 = (bf16[112,512]{1,0:T(8,128)(2,1)}, bf16[112,512]{1,0:T(8,128)(2,1)S(1)}, u32[]{:S(2)}, u32[]{:S(2)}) collective-permute-start(bf16[112,512]{1,0:T(8,128)(2,1)} %get-tuple-element.58), channel_id=1, source_target_pairs={{0,20},{1,21},{2,22},{3,23},{4,16},{5,17},{6,18},{7,19},{8,28},{9,... | collective-permute-start | bytes 344072 | tf_op jit(solution)/shard_map/ppermute | solution.py:503
  25.8 9.0 %collective-permute-start.4 = (bf16[112,512]{1,0:T(8,128)(2,1)}, bf16[112,512]{1,0:T(8,128)(2,1)S(1)}, u32[]{:S(2)}, u32[]{:S(2)}) collective-permute-start(bf16[112,512]{1,0:T(8,128)(2,1)} %get-tuple-element.59), channel_id=1, source_target_pairs={{0,8},{1,9},{2,10},{3,11},{4,12},{5,13},{6,14},{7,15},{8,16},{9,17... | collective-permute-start | bytes 344072 | tf_op jit(solution)/shard_map/ppermute | solution.py:503
  25.9 9.7 %collective-permute-start.5 = (bf16[112,512]{1,0:T(8,128)(2,1)}, bf16[112,512]{1,0:T(8,128)(2,1)S(1)}, u32[]{:S(2)}, u32[]{:S(2)}) collective-permute-start(bf16[112,512]{1,0:T(8,128)(2,1)} %get-tuple-element.60), channel_id=1, source_target_pairs={{0,12},{1,13},{2,14},{3,15},{4,8},{5,9},{6,10},{7,11},{8,20},{9,21... | collective-permute-start | bytes 344072 | tf_op jit(solution)/shard_map/ppermute | solution.py:503
  29.6 6.8 %collective-permute-start.6 = (bf16[112,512]{1,0:T(8,128)(2,1)}, bf16[112,512]{1,0:T(8,128)(2,1)S(1)}, u32[]{:S(2)}, u32[]{:S(2)}) collective-permute-start(bf16[112,512]{1,0:T(8,128)(2,1)} %get-tuple-element.61), channel_id=1, source_target_pairs={{0,24},{1,25},{2,26},{3,27},{4,28},{5,29},{6,30},{7,31},{8,0},{9,1... | collective-permute-start | bytes 344072 | tf_op jit(solution)/shard_map/ppermute | solution.py:503
  31.6 7.2 %collective-permute-start.7 = (bf16[112,512]{1,0:T(8,128)(2,1)}, bf16[112,512]{1,0:T(8,128)(2,1)S(1)}, u32[]{:S(2)}, u32[]{:S(2)}) collective-permute-start(bf16[112,512]{1,0:T(8,128)(2,1)} %get-tuple-element.62), channel_id=1, source_target_pairs={{0,28},{1,29},{2,30},{3,31},{4,24},{5,25},{6,26},{7,27},{8,4},{9,5... | collective-permute-start | bytes 344072 | tf_op jit(solution)/shard_map/ppermute | solution.py:503
  33.2 5.7 %collective-permute-start.8 = (bf16[112,512]{1,0:T(8,128)(2,1)}, bf16[112,512]{1,0:T(8,128)(2,1)S(1)}, u32[]{:S(2)}, u32[]{:S(2)}) collective-permute-start(bf16[112,512]{1,0:T(8,128)(2,1)} %get-tuple-element.63), channel_id=1, source_target_pairs={{0,4},{1,5},{2,6},{3,7},{4,0},{5,1},{6,2},{7,3},{8,12},{9,13},{10,... | collective-permute-start | bytes 344072 | tf_op jit(solution)/shard_map/ppermute | solution.py:503
  39.8 41.3 %copy-start.16 = (bf16[2304,512]{1,0:T(8,128)(2,1)S(1)}, bf16[2304,512]{1,0:T(8,128)(2,1)}, u32[]{:S(2)}) copy-start(bf16[2304,512]{1,0:T(8,128)(2,1)} %get-tuple-element.67.refs_7_) | copy-start | bytes 7077892
  67.6 8.0 %collective-permute-start.9 = (bf16[96,512]{1,0:T(8,128)(2,1)S(1)}, bf16[96,512]{1,0:T(8,128)(2,1)S(1)}, u32[]{:S(2)}, u32[]{:S(2)}) collective-permute-start(bf16[96,512]{1,0:T(8,128)(2,1)S(1)} %get-tuple-element.71), channel_id=1, source_target_pairs={{0,16},{1,17},{2,18},{3,19},{4,20},{5,21},{6,22},{7,23},{8,24},{9,... | collective-permute-start | bytes 294920 | tf_op jit(solution)/shard_map/ppermute | solution.py:519
  67.7 10.7 %collective-permute-start.10 = (bf16[96,512]{1,0:T(8,128)(2,1)S(1)}, bf16[96,512]{1,0:T(8,128)(2,1)S(1)}, u32[]{:S(2)}, u32[]{:S(2)}) collective-permute-start(bf16[96,512]{1,0:T(8,128)(2,1)S(1)} %get-tuple-element.72), channel_id=1, source_target_pairs={{0,20},{1,21},{2,22},{3,23},{4,16},{5,17},{6,18},{7,19},{8,28},{9,... | collective-permute-start | bytes 294920 | tf_op jit(solution)/shard_map/ppermute | solution.py:519
  72.9 6.7 %collective-permute-start.11 = (bf16[96,512]{1,0:T(8,128)(2,1)S(1)}, bf16[96,512]{1,0:T(8,128)(2,1)S(1)}, u32[]{:S(2)}, u32[]{:S(2)}) collective-permute-start(bf16[96,512]{1,0:T(8,128)(2,1)S(1)} %get-tuple-element.73), channel_id=1, source_target_pairs={{0,24},{1,25},{2,26},{3,27},{4,28},{5,29},{6,30},{7,31},{8,0},{9,1... | collective-permute-start | bytes 294920 | tf_op jit(solution)/shard_map/ppermute | solution.py:519
  73.4 7.5 %collective-permute-start.12 = (bf16[96,512]{1,0:T(8,128)(2,1)S(1)}, bf16[96,512]{1,0:T(8,128)(2,1)S(1)}, u32[]{:S(2)}, u32[]{:S(2)}) collective-permute-start(bf16[96,512]{1,0:T(8,128)(2,1)S(1)} %get-tuple-element.74), channel_id=1, source_target_pairs={{0,28},{1,29},{2,30},{3,31},{4,24},{5,25},{6,26},{7,27},{8,4},{9,5... | collective-permute-start | bytes 294920 | tf_op jit(solution)/shard_map/ppermute | solution.py:519
  73.4 7.5 %collective-permute-start.13 = (bf16[96,512]{1,0:T(8,128)(2,1)S(1)}, bf16[96,512]{1,0:T(8,128)(2,1)S(1)}, u32[]{:S(2)}, u32[]{:S(2)}) collective-permute-start(bf16[96,512]{1,0:T(8,128)(2,1)S(1)} %get-tuple-element.75), channel_id=1, source_target_pairs={{0,8},{1,9},{2,10},{3,11},{4,12},{5,13},{6,14},{7,15},{8,16},{9,17... | collective-permute-start | bytes 294920 | tf_op jit(solution)/shard_map/ppermute | solution.py:519
  75.6 5.4 %collective-permute-start.14 = (bf16[96,512]{1,0:T(8,128)(2,1)S(1)}, bf16[96,512]{1,0:T(8,128)(2,1)S(1)}, u32[]{:S(2)}, u32[]{:S(2)}) collective-permute-start(bf16[96,512]{1,0:T(8,128)(2,1)S(1)} %get-tuple-element.76), channel_id=1, source_target_pairs={{0,12},{1,13},{2,14},{3,15},{4,8},{5,9},{6,10},{7,11},{8,20},{9,21... | collective-permute-start | bytes 294920 | tf_op jit(solution)/shard_map/ppermute | solution.py:519
  78.4 2.6 %collective-permute-start.15 = (bf16[96,512]{1,0:T(8,128)(2,1)S(1)}, bf16[96,512]{1,0:T(8,128)(2,1)S(1)}, u32[]{:S(2)}, u32[]{:S(2)}) collective-permute-start(bf16[96,512]{1,0:T(8,128)(2,1)S(1)} %get-tuple-element.77), channel_id=1, source_target_pairs={{0,4},{1,5},{2,6},{3,7},{4,0},{5,1},{6,2},{7,3},{8,12},{9,13},{10,... | collective-permute-start | bytes 294920 | tf_op jit(solution)/shard_map/ppermute | solution.py:519
  90.2 4.4 %collective-permute-start.16 = (bf16[1792,512]{1,0:T(8,128)(2,1)S(1)}, bf16[1792,512]{1,0:T(8,128)(2,1)S(1)}, u32[]{:S(2)}, u32[]{:S(2)}) collective-permute-start(bf16[1792,512]{1,0:T(8,128)(2,1)S(1)} %get-tuple-element.88), channel_id=1, source_target_pairs={{0,4},{1,5},{2,6},{3,7},{4,0},{5,1},{6,2},{7,3},{8,12},{9,13},{10,... | collective-permute-start | bytes 5505032 | tf_op jit(solution)/shard_map/ppermute | solution.py:540
  123.7 25.3 %all-to-all-start.3 = ((bf16[8,16,512]{2,1,0:T(8,128)(2,1)}), bf16[8,16,512]{2,1,0:T(8,128)(2,1)S(1)}, u32[]{:S(2)}, u32[]{:S(2)}) async-start(bf16[8,16,512]{2,1,0:T(8,128)(2,1)} %shard_map.192), calls=%async_computation.3 | async-start | bytes 262144 | tf_op jit(solution)/shard_map/all_to_all | solution.py:555
  130.8 9.3 %collective-permute-start.17 = (bf16[96,512]{1,0:T(8,128)(2,1)S(1)}, bf16[96,512]{1,0:T(8,128)(2,1)S(1)}, u32[]{:S(2)}, u32[]{:S(2)}) collective-permute-start(bf16[96,512]{1,0:T(8,128)(2,1)S(1)} %copy-done.12), channel_id=1, source_target_pairs={{0,1},{1,2},{2,3},{3,4},{4,5},{5,6},{6,7},{7,8},{8,9},{9,10},{10,1... | collective-permute-start | bytes 294920 | tf_op jit(solution)/shard_map/ppermute | solution.py:552
  138.4 9.5 %collective-permute-start.18 = (bf16[96,512]{1,0:T(8,128)(2,1)S(1)}, bf16[96,512]{1,0:T(8,128)(2,1)S(1)}, u32[]{:S(2)}, u32[]{:S(2)}) collective-permute-start(bf16[96,512]{1,0:T(8,128)(2,1)S(1)} %get-tuple-element.92), channel_id=1, source_target_pairs={{1,0},{2,1},{3,2},{4,3},{5,4},{6,5},{7,6},{8,7},{9,8},{10,9},{11,1... | collective-permute-start | bytes 294920 | tf_op jit(solution)/shard_map/ppermute | solution.py:553
  (11 other events, 68.1 us)
